TPU v7x, 32 devices: a whole 2x2x4 slice. The times are simulated.
32 devices in a mesh: batch: 8 (over z, x), mp: 4 (over y, core).
Axes of the slice: x: 2, y: 2, z: 4, core: 2. Of those that a mesh axis runs over, the one named last changes fastest.
Arguments:
- query_hidden: bfloat16 [8192, 768], P(('batch', 'mp')), may hold values from -28 to 28
- passage_hidden: bfloat16 [40960, 768], P(('batch', 'mp')), may hold values from -28 to 28
- projection: bfloat16 [768, 128], replicated, may hold values from -0.21875 to 0.21875
- query_lengths: int32 [256], P(('batch', 'mp')), may hold values from 8 to 32, as said below
- passage_lengths: int32 [320], P(('batch', 'mp')), may hold values from 64 to 128, as said below
- positives: int32 [256], P(('batch', 'mp')), may hold values from 0 to 9
Outputs:
- query_loss: float32 [256], P(('batch', 'mp'))
- grad_query_hidden: bfloat16 [8192, 768], P(('batch', 'mp'))
- grad_passage_hidden: bfloat16 [40960, 768], P(('batch', 'mp'))
- grad_projection: float32 [768, 128], replicated
Inputs may be any that keep to these rules, and one draw needn't show every extreme that they name: `query_lengths`: the first query of each block of 8 queries has all 32 tokens. `passage_lengths`: the first passage of each block of 10 passages has all 128 tokens.
All inputs are finite; a program needn't handle non-finite values.
Results may differ from a plain program's by a relative error of at most 0.012.
The roundings to bfloat16 on the way count: a program that leaves them out, or rounds other values in their place, can miss the bound.
Values may be sent and summed in bfloat16 or wider, within the bound.
No kernel may reach another device: no remote copies, remote signals or barrier semaphores. Data moves between devices by JAX's collectives and lax.ppermute only.
A program may use at most 64 MiB of HBM per device.

v0:
```python
import functools
import math

import jax
import jax.numpy as jnp
from jax import lax
from jax.experimental import pallas as pl
from jax.experimental.pallas import tpu as pltpu
from jax.sharding import PartitionSpec as P

inner_scale = 128.0
outer_scale = 8.0
loss_scale = 32.0
norm_eps = 1e-06

LANES = 128
ROWS = 16
LOG2E = 1.0 / math.log(2.0)
NT = (((1,), (1,)), ((), ()))

vmem = pl.BlockSpec(memory_space=pltpu.VMEM)
smem = pl.BlockSpec(memory_space=pltpu.SMEM)


def shifted(block, axis, distance):
    devices = range(lax.axis_size(axis))
    route = [((i - distance) % len(devices), i) for i in devices]
    return lax.ppermute(block, axis, route)


def dot32(left, right, dims=(((1,), (0,)), ((), ()))):
    return lax.dot_general(left, right, dims, preferred_element_type=jnp.float32)


def call(body, outs, in_specs, args, scratch=(), flops=0, trans=0):
    moved = sum(a.size * a.dtype.itemsize for a in args)
    moved += sum(math.prod(o.shape) * o.dtype.itemsize for o in outs)
    return pl.pallas_call(
        body,
        out_shape=tuple(outs),
        in_specs=list(in_specs),
        out_specs=tuple(vmem for _ in outs),
        scratch_shapes=list(scratch),
        compiler_params=pltpu.CompilerParams(vmem_limit_bytes=24 * 2**20),
        cost_estimate=pl.CostEstimate(flops=flops, bytes_accessed=moved, transcendentals=trans),
    )(*args)


def spread(values, count, group):
    lane = lax.broadcasted_iota(jnp.int32, (1, count * group), 1) // group
    row = jnp.zeros((1, count * group), jnp.int32)
    for item in range(count):
        row = jnp.where(lane == item, values[item], row)
    return row


def keep_row(lengths, queries, tokens):
    slot = lax.broadcasted_iota(jnp.int32, (1, queries * tokens), 1) % tokens
    return (slot < spread(lengths, queries, tokens)).astype(jnp.float32)


def unit_rows(before):
    inverse = lax.rsqrt(jnp.sum(before * before, axis=1, keepdims=True) + norm_eps)
    return before * inverse, inverse


def back_rows(grad, before):
    unit, inverse = unit_rows(before)
    inner = jnp.sum(unit * grad, axis=1, keepdims=True)
    return ((grad - unit * inner) * inverse).astype(jnp.bfloat16)


def query_embed_body(queries, lengths, hidden, projection, before_out, sent_out):
    rows = hidden.shape[0]
    before = dot32(hidden[...], projection[...])
    before_out[...] = before
    sent_out[:rows, :] = unit_rows(before)[0].astype(jnp.bfloat16)
    keep = keep_row(lengths, queries, rows // queries)
    row = lax.broadcasted_iota(jnp.int32, (ROWS, LANES), 0)
    tail = jnp.zeros((ROWS, LANES), jnp.float32)
    for piece in range(rows // LANES):
        tail = jnp.where(row == piece, keep[:, piece * LANES : (piece + 1) * LANES], tail)
    sent_out[rows:, :] = tail.astype(jnp.bfloat16)


def sent_keep(sent, rows):
    tail = sent[rows:, :].astype(jnp.float32)
    return jnp.concatenate([tail[i : i + 1, :] for i in range(rows // LANES)], axis=1)


def score_block(queries, passages, lengths, embed, sent, powers, totals, scores, tops):
    rows = sent.shape[0] - ROWS
    tokens = embed.shape[0] // passages
    query = sent[:rows, :]
    slot = lax.broadcasted_iota(jnp.int32, (tokens, rows), 0)
    totals[...] = jnp.ones(totals.shape, jnp.float32)
    tops[...] = jnp.zeros(tops.shape, jnp.float32)
    for c in range(passages):
        part = slice(c * tokens, (c + 1) * tokens)
        sims = dot32(embed[part, :], query, NT)
        sims = jnp.where(slot < lengths[c], sims, -jnp.inf)
        top = jnp.max(sims, axis=0, keepdims=True)
        power = jnp.exp2((sims - top) * (inner_scale * LOG2E))
        powers[part, :] = power
        tops[c : c + 1, :] = top
        totals[c : c + 1, :] = jnp.sum(power, axis=0, keepdims=True)
    best = tops[...] + jnp.log(totals[...]) / inner_scale
    best = best * sent_keep(sent, rows)
    group = rows // queries
    same = lax.broadcasted_iota(jnp.int32, (rows, rows), 0) // group
    same = (same == lax.broadcasted_iota(jnp.int32, (rows, rows), 1) // group).astype(jnp.bfloat16)
    high = best.astype(jnp.bfloat16)
    rest = best - high.astype(jnp.float32)
    middle = rest.astype(jnp.bfloat16)
    low = (rest - middle.astype(jnp.float32)).astype(jnp.bfloat16)
    total = dot32(high, same) + dot32(middle, same) + dot32(low, same)
    c = lax.broadcasted_iota(jnp.int32, total.shape, 0)
    scores[...] = jnp.where(c < passages, outer_scale * total, -jnp.inf)


def own_score_body(
    queries, lengths, hidden, projection, sent, before_out, embed_out, powers, totals, scores, tops
):
    before = dot32(hidden[...], projection[...])
    before_out[...] = before
    embed_out[...] = unit_rows(before)[0].astype(jnp.bfloat16)
    score_block(
        queries, lengths.shape[0], lengths, embed_out, sent, powers, totals, scores, tops
    )


def other_score_body(
    queries, lengths, embed, sent1, sent2, powers1, powers2, totals1, totals2, scores1, scores2, tops
):
    passages = lengths.shape[0]
    score_block(queries, passages, lengths, embed, sent1, powers1, totals1, scores1, tops)
    score_block(queries, passages, lengths, embed, sent2, powers2, totals2, scores2, tops)


def score_softmax(first, second, third):
    parts = (first, second, third)
    top = functools.reduce(
        jnp.maximum, [jnp.max(part, axis=0, keepdims=True) for part in parts]
    )
    total = sum(jnp.sum(jnp.exp(part - top), axis=0, keepdims=True) for part in parts)
    return top + jnp.log(total)


def fill_grad_sim(passages, coefficient, powers, out, column):
    tokens = powers.shape[0] // passages
    rows = powers.shape[1]
    for c in range(passages):
        part = slice(c * tokens, (c + 1) * tokens)
        out[part, column : column + rows] = (powers[part, :] * coefficient[c : c + 1, :]).astype(
            jnp.bfloat16
        )


def other_grad_body(
    passages, embed, powers1, powers2, totals1, totals2, sent1, sent2,
    first1, own1, third1, first2, second2, own2, to_query1, to_query2, grad_sim,
):
    rows = powers1.shape[1]
    turned = embed[...].T
    for column, powers, totals, sent, parts, own, out in (
        (rows, powers2, totals2, sent2, (first2, second2, own2), own2, to_query2),
        (0, powers1, totals1, sent1, (first1, own1, third1), own1, to_query1),
    ):
        log_total = score_softmax(*[part[...] for part in parts])
        dscore = loss_scale * jnp.exp(own[...] - log_total)
        coefficient = outer_scale * dscore * sent_keep(sent, rows) / totals[...]
        fill_grad_sim(passages, coefficient, powers, grad_sim, column)
        out[...] = dot32(turned, grad_sim[:, column : column + rows]).astype(jnp.bfloat16)


def own_grad_body(
    queries, passages, positives, hidden, embed, before, powers, totals, sent0, sent1, sent2,
    own, second, third, other_grad_sim,
    losses, to_query, pre_grad, partial, grad_sim,
):
    rows = powers.shape[1]
    scores = own[...]
    log_total = score_softmax(scores, second[...], third[...])
    wanted = spread(positives, queries, rows // queries)
    onehot = lax.broadcasted_iota(jnp.int32, scores.shape, 0) == wanted
    losses[...] = log_total - jnp.sum(jnp.where(onehot, scores, 0.0), axis=0, keepdims=True)
    dscore = loss_scale * (jnp.exp(scores - log_total) - onehot.astype(jnp.float32))
    coefficient = outer_scale * dscore * sent_keep(sent0, rows) / totals[...]
    fill_grad_sim(passages, coefficient, powers, grad_sim, 0)
    to_query[...] = dot32(embed[...].T, grad_sim[...])
    grad = dot32(grad_sim[...], sent0[:rows, :])
    grad += dot32(other_grad_sim[:, :rows], sent1[:rows, :])
    grad += dot32(other_grad_sim[:, rows:], sent2[:rows, :])
    pre = back_rows(grad, before[...])
    pre_grad[...] = pre
    partial[...] = dot32(pre.T, hidden[...])


def query_grad_body(hidden, before, own, back1, back2, passage_partial, pre_grad, partial):
    total = own[...] + back1[...].astype(jnp.float32) + back2[...].astype(jnp.float32)
    pre = back_rows(total.T, before[...])
    pre_grad[...] = pre
    both = passage_partial[...] + dot32(pre.T, hidden[...])
    partial[...] = both.T.astype(jnp.bfloat16)


def mean_over_devices(partial):
    axes = ("batch", "mp")
    devices = lax.axis_size("batch") * lax.axis_size("mp")
    rows, columns = partial.shape
    share = -(-rows // (devices * 8)) * 8
    padded = jnp.pad(partial, ((0, share * devices - rows), (0, 0)))
    pieces = padded.reshape(devices, share, columns)
    pieces = lax.all_to_all(pieces, axes, 0, 0)
    mean = (jnp.sum(pieces.astype(jnp.float32), axis=0) / devices).astype(jnp.bfloat16)
    whole = lax.all_to_all(jnp.broadcast_to(mean[None], (devices, share, columns)), axes, 0, 0)
    return whole.reshape(devices * share, columns)[:rows].astype(jnp.float32)


def per_device(query_hidden, passage_hidden, projection, query_lengths, passage_lengths, positives):
    queries = query_lengths.shape[0]
    passages = passage_lengths.shape[0]
    rows, width = query_hidden.shape
    slots = passage_hidden.shape[0]
    dim = projection.shape[1]
    f32, bf16 = jnp.float32, jnp.bfloat16
    of = jax.ShapeDtypeStruct
    pair = of((ROWS, rows), f32)
    pairs = pltpu.VMEM((ROWS, rows), f32)

    query_before, sent0 = call(
        functools.partial(query_embed_body, queries),
        (of((rows, dim), f32), of((rows + ROWS, dim), bf16)),
        (smem, vmem, vmem),
        (query_lengths, query_hidden, projection),
        flops=2 * rows * width * dim,
    )
    sent1 = shifted(sent0, "batch", 1)
    sent2 = shifted(sent0, "batch", 2)
    passage_before, embed, powers0, totals0, scores0 = call(
        functools.partial(own_score_body, queries),
        (of((slots, dim), f32), of((slots, dim), bf16), of((slots, rows), f32), pair, pair),
        (smem, vmem, vmem, vmem),
        (passage_lengths, passage_hidden, projection, sent0),
        scratch=(pairs,),
        flops=2 * slots * dim * (width + rows),
        trans=slots * rows,
    )
    first1 = shifted(scores0, "batch", 1)
    first2 = shifted(scores0, "batch", 2)
    powers1, powers2, totals1, totals2, scores1, scores2 = call(
        functools.partial(other_score_body, queries),
        (of((slots, rows), f32),) * 2 + (pair,) * 4,
        (smem, vmem, vmem, vmem),
        (passage_lengths, embed, sent1, sent2),
        scratch=(pairs,),
        flops=4 * slots * dim * rows,
        trans=2 * slots * rows,
    )
    second2 = shifted(scores1, "batch", 1)
    below = shifted(jnp.concatenate([scores1, scores2], axis=0), "batch", -1)
    second0, third1 = below[:ROWS], below[ROWS:]
    third0 = shifted(scores2, "batch", -2)
    to_query1, to_query2, grad_sim = call(
        functools.partial(other_grad_body, passages),
        (of((dim, rows), bf16),) * 2 + (of((slots, 2 * rows), bf16),),
        (vmem,) * 13,
        (embed, powers1, powers2, totals1, totals2, sent1, sent2,
         first1, scores1, third1, first2, second2, scores2),
        flops=4 * slots * dim * rows,
    )
    back1 = shifted(to_query1, "batch", -1)
    back2 = shifted(to_query2, "batch", -2)
    losses, to_query0, passage_pre_grad, passage_partial = call(
        functools.partial(own_grad_body, queries, passages),
        (of((1, rows), f32), of((dim, rows), f32), of((slots, dim), bf16), of((dim, width), f32)),
        (smem,) + (vmem,) * 12,
        (positives, passage_hidden, embed, passage_before, powers0, totals0, sent0, sent1, sent2,
         scores0, second0, third0, grad_sim),
        scratch=(pltpu.VMEM((slots, rows), bf16),),
        flops=8 * slots * dim * rows + 2 * slots * width * dim,
    )
    query_pre_grad, partial = call(
        query_grad_body,
        (of((rows, dim), bf16), of((width, dim), bf16)),
        (vmem,) * 6,
        (query_hidden, query_before, to_query0, back1, back2, passage_partial),
        flops=2 * rows * width * dim,
    )
    grad_projection = mean_over_devices(partial)
    grad_query_hidden = dot32(query_pre_grad, projection, NT).astype(bf16)
    grad_passage_hidden = dot32(passage_pre_grad, projection, NT).astype(bf16)
    losses = losses.reshape(queries, rows // queries)[:, 0]
    return (losses, grad_query_hidden, grad_passage_hidden, grad_projection)


def solution(mesh):
    in_specs = (
        P(("batch", "mp"), None),
        P(("batch", "mp"), None),
        P(),
        P(("batch", "mp")),
        P(("batch", "mp")),
        P(("batch", "mp")),
    )
    out_specs = (P(("batch", "mp")), P(("batch", "mp"), None), P(("batch", "mp"), None), P())
    return jax.shard_map(
        per_device, mesh=mesh, in_specs=in_specs, out_specs=out_specs, check_vma=False
    )
```

profile of v0, /device:TPU:1, one launch (start us, length us, event | category | flops | bytes accessed | tf_op | source)
XLA Modules:
  0.0 59.8 jit_solution(3656278852737202180)
XLA Ops:
  0.6 0.0 copy-start.2
  0.6 0.9 %copy-done.2 = bf16[768,128]{1,0:T(8,128)(2,1)S(1)} copy-done((bf16[768,128]{1,0:T(8,128)(2,1)S(1)}, bf16[768,128]{1,0:T(8,128)(2,1)}, u32[]{:S(2)}) %copy-start.2) | copy-done | bytes 196632
  1.6 1.0 %copy-done.5 = bf16[256,768]{1,0:T(8,128)(2,1)S(1)} copy-done((bf16[256,768]{1,0:T(8,128)(2,1)S(1)}, bf16[256,768]{1,0:T(8,128)(2,1)}, u32[]{:S(2)}) %copy-start.5) | copy-done | bytes 393240
  2.6 0.7 %copy-done.8 = s32[8]{0:T(128)S(1)} copy-done((s32[8]{0:T(128)S(1)}, s32[8]{0:T(128)}, u32[]{:S(2)}) %copy-start.8) | copy-done | bytes 56
  3.2 0.9 %shard_map.93 = (f32[256,128]{1,0:T(8,128)S(1)}, bf16[272,128]{1,0:T(8,128)(2,1)S(1)}) custom-call(s32[8]{0:T(128)S(1)} %copy-done.8, bf16[256,768]{1,0:T(8,128)(2,1)S(1)} %copy-done.5, bf16[768,128]{1,0:T(8,128)(2,1)S(1)} %copy-done.2), custom_call_target="tpu_custom_call" | custom-call | flops 50331648 | bytes 790560 | tf_op jit(solution)/shard_map/pallas_call | solution.py:38
  4.1 2.1 %collective-permute-start = (bf16[272,128]{1,0:T(8,128)(2,1)S(1)}, bf16[272,128]{1,0:T(8,128)(2,1)S(1)}, u32[]{:S(2)}, u32[]{:S(2)}) collective-permute-start(bf16[272,128]{1,0:T(8,128)(2,1)S(1)} %get-tuple-element.26.sent.sent0), channel_id=1, source_target_pairs={{28,0},{0,4},{4,8},{8,12},{12,16},{16,20},{20,24},{24,28},{29,1},{... | collective-permute-start | bytes 208904 | tf_op jit(solution)/shard_map/ppermute | solution.py:28
  6.2 1.3 %collective-permute-start.1 = (bf16[272,128]{1,0:T(8,128)(2,1)S(1)}, bf16[272,128]{1,0:T(8,128)(2,1)S(1)}, u32[]{:S(2)}, u32[]{:S(2)}) collective-permute-start(bf16[272,128]{1,0:T(8,128)(2,1)S(1)} %get-tuple-element.26.sent.sent0), channel_id=1, source_target_pairs={{24,0},{28,4},{0,8},{4,12},{8,16},{12,20},{16,24},{20,28},{25,1},{... | collective-permute-start | bytes 208904 | tf_op jit(solution)/shard_map/ppermute | solution.py:28
  7.5 1.5 %copy-done = bf16[1280,768]{1,0:T(8,128)(2,1)S(1)} copy-done((bf16[1280,768]{1,0:T(8,128)(2,1)S(1)}, bf16[1280,768]{1,0:T(8,128)(2,1)}, u32[]{:S(2)}) %copy-start) | copy-done | bytes 1966104
  9.0 0.9 %copy-done.3 = bf16[768,128]{1,0:T(8,128)(2,1)S(1)} copy-done((bf16[768,128]{1,0:T(8,128)(2,1)S(1)}, bf16[768,128]{1,0:T(8,128)(2,1)}, u32[]{:S(2)}) %copy-start.3) | copy-done | bytes 196632
  10.0 0.7 %copy-done.7 = s32[10]{0:T(128)S(1)} copy-done((s32[10]{0:T(128)S(1)}, s32[10]{0:T(128)}, u32[]{:S(2)}) %copy-start.7) | copy-done | bytes 64
  10.6 2.0 %shard_map.94 = (f32[1280,128]{1,0:T(8,128)S(1)}, bf16[1280,128]{1,0:T(8,128)(2,1)S(1)}, f32[1280,256]{1,0:T(8,128)S(1)}, f32[16,256]{1,0:T(8,128)S(1)}, f32[16,256]{1,0:T(8,128)S(1)}) custom-call(s32[10]{0:T(128)S(1)} %copy-done.7, bf16[1280,768]{1,0:T(8,128)(2,1)S(1)} %copy-done, bf16[768,128]{1,0:T(8,128)(2,1)S(1)} %copy-done.3, ...), custom_call_target="tpu_custom_call" | custom-call | flops 335544320 | bytes 4558888 | tf_op jit(solution)/shard_map/pallas_call | solution.py:38
  12.6 0.0 collective-permute-done.sent1
  12.6 0.0 collective-permute-done.1.sent2
  12.7 1.7 %shard_map.95 = (f32[1280,256]{1,0:T(8,128)S(1)}, f32[1280,256]{1,0:T(8,128)S(1)}, f32[16,256]{1,0:T(8,128)S(1)}, f32[16,256]{1,0:T(8,128)S(1)}, f32[16,256]{1,0:T(8,128)S(1)}, /*index=5*/f32[16,256]{1,0:T(8,128)S(1)}) custom-call(s32[10]{0:T(128)S(1)} %copy-done.7, bf16[1280,128]{1,0:T(8,128)(2,1)S(1)} %get-tuple-element.27.embed, ...), custom_call_target="tpu_custom_call" | custom-call | flops 167772160 | bytes 3153960 | tf_op jit(solution)/shard_map/pallas_call | solution.py:38
  14.4 0.0 copy-start.1
  14.4 0.0 copy-start.9
  14.5 3.0 %collective-permute-start.2 = (f32[32,256]{1,0:T(8,128)S(1)}, f32[32,256]{1,0:T(8,128)S(1)}, u32[]{:S(2)}, u32[]{:S(2)}) collective-permute-start(f32[32,256]{1,0:T(8,128)S(1)} %pad_maximum_fusion), channel_id=1, source_target_pairs={{4,0},{8,4},{12,8},{16,12},{20,16},{24,20},{28,24},{0,28},{5,1},{9... | collective-permute-start | bytes 98312 | tf_op jit(solution)/shard_map/ppermute | solution.py:28
  17.5 0.0 collective-permute-start.4
  17.5 0.0 collective-permute-start.5
  17.5 2.0 %collective-permute-start.6 = (f32[16,256]{1,0:T(8,128)S(1)}, f32[16,256]{1,0:T(8,128)S(1)}, u32[]{:S(2)}, u32[]{:S(2)}) collective-permute-start(f32[16,256]{1,0:T(8,128)S(1)} %get-tuple-element.32.own1), channel_id=1, source_target_pairs={{28,0},{0,4},{4,8},{8,12},{12,16},{16,20},{20,24},{24,28},{29,1},{... | collective-permute-start | bytes 49160 | tf_op jit(solution)/shard_map/ppermute | solution.py:28
  19.4 2.5 %collective-permute-start.3 = (f32[16,256]{1,0:T(8,128)S(1)}, f32[16,256]{1,0:T(8,128)S(1)}, u32[]{:S(2)}, u32[]{:S(2)}) collective-permute-start(f32[16,256]{1,0:T(8,128)S(1)} %get-tuple-element.33.own2), channel_id=1, source_target_pairs={{8,0},{12,4},{16,8},{20,12},{24,16},{28,20},{0,24},{4,28},{9,1},{1... | collective-permute-start | bytes 49160 | tf_op jit(solution)/shard_map/ppermute | solution.py:28
  21.9 0.0 collective-permute-done.2
  21.9 0.8 %collective-permute-done.4.first1 = f32[16,256]{1,0:T(8,128)S(1)} collective-permute-done((f32[16,256]{1,0:T(8,128)S(1)}, f32[16,256]{1,0:T(8,128)S(1)}, u32[]{:S(2)}, u32[]{:S(2)}) %collective-permute-start.4) | collective-permute-done | bytes 16416 | tf_op jit(solution)/shard_map/ppermute | solution.py:28
  22.7 0.0 collective-permute-done.5.first2
  22.8 0.4 collective-permute-done.6.second2
  23.1 0.5 shard_map.96
  23.6 1.4 %collective-permute-start.7 = (bf16[128,256]{1,0:T(8,128)(2,1)S(1)}, bf16[128,256]{1,0:T(8,128)(2,1)S(1)}, u32[]{:S(2)}, u32[]{:S(2)}) collective-permute-start(bf16[128,256]{1,0:T(8,128)(2,1)S(1)} %get-tuple-element.42), channel_id=1, source_target_pairs={{4,0},{8,4},{12,8},{16,12},{20,16},{24,20},{28,24},{0,28},{5,1},{9... | collective-permute-start | bytes 196616 | tf_op jit(solution)/shard_map/ppermute | solution.py:28
  25.0 1.2 %collective-permute-start.8 = (bf16[128,256]{1,0:T(8,128)(2,1)S(1)}, bf16[128,256]{1,0:T(8,128)(2,1)S(1)}, u32[]{:S(2)}, u32[]{:S(2)}) collective-permute-start(bf16[128,256]{1,0:T(8,128)(2,1)S(1)} %get-tuple-element.43), channel_id=1, source_target_pairs={{8,0},{12,4},{16,8},{20,12},{24,16},{28,20},{0,24},{4,28},{9,1},{1... | collective-permute-start | bytes 196616 | tf_op jit(solution)/shard_map/ppermute | solution.py:28
  26.2 0.0 collective-permute-done.3.third
  26.2 0.0 copy-done.9
  26.2 0.0 copy-start.6
  26.2 2.2 %shard_map.97 = (f32[1,256]{1,0:T(1,128)S(1)}, f32[128,256]{1,0:T(8,128)S(1)}, bf16[1280,128]{1,0:T(8,128)(2,1)S(1)}, f32[128,768]{1,0:T(8,128)S(1)}) custom-call(s32[8]{0:T(128)S(1)} %copy-done.9, bf16[1280,768]{1,0:T(8,128)(2,1)S(1)} %copy-done.1, bf16[1280,128]{1,0:T(8,128)(2,1)S(1)} %get-tuple-element.27.embed, ...), custom_call_target="tpu_custom_call" | custom-call | flops 587202560 | bytes 6698016 | tf_op jit(solution)/shard_map/pallas_call | solution.py:38
  28.5 0.0 copy-start.4
  28.5 0.0 collective-permute-done.7.back1
  28.5 0.0 collective-permute-done.8.back2
  28.5 0.5 shard_map.98
  29.1 17.6 %all_to_all.10 = bf16[32,24,128]{2,1,0:T(8,128)(2,1)S(1)} all-to-all(bf16[32,24,128]{2,1,0:T(8,128)(2,1)S(1)} %bitcast.10), channel_id=1, replica_groups=mesh['batch'=8,'mp'=4] {'batch','mp'}, dimensions={0} | all-to-all | bytes 393216 | tf_op jit(solution)/shard_map/all_to_all | solution.py:214
  46.7 0.7 %broadcast_in_dim.2 = bf16[32,24,128]{2,1,0:T(8,128)(2,1)} broadcast(bf16[24,128]{1,0:T(8,128)(2,1)S(1)} %multiply_convert_fusion), dimensions={1,2} | broadcast | bytes 202752 | tf_op jit(solution)/shard_map/broadcast_in_dim | solution.py:216
  47.4 2.4 %all-to-all-start.1 = ((bf16[32,24,128]{2,1,0:T(8,128)(2,1)}), bf16[32,24,128]{2,1,0:T(8,128)(2,1)S(1)}, u32[]{:S(2)}, u32[]{:S(2)}) async-start(bf16[32,24,128]{2,1,0:T(8,128)(2,1)} %broadcast_in_dim.2), calls=%async_computation.1 | async-start | bytes 393216 | tf_op jit(solution)/shard_map/all_to_all | solution.py:216
  49.8 0.0 copy-done.4
  49.8 1.9 %convolution_convert_fusion = bf16[1280,768]{1,0:T(8,128)(2,1)} fusion(bf16[1280,128]{1,0:T(8,128)(2,1)S(1)} %get-tuple-element.46, bf16[768,128]{1,0:T(8,128)(2,1)S(1)} %copy-done.4), kind=kOutput, calls=%fused_computation | convolution fusion | flops 252641280 | bytes 2490368 | tf_op jit(solution)/shard_map/dot_general | solution.py:32
  51.8 0.5 broadcast.8
  52.3 0.7 %reduce.3 = f32[256]{0:T(256)S(1)} reduce(f32[1,256]{1,0:T(1,128)S(1)} %get-tuple-element.39, f32[]{:T(128)} %broadcast.8), dimensions={0}, to_apply=%get-tuple-element.39.reduce_sub_computation.3 | reduce | bytes 2052 | tf_op jit(solution)/shard_map/pallas_call | solution.py:38
  53.0 0.1 reshape.21
  53.0 0.6 copy.11
  53.6 1.0 %convolution_convert_fusion.1 = bf16[256,768]{1,0:T(8,128)(2,1)} fusion(bf16[256,128]{1,0:T(8,128)(2,1)S(1)} %get-tuple-element.45, bf16[768,128]{1,0:T(8,128)(2,1)S(1)} %copy-done.4), kind=kOutput, calls=%fused_computation.1 | convolution fusion | flops 50528256 | bytes 655360 | tf_op jit(solution)/shard_map/dot_general | solution.py:32
  54.6 4.4 %all-to-all-done.1 = bf16[32,24,128]{2,1,0:T(8,128)(2,1)S(1)} async-done(((bf16[32,24,128]{2,1,0:T(8,128)(2,1)}), bf16[32,24,128]{2,1,0:T(8,128)(2,1)S(1)}, u32[]{:S(2)}, u32[]{:S(2)}) %all-to-all-start.1) | async-done | bytes 196640 | tf_op jit(solution)/shard_map/all_to_all | solution.py:216
  59.1 0.8 %bitcast_convert_fusion = f32[768,128]{1,0:T(8,128)} fusion(bf16[32,24,128]{2,1,0:T(8,128)(2,1)S(1)} %all-to-all-done.1), kind=kLoop, calls=%fused_computation.3 | loop fusion | flops 98304 | bytes 589824 | tf_op jit(solution)/shard_map/convert_element_type | solution.py:217
  (11 shorter events, 0.1 us)
Async XLA Ops:
  0.6 0.9 %copy-start.2 = (bf16[768,128]{1,0:T(8,128)(2,1)S(1)}, bf16[768,128]{1,0:T(8,128)(2,1)}, u32[]{:S(2)}) copy-start(bf16[768,128]{1,0:T(8,128)(2,1)} %projection.3) | copy-start | bytes 589828
  1.6 1.0 %copy-start.5 = (bf16[256,768]{1,0:T(8,128)(2,1)S(1)}, bf16[256,768]{1,0:T(8,128)(2,1)}, u32[]{:S(2)}) copy-start(bf16[256,768]{1,0:T(8,128)(2,1)} %hidden.7) | copy-start | bytes 1179652
  2.6 0.7 %copy-start.8 = (s32[8]{0:T(128)S(1)}, s32[8]{0:T(128)}, u32[]{:S(2)}) copy-start(s32[8]{0:T(128)} %lengths.3) | copy-start | bytes 100
  4.1 8.6 %collective-permute-start = (bf16[272,128]{1,0:T(8,128)(2,1)S(1)}, bf16[272,128]{1,0:T(8,128)(2,1)S(1)}, u32[]{:S(2)}, u32[]{:S(2)}) collective-permute-start(bf16[272,128]{1,0:T(8,128)(2,1)S(1)} %get-tuple-element.26.sent.sent0), channel_id=1, source_target_pairs={{28,0},{0,4},{4,8},{8,12},{12,16},{16,20},{20,24},{24,28},{29,1},{... | collective-permute-start | bytes 208904 | tf_op jit(solution)/shard_map/ppermute | solution.py:28
  6.2 6.5 %collective-permute-start.1 = (bf16[272,128]{1,0:T(8,128)(2,1)S(1)}, bf16[272,128]{1,0:T(8,128)(2,1)S(1)}, u32[]{:S(2)}, u32[]{:S(2)}) collective-permute-start(bf16[272,128]{1,0:T(8,128)(2,1)S(1)} %get-tuple-element.26.sent.sent0), channel_id=1, source_target_pairs={{24,0},{28,4},{0,8},{4,12},{8,16},{12,20},{16,24},{20,28},{25,1},{... | collective-permute-start | bytes 208904 | tf_op jit(solution)/shard_map/ppermute | solution.py:28
  7.5 1.5 %copy-start = (bf16[1280,768]{1,0:T(8,128)(2,1)S(1)}, bf16[1280,768]{1,0:T(8,128)(2,1)}, u32[]{:S(2)}) copy-start(bf16[1280,768]{1,0:T(8,128)(2,1)} %hidden.6) | copy-start | bytes 5898244
  9.0 0.9 %copy-start.3 = (bf16[768,128]{1,0:T(8,128)(2,1)S(1)}, bf16[768,128]{1,0:T(8,128)(2,1)}, u32[]{:S(2)}) copy-start(bf16[768,128]{1,0:T(8,128)(2,1)} %projection.3) | copy-start | bytes 589828
  10.0 0.7 %copy-start.7 = (s32[10]{0:T(128)S(1)}, s32[10]{0:T(128)}, u32[]{:S(2)}) copy-start(s32[10]{0:T(128)} %lengths.5) | copy-start | bytes 124
  14.4 11.8 %copy-start.1 = (bf16[1280,768]{1,0:T(8,128)(2,1)S(1)}, bf16[1280,768]{1,0:T(8,128)(2,1)}, u32[]{:S(2)}) copy-start(bf16[1280,768]{1,0:T(8,128)(2,1)} %hidden.6) | copy-start | bytes 5898244
  14.4 11.8 %copy-start.9 = (s32[8]{0:T(128)S(1)}, s32[8]{0:T(128)}, u32[]{:S(2)}) copy-start(s32[8]{0:T(128)} %positives.1) | copy-start | bytes 100
  14.5 7.5 %collective-permute-start.2 = (f32[32,256]{1,0:T(8,128)S(1)}, f32[32,256]{1,0:T(8,128)S(1)}, u32[]{:S(2)}, u32[]{:S(2)}) collective-permute-start(f32[32,256]{1,0:T(8,128)S(1)} %pad_maximum_fusion), channel_id=1, source_target_pairs={{4,0},{8,4},{12,8},{16,12},{20,16},{24,20},{28,24},{0,28},{5,1},{9... | collective-permute-start | bytes 98312 | tf_op jit(solution)/shard_map/ppermute | solution.py:28
  17.5 5.3 %collective-permute-start.4 = (f32[16,256]{1,0:T(8,128)S(1)}, f32[16,256]{1,0:T(8,128)S(1)}, u32[]{:S(2)}, u32[]{:S(2)}) collective-permute-start(f32[16,256]{1,0:T(8,128)S(1)} %get-tuple-element.31.own), channel_id=1, source_target_pairs={{28,0},{0,4},{4,8},{8,12},{12,16},{16,20},{20,24},{24,28},{29,1},{... | collective-permute-start | bytes 49160 | tf_op jit(solution)/shard_map/ppermute | solution.py:28
  17.5 5.3 %collective-permute-start.5 = (f32[16,256]{1,0:T(8,128)S(1)}, f32[16,256]{1,0:T(8,128)S(1)}, u32[]{:S(2)}, u32[]{:S(2)}) collective-permute-start(f32[16,256]{1,0:T(8,128)S(1)} %get-tuple-element.31.own), channel_id=1, source_target_pairs={{24,0},{28,4},{0,8},{4,12},{8,16},{12,20},{16,24},{20,28},{25,1},{... | collective-permute-start | bytes 49160 | tf_op jit(solution)/shard_map/ppermute | solution.py:28
  17.5 5.7 %collective-permute-start.6 = (f32[16,256]{1,0:T(8,128)S(1)}, f32[16,256]{1,0:T(8,128)S(1)}, u32[]{:S(2)}, u32[]{:S(2)}) collective-permute-start(f32[16,256]{1,0:T(8,128)S(1)} %get-tuple-element.32.own1), channel_id=1, source_target_pairs={{28,0},{0,4},{4,8},{8,12},{12,16},{16,20},{20,24},{24,28},{29,1},{... | collective-permute-start | bytes 49160 | tf_op jit(solution)/shard_map/ppermute | solution.py:28
  19.4 6.8 %collective-permute-start.3 = (f32[16,256]{1,0:T(8,128)S(1)}, f32[16,256]{1,0:T(8,128)S(1)}, u32[]{:S(2)}, u32[]{:S(2)}) collective-permute-start(f32[16,256]{1,0:T(8,128)S(1)} %get-tuple-element.33.own2), channel_id=1, source_target_pairs={{8,0},{12,4},{16,8},{20,12},{24,16},{28,20},{0,24},{4,28},{9,1},{1... | collective-permute-start | bytes 49160 | tf_op jit(solution)/shard_map/ppermute | solution.py:28
  23.6 4.9 %collective-permute-start.7 = (bf16[128,256]{1,0:T(8,128)(2,1)S(1)}, bf16[128,256]{1,0:T(8,128)(2,1)S(1)}, u32[]{:S(2)}, u32[]{:S(2)}) collective-permute-start(bf16[128,256]{1,0:T(8,128)(2,1)S(1)} %get-tuple-element.42), channel_id=1, source_target_pairs={{4,0},{8,4},{12,8},{16,12},{20,16},{24,20},{28,24},{0,28},{5,1},{9... | collective-permute-start | bytes 196616 | tf_op jit(solution)/shard_map/ppermute | solution.py:28
  25.0 3.5 %collective-permute-start.8 = (bf16[128,256]{1,0:T(8,128)(2,1)S(1)}, bf16[128,256]{1,0:T(8,128)(2,1)S(1)}, u32[]{:S(2)}, u32[]{:S(2)}) collective-permute-start(bf16[128,256]{1,0:T(8,128)(2,1)S(1)} %get-tuple-element.43), channel_id=1, source_target_pairs={{8,0},{12,4},{16,8},{20,12},{24,16},{28,20},{0,24},{4,28},{9,1},{1... | collective-permute-start | bytes 196616 | tf_op jit(solution)/shard_map/ppermute | solution.py:28
  26.2 2.3 %copy-start.6 = (bf16[256,768]{1,0:T(8,128)(2,1)S(1)}, bf16[256,768]{1,0:T(8,128)(2,1)}, u32[]{:S(2)}) copy-start(bf16[256,768]{1,0:T(8,128)(2,1)} %hidden.7) | copy-start | bytes 1179652
  28.5 21.3 %copy-start.4 = (bf16[768,128]{1,0:T(8,128)(2,1)S(1)}, bf16[768,128]{1,0:T(8,128)(2,1)}, u32[]{:S(2)}) copy-start(bf16[768,128]{1,0:T(8,128)(2,1)} %projection.3) | copy-start | bytes 589828
  47.4 11.6 %all-to-all-start.1 = ((bf16[32,24,128]{2,1,0:T(8,128)(2,1)}), bf16[32,24,128]{2,1,0:T(8,128)(2,1)S(1)}, u32[]{:S(2)}, u32[]{:S(2)}) async-start(bf16[32,24,128]{2,1,0:T(8,128)(2,1)} %broadcast_in_dim.2), calls=%async_computation.1 | async-start | bytes 393216 | tf_op jit(solution)/shard_map/all_to_all | solution.py:216
where the time goes:
time: 60.2 us; the launch traced here: 59.8 us
  blocking collectives  17.6 us (29%)
  starting transfers between devices  15.8 us (26%)
  Pallas kernels  7.88 us (13%)
  local copies, waits for them, and re-layouts  7.64 us (13%)
  waiting for transfers between devices  5.64 us (9%)
  matrix products  2.96 us (5%)
  other arithmetic  1.5 us (2%)
  between operations  0.78 us (1%)
    all_to_all x1, blocking collectives, mean_over_devices(): pieces = lax.all_to_all(pieces, axes, 0, 0)  17.6 us
    ppermute x9, starting transfers between devices, shifted(): return lax.ppermute(block, axis, route)  13.5 us
    pallas_call x6, Pallas kernels, call(): pl.pallas_call(body, out_shape=tuple(outs), in_specs=list(in_specs), out_...  7.88 us
    unnamed x21, local copies, waits for them, and re-layouts  6.34 us
    all_to_all x1, waiting for transfers between devices, mean_over_devices(): lax.all_to_all(jnp.broadcast_to(mean[None], (devices, share, columns)), a...  4.42 us
    dot_general x2, matrix products, dot32(): lax.dot_general(left, right, dims, preferred_element_type=jnp.float32)  2.96 us
    all_to_all x1, starting transfers between devices, mean_over_devices(): lax.all_to_all(jnp.broadcast_to(mean[None], (devices, share, columns)), a...  2.37 us
    ppermute x9, waiting for transfers between devices, shifted(): return lax.ppermute(block, axis, route)  1.23 us
  transfers between devices with their start and end apart: 10, of which 3 were waited for; matrix products, arithmetic and copies ran while one was open for 8% of the time, Pallas kernels for 8%

commit v1 on v0

--- a/solution.py
+++ b/solution.py
@@ -19,7 +19,7 @@
 NT = (((1,), (1,)), ((), ()))
 
 vmem = pl.BlockSpec(memory_space=pltpu.VMEM)
-smem = pl.BlockSpec(memory_space=pltpu.SMEM)
+hbm = pl.BlockSpec(memory_space=pltpu.HBM)
 
 
 def shifted(block, axis, distance):
@@ -70,17 +70,47 @@
     return ((grad - unit * inner) * inverse).astype(jnp.bfloat16)
 
 
-def query_embed_body(queries, lengths, hidden, projection, before_out, sent_out):
-    rows = hidden.shape[0]
-    before = dot32(hidden[...], projection[...])
+def load_all(pairs, sems):
+    copies = [pltpu.make_async_copy(a, b, sems.at[i]) for i, (a, b) in enumerate(pairs)]
+    for copy in copies:
+        copy.start()
+    return copies
+
+
+def query_embed_body(
+    queries, query_lengths_in, passage_lengths_in, positives_in, query_hidden_in, passage_hidden_in,
+    projection_in,
+    before_out, sent_out, slots_out, wanted_out, query_hidden, passage_hidden, projection,
+    query_lengths, passage_lengths, positives, sems,
+):
+    pairs = (
+        (projection_in, projection), (query_hidden_in, query_hidden),
+        (query_lengths_in, query_lengths), (positives_in, positives),
+        (passage_lengths_in, passage_lengths), (passage_hidden_in, passage_hidden),
+    )
+    copies = load_all(pairs, sems)
+    copies[0].wait()
+    copies[1].wait()
+    rows = query_hidden.shape[0]
+    before = dot32(query_hidden[...], projection[...])
     before_out[...] = before
     sent_out[:rows, :] = unit_rows(before)[0].astype(jnp.bfloat16)
-    keep = keep_row(lengths, queries, rows // queries)
+    copies[2].wait()
+    keep = keep_row(query_lengths, queries, rows // queries)
     row = lax.broadcasted_iota(jnp.int32, (ROWS, LANES), 0)
     tail = jnp.zeros((ROWS, LANES), jnp.float32)
     for piece in range(rows // LANES):
         tail = jnp.where(row == piece, keep[:, piece * LANES : (piece + 1) * LANES], tail)
     sent_out[rows:, :] = tail.astype(jnp.bfloat16)
+    copies[3].wait()
+    wanted_out[...] = spread(positives, queries, rows // queries)
+    copies[4].wait()
+    c = lax.broadcasted_iota(jnp.int32, slots_out.shape, 0)
+    valid = jnp.zeros(slots_out.shape, jnp.int32)
+    for item in range(passage_lengths.shape[0]):
+        valid = jnp.where(c == item, passage_lengths[item], valid)
+    slots_out[...] = valid
+    copies[5].wait()
 
 
 def sent_keep(sent, rows):
@@ -88,7 +118,7 @@
     return jnp.concatenate([tail[i : i + 1, :] for i in range(rows // LANES)], axis=1)
 
 
-def score_block(queries, passages, lengths, embed, sent, powers, totals, scores, tops):
+def score_block(queries, passages, valid, embed, sent, powers, totals, scores, tops):
     rows = sent.shape[0] - ROWS
     tokens = embed.shape[0] // passages
     query = sent[:rows, :]
@@ -98,7 +128,7 @@
     for c in range(passages):
         part = slice(c * tokens, (c + 1) * tokens)
         sims = dot32(embed[part, :], query, NT)
-        sims = jnp.where(slot < lengths[c], sims, -jnp.inf)
+        sims = jnp.where(slot < valid[c : c + 1, :], sims, -jnp.inf)
         top = jnp.max(sims, axis=0, keepdims=True)
         power = jnp.exp2((sims - top) * (inner_scale * LOG2E))
         powers[part, :] = power
@@ -119,31 +149,39 @@
 
 
 def own_score_body(
-    queries, lengths, hidden, projection, sent, before_out, embed_out, powers, totals, scores, tops
+    queries, passages, valid, hidden, projection, sent,
+    before_out, embed_out, powers, totals, scores, tops,
 ):
     before = dot32(hidden[...], projection[...])
     before_out[...] = before
     embed_out[...] = unit_rows(before)[0].astype(jnp.bfloat16)
-    score_block(
-        queries, lengths.shape[0], lengths, embed_out, sent, powers, totals, scores, tops
-    )
+    score_block(queries, passages, valid, embed_out, sent, powers, totals, scores, tops)
+
+
+def log_sum(scores):
+    top = jnp.max(scores, axis=0, keepdims=True)
+    return top + jnp.log(jnp.sum(jnp.exp(scores - top), axis=0, keepdims=True))
 
 
 def other_score_body(
-    queries, lengths, embed, sent1, sent2, powers1, powers2, totals1, totals2, scores1, scores2, tops
-):
-    passages = lengths.shape[0]
-    score_block(queries, passages, lengths, embed, sent1, powers1, totals1, scores1, tops)
-    score_block(queries, passages, lengths, embed, sent2, powers2, totals2, scores2, tops)
-
-
-def score_softmax(first, second, third):
-    parts = (first, second, third)
-    top = functools.reduce(
-        jnp.maximum, [jnp.max(part, axis=0, keepdims=True) for part in parts]
-    )
-    total = sum(jnp.sum(jnp.exp(part - top), axis=0, keepdims=True) for part in parts)
-    return top + jnp.log(total)
+    queries, passages, valid, embed, sent1, sent2, scores0,
+    powers1, powers2, totals1, totals2, scores1, scores2, logs, tops,
+):
+    score_block(queries, passages, valid, embed, sent1, powers1, totals1, scores1, tops)
+    score_block(queries, passages, valid, embed, sent2, powers2, totals2, scores2, tops)
+    row = lax.broadcasted_iota(jnp.int32, logs.shape[1:], 0)
+    mine = jnp.zeros(logs.shape[1:], jnp.float32)
+    for part, scores in enumerate((scores0, scores1, scores2)):
+        mine = jnp.where(row == part, log_sum(scores[...]), mine)
+    for target in range(logs.shape[0]):
+        logs[target] = mine
+
+
+def all_logs(logs, block):
+    count = logs.shape[0]
+    parts = [logs[lax.rem(block + t, count)][t : t + 1, :] for t in range(3)]
+    top = functools.reduce(jnp.maximum, parts)
+    return top + jnp.log(sum(jnp.exp(part - top) for part in parts))
 
 
 def fill_grad_sim(passages, coefficient, powers, out, column):
@@ -158,15 +196,18 @@
 
 def other_grad_body(
     passages, embed, powers1, powers2, totals1, totals2, sent1, sent2,
-    first1, own1, third1, first2, second2, own2, to_query1, to_query2, grad_sim,
+    scores1, scores2, logs, to_query1, to_query2, grad_sim,
 ):
     rows = powers1.shape[1]
     turned = embed[...].T
-    for column, powers, totals, sent, parts, own, out in (
-        (rows, powers2, totals2, sent2, (first2, second2, own2), own2, to_query2),
-        (0, powers1, totals1, sent1, (first1, own1, third1), own1, to_query1),
+    count = logs.shape[0]
+    me = lax.axis_index("batch")
+    for distance, powers, totals, sent, own, out in (
+        (2, powers2, totals2, sent2, scores2, to_query2),
+        (1, powers1, totals1, sent1, scores1, to_query1),
     ):
-        log_total = score_softmax(*[part[...] for part in parts])
+        column = (distance - 1) * rows
+        log_total = all_logs(logs, lax.rem(me + (count - distance), count))
         dscore = loss_scale * jnp.exp(own[...] - log_total)
         coefficient = outer_scale * dscore * sent_keep(sent, rows) / totals[...]
         fill_grad_sim(passages, coefficient, powers, grad_sim, column)
@@ -174,15 +215,14 @@
 
 
 def own_grad_body(
-    queries, passages, positives, hidden, embed, before, powers, totals, sent0, sent1, sent2,
-    own, second, third, other_grad_sim,
+    passages, wanted, hidden, embed, before, powers, totals, sent0, sent1, sent2,
+    own, logs, other_grad_sim,
     losses, to_query, pre_grad, partial, grad_sim,
 ):
     rows = powers.shape[1]
     scores = own[...]
-    log_total = score_softmax(scores, second[...], third[...])
-    wanted = spread(positives, queries, rows // queries)
-    onehot = lax.broadcasted_iota(jnp.int32, scores.shape, 0) == wanted
+    log_total = all_logs(logs, lax.axis_index("batch"))
+    onehot = lax.broadcasted_iota(jnp.int32, scores.shape, 0) == wanted[...]
     losses[...] = log_total - jnp.sum(jnp.where(onehot, scores, 0.0), axis=0, keepdims=True)
     dscore = loss_scale * (jnp.exp(scores - log_total) - onehot.astype(jnp.float32))
     coefficient = outer_scale * dscore * sent_keep(sent0, rows) / totals[...]
@@ -204,16 +244,46 @@
     partial[...] = both.T.astype(jnp.bfloat16)
 
 
+def sum_body(scale, copies, pieces, out):
+    total = jnp.sum(pieces[...].astype(jnp.float32), axis=0) * scale
+    total = total.astype(jnp.bfloat16)
+    for copy in range(copies):
+        out[copy] = total
+
+
+def copies_body(pieces, out):
+    for copy in range(out.shape[0]):
+        out[copy] = pieces[...]
+
+
+def sum_call(pieces, scale, copies):
+    return call(
+        functools.partial(sum_body, scale, copies),
+        (jax.ShapeDtypeStruct((copies,) + pieces.shape[1:], jnp.bfloat16),),
+        (vmem,),
+        (pieces,),
+    )[0]
+
+
 def mean_over_devices(partial):
-    axes = ("batch", "mp")
-    devices = lax.axis_size("batch") * lax.axis_size("mp")
+    outer, inner = lax.axis_size("batch"), lax.axis_size("mp")
+    devices = outer * inner
     rows, columns = partial.shape
     share = -(-rows // (devices * 8)) * 8
     padded = jnp.pad(partial, ((0, share * devices - rows), (0, 0)))
-    pieces = padded.reshape(devices, share, columns)
-    pieces = lax.all_to_all(pieces, axes, 0, 0)
-    mean = (jnp.sum(pieces.astype(jnp.float32), axis=0) / devices).astype(jnp.bfloat16)
-    whole = lax.all_to_all(jnp.broadcast_to(mean[None], (devices, share, columns)), axes, 0, 0)
+    pieces = padded.reshape(inner, outer * share, columns)
+    pieces = lax.all_to_all(pieces, "mp", 0, 0)
+    pieces = sum_call(pieces, 1.0, 1).reshape(outer, share, columns)
+    pieces = lax.all_to_all(pieces, "batch", 0, 0)
+    whole = lax.all_to_all(sum_call(pieces, 1.0 / devices, outer), "batch", 0, 0)
+    whole = whole.reshape(outer * share, columns)
+    whole = call(
+        copies_body,
+        (jax.ShapeDtypeStruct((inner,) + whole.shape, jnp.bfloat16),),
+        (vmem,),
+        (whole,),
+    )[0]
+    whole = lax.all_to_all(whole, "mp", 0, 0)
     return whole.reshape(devices * share, columns)[:rows].astype(jnp.float32)
 
 
@@ -227,56 +297,65 @@
     of = jax.ShapeDtypeStruct
     pair = of((ROWS, rows), f32)
     pairs = pltpu.VMEM((ROWS, rows), f32)
-
-    query_before, sent0 = call(
+    count = lax.axis_size("batch")
+
+    taken = (
+        query_lengths, passage_lengths, positives, query_hidden, passage_hidden, projection
+    )
+    taken = tuple(pltpu.with_memory_space_constraint(x, pltpu.HBM) for x in taken)
+    query_before, sent0, valid, wanted, query_rows, passage_rows, weight = call(
         functools.partial(query_embed_body, queries),
-        (of((rows, dim), f32), of((rows + ROWS, dim), bf16)),
-        (smem, vmem, vmem),
-        (query_lengths, query_hidden, projection),
+        (
+            of((rows, dim), f32), of((rows + ROWS, dim), bf16), of((ROWS, rows), jnp.int32),
+            of((1, rows), jnp.int32), of((rows, width), bf16), of((slots, width), bf16),
+            of((width, dim), bf16),
+        ),
+        (hbm,) * 6,
+        taken,
+        scratch=(
+            pltpu.SMEM((queries,), jnp.int32),
+            pltpu.SMEM((passages,), jnp.int32),
+            pltpu.SMEM((queries,), jnp.int32),
+            pltpu.SemaphoreType.DMA((6,)),
+        ),
         flops=2 * rows * width * dim,
     )
     sent1 = shifted(sent0, "batch", 1)
     sent2 = shifted(sent0, "batch", 2)
     passage_before, embed, powers0, totals0, scores0 = call(
-        functools.partial(own_score_body, queries),
+        functools.partial(own_score_body, queries, passages),
         (of((slots, dim), f32), of((slots, dim), bf16), of((slots, rows), f32), pair, pair),
-        (smem, vmem, vmem, vmem),
-        (passage_lengths, passage_hidden, projection, sent0),
+        (vmem,) * 4,
+        (valid, passage_rows, weight, sent0),
         scratch=(pairs,),
         flops=2 * slots * dim * (width + rows),
         trans=slots * rows,
     )
-    first1 = shifted(scores0, "batch", 1)
-    first2 = shifted(scores0, "batch", 2)
-    powers1, powers2, totals1, totals2, scores1, scores2 = call(
-        functools.partial(other_score_body, queries),
-        (of((slots, rows), f32),) * 2 + (pair,) * 4,
-        (smem, vmem, vmem, vmem),
-        (passage_lengths, embed, sent1, sent2),
+    powers1, powers2, totals1, totals2, scores1, scores2, logs = call(
+        functools.partial(other_score_body, queries, passages),
+        (of((slots, rows), f32),) * 2 + (pair,) * 4 + (of((count, 8, rows), f32),),
+        (vmem,) * 5,
+        (valid, embed, sent1, sent2, scores0),
         scratch=(pairs,),
         flops=4 * slots * dim * rows,
         trans=2 * slots * rows,
     )
-    second2 = shifted(scores1, "batch", 1)
-    below = shifted(jnp.concatenate([scores1, scores2], axis=0), "batch", -1)
-    second0, third1 = below[:ROWS], below[ROWS:]
-    third0 = shifted(scores2, "batch", -2)
+    logs = lax.all_to_all(logs, "batch", 0, 0)
     to_query1, to_query2, grad_sim = call(
         functools.partial(other_grad_body, passages),
         (of((dim, rows), bf16),) * 2 + (of((slots, 2 * rows), bf16),),
-        (vmem,) * 13,
-        (embed, powers1, powers2, totals1, totals2, sent1, sent2,
-         first1, scores1, third1, first2, second2, scores2),
+        (vmem,) * 10,
+        (embed, powers1, powers2, totals1, totals2, sent1, sent2, scores1, scores2, logs),
         flops=4 * slots * dim * rows,
     )
     back1 = shifted(to_query1, "batch", -1)
     back2 = shifted(to_query2, "batch", -2)
     losses, to_query0, passage_pre_grad, passage_partial = call(
-        functools.partial(own_grad_body, queries, passages),
+        functools.partial(own_grad_body, passages),
         (of((1, rows), f32), of((dim, rows), f32), of((slots, dim), bf16), of((dim, width), f32)),
-        (smem,) + (vmem,) * 12,
-        (positives, passage_hidden, embed, passage_before, powers0, totals0, sent0, sent1, sent2,
-         scores0, second0, third0, grad_sim),
+        (vmem,) * 12,
+        (wanted, passage_rows, embed, passage_before, powers0, totals0, sent0, sent1, sent2,
+         scores0, logs, grad_sim),
         scratch=(pltpu.VMEM((slots, rows), bf16),),
         flops=8 * slots * dim * rows + 2 * slots * width * dim,
     )
@@ -284,12 +363,12 @@
         query_grad_body,
         (of((rows, dim), bf16), of((width, dim), bf16)),
         (vmem,) * 6,
-        (query_hidden, query_before, to_query0, back1, back2, passage_partial),
+        (query_rows, query_before, to_query0, back1, back2, passage_partial),
         flops=2 * rows * width * dim,
     )
     grad_projection = mean_over_devices(partial)
-    grad_query_hidden = dot32(query_pre_grad, projection, NT).astype(bf16)
-    grad_passage_hidden = dot32(passage_pre_grad, projection, NT).astype(bf16)
+    grad_query_hidden = dot32(query_pre_grad, weight, NT).astype(bf16)
+    grad_passage_hidden = dot32(passage_pre_grad, weight, NT).astype(bf16)
     losses = losses.reshape(queries, rows // queries)[:, 0]
     return (losses, grad_query_hidden, grad_passage_hidden, grad_projection)
 

time: 60.2 us -> 69.5 us (1.15); the launches traced: 59.8 us -> 68.3 us
  blocking collectives: 17.6 us -> 30.1 us
  local copies, waits for them, and re-layouts: 7.64 us -> 1.18 us
  waiting for transfers between devices: 5.64 us -> 8.48 us
  starting transfers between devices: 15.8 us -> 14.7 us
  Pallas kernels: 7.88 us -> 8.74 us
    all_to_all x1 -> x3, blocking collectives: 17.6 us -> 30.1 us  [the longest x1 11.6 us: mean_over_devices(): pieces = lax.all_to_all(pieces, 'mp', 0, 0)]
    ppermute x9 -> x4, starting transfers between devices: 13.5 us -> 4.65 us  [shifted(): return lax.ppermute(block, axis, route)]
    all_to_all x1 -> x2, starting transfers between devices: 2.37 us -> 10 us  [the longest x1 6.66 us: mean_over_devices(): whole = lax.all_to_all(whole, 'mp', 0, 0)]
    unnamed x21 -> x1, local copies, waits for them, and re-layouts: 6.34 us -> 0.59 us
    ppermute x9 -> x4, waiting for transfers between devices: 1.23 us -> 3.24 us  [shifted(): return lax.ppermute(block, axis, route)]
    pallas_call x6 -> x9, Pallas kernels: 7.88 us -> 8.74 us  [call(): pl.pallas_call(body, out_shape=tuple(outs), in_specs=list(in_specs), out_...]
    all_to_all x1 -> x2, waiting for transfers between devices: 4.42 us -> 5.24 us  [the longest x1 3.45 us: mean_over_devices(): whole = lax.all_to_all(whole, 'mp', 0, 0)]
    broadcast_in_dim x1 -> x0, local copies, waits for them, and re-layouts: 0.7 us -> none  [mean_over_devices(): jnp.broadcast_to(mean[None], (devices, share, columns))]
  transfers between devices with their start and end apart: 10 -> 6, of which waited for: 3 -> 6; matrix products, arithmetic and copies ran while one was open for 8% -> 7% of each run, Pallas kernels for 8% -> 5%
where the time goes in v1:
time: 69.5 us; the launch traced here: 68.3 us
  blocking collectives  30.1 us (43%)
  starting transfers between devices  14.7 us (21%)
  Pallas kernels  8.74 us (13%)
  waiting for transfers between devices  8.48 us (12%)
  matrix products  2.96 us (4%)
  other arithmetic  1.45 us (2%)
  local copies, waits for them, and re-layouts  1.18 us (2%)
    all_to_all x1, blocking collectives, mean_over_devices(): pieces = lax.all_to_all(pieces, 'mp', 0, 0)  11.6 us
    all_to_all x1, blocking collectives, mean_over_devices(): pieces = lax.all_to_all(pieces, 'batch', 0, 0)  9.44 us
    all_to_all x1, blocking collectives, per_device(): logs = lax.all_to_all(logs, 'batch', 0, 0)  9.07 us
    pallas_call x9, Pallas kernels, call(): pl.pallas_call(body, out_shape=tuple(outs), in_specs=list(in_specs), out_...  8.74 us
    all_to_all x1, starting transfers between devices, mean_over_devices(): whole = lax.all_to_all(whole, 'mp', 0, 0)  6.66 us
    ppermute x4, starting transfers between devices, shifted(): return lax.ppermute(block, axis, route)  4.65 us
    all_to_all x1, waiting for transfers between devices, mean_over_devices(): whole = lax.all_to_all(whole, 'mp', 0, 0)  3.45 us
    all_to_all x1, starting transfers between devices, mean_over_devices(): lax.all_to_all(sum_call(pieces, 1.0 / devices, outer), 'batch', 0, 0)  3.35 us
  transfers between devices with their start and end apart: 6, of which 6 were waited for; matrix products, arithmetic and copies ran while one was open for 7% of the time, Pallas kernels for 5%

profile of v1, /device:TPU:1, one launch (start us, length us, event | category | flops | bytes accessed | tf_op | source)
XLA Modules:
  0.0 68.3 jit_solution(7680148056599196990)
XLA Ops:
  0.6 1.8 %shard_map.93 = (f32[256,128]{1,0:T(8,128)S(1)}, bf16[272,128]{1,0:T(8,128)(2,1)S(1)}, s32[16,256]{1,0:T(8,128)S(1)}, s32[1,256]{1,0:T(1,128)S(1)}, bf16[256,768...) custom-call(s32[8]{0:T(128)} %query_lengths_in.1, s32[10]{0:T(128)} %passage_lengths_in.1, ...), custom_call_target="tpu_custom_call" | custom-call | flops 50331648 | bytes 5330024 | tf_op jit(solution)/shard_map/pallas_call | solution.py:38
  2.5 2.1 %collective-permute-start = (bf16[272,128]{1,0:T(8,128)(2,1)S(1)}, bf16[272,128]{1,0:T(8,128)(2,1)S(1)}, u32[]{:S(2)}, u32[]{:S(2)}) collective-permute-start(bf16[272,128]{1,0:T(8,128)(2,1)S(1)} %get-tuple-element.36.sent.sent0), channel_id=1, source_target_pairs={{28,0},{0,4},{4,8},{8,12},{12,16},{16,20},{20,24},{24,28},{29,1},{... | collective-permute-start | bytes 208904 | tf_op jit(solution)/shard_map/ppermute | solution.py:28
  4.6 1.3 %collective-permute-start.1 = (bf16[272,128]{1,0:T(8,128)(2,1)S(1)}, bf16[272,128]{1,0:T(8,128)(2,1)S(1)}, u32[]{:S(2)}, u32[]{:S(2)}) collective-permute-start(bf16[272,128]{1,0:T(8,128)(2,1)S(1)} %get-tuple-element.36.sent.sent0), channel_id=1, source_target_pairs={{24,0},{28,4},{0,8},{4,12},{8,16},{12,20},{16,24},{20,28},{25,1},{... | collective-permute-start | bytes 208904 | tf_op jit(solution)/shard_map/ppermute | solution.py:28
  5.9 1.5 %shard_map.94 = (f32[1280,128]{1,0:T(8,128)S(1)}, bf16[1280,128]{1,0:T(8,128)(2,1)S(1)}, f32[1280,256]{1,0:T(8,128)S(1)}, f32[16,256]{1,0:T(8,128)S(1)}, f32[16,256]{1,0:T(8,128)S(1)}) custom-call(s32[16,256]{1,0:T(8,128)S(1)} %get-tuple-element.34.valid, bf16[1280,768]{1,0:T(8,128)(2,1)S(1)} %get-tuple-element.33.hidden, ...), custom_call_target="tpu_custom_call" | custom-call | flops 335544320 | bytes 4575232 | tf_op jit(solution)/shard_map/pallas_call | solution.py:38
  7.4 1.9 %collective-permute-done.sent1 = bf16[272,128]{1,0:T(8,128)(2,1)S(1)} collective-permute-done((bf16[272,128]{1,0:T(8,128)(2,1)S(1)}, bf16[272,128]{1,0:T(8,128)(2,1)S(1)}, u32[]{:S(2)}, u32[]{:S(2)}) %collective-permute-start) | collective-permute-done | bytes 69664 | tf_op jit(solution)/shard_map/ppermute | solution.py:28
  9.3 0.6 collective-permute-done.1.sent2
  9.9 1.3 %shard_map.95 = (f32[1280,256]{1,0:T(8,128)S(1)}, f32[1280,256]{1,0:T(8,128)S(1)}, f32[16,256]{1,0:T(8,128)S(1)}, f32[16,256]{1,0:T(8,128)S(1)}, f32[16,256]{1,0...) custom-call(s32[16,256]{1,0:T(8,128)S(1)} %get-tuple-element.34.valid, ...), custom_call_target="tpu_custom_call" | custom-call | flops 167772160 | bytes 3252224 | tf_op jit(solution)/shard_map/pallas_call | solution.py:38
  11.2 9.1 %all_to_all.25.logs = f32[8,8,256]{2,1,0:T(8,128)S(1)} all-to-all(f32[8,8,256]{2,1,0:T(8,128)S(1)} %get-tuple-element.42), channel_id=1, replica_groups=mesh['batch'=8,'mp'=4] {'batch'}, dimensions={0} | all-to-all | bytes 131072 | tf_op jit(solution)/shard_map/all_to_all | solution.py:343
  20.3 0.5 shard_map.96
  20.7 0.6 collective-permute-start.2
  21.3 0.7 collective-permute-start.3
  22.0 1.7 %shard_map.97 = (f32[1,256]{1,0:T(1,128)S(1)}, f32[128,256]{1,0:T(8,128)S(1)}, bf16[1280,128]{1,0:T(8,128)(2,1)S(1)}, f32[128,768]{1,0:T(8,128)S(1)}) custom-call(s32[1,256]{1,0:T(1,128)S(1)} %get-tuple-element.32.wanted, bf16[1280,768]{1,0:T(8,128)(2,1)S(1)} %get-tuple-element.33.hidden, bf16[1280,128]{1,0:T(8,128)(2,1)S(1)} %get-tuple-element.37.embed, ...), custom_call_target="tpu_custom_call" | custom-call | flops 587202560 | bytes 6731776 | tf_op jit(solution)/shard_map/pallas_call | solution.py:38
  23.7 0.2 collective-permute-done.2.back1
  23.9 0.5 collective-permute-done.3.back2
  24.5 0.5 shard_map.98
  25.0 11.6 %all_to_all.26.pieces = bf16[4,192,128]{2,1,0:T(8,128)(2,1)S(1)} all-to-all(bf16[4,192,128]{2,1,0:T(8,128)(2,1)S(1)} %bitcast.12), channel_id=1, replica_groups=mesh['batch'=8,'mp'=4] {'mp'}, dimensions={0} | all-to-all | bytes 393216 | tf_op jit(solution)/shard_map/all_to_all | solution.py:275
  36.6 9.4 %all_to_all.27.pieces = bf16[8,24,128]{2,1,0:T(8,128)(2,1)S(1)} all-to-all(bf16[8,24,128]{2,1,0:T(8,128)(2,1)S(1)} %bitcast.14), channel_id=1, replica_groups=mesh['batch'=8,'mp'=4] {'batch'}, dimensions={0} | all-to-all | bytes 98304 | tf_op jit(solution)/shard_map/all_to_all | solution.py:277
  46.1 0.6 shard_map.100
  46.7 3.3 %all-to-all-start.3 = ((bf16[8,24,128]{2,1,0:T(8,128)(2,1)}), bf16[8,24,128]{2,1,0:T(8,128)(2,1)S(1)}, u32[]{:S(2)}, u32[]{:S(2)}) async-start(bf16[8,24,128]{2,1,0:T(8,128)(2,1)} %shard_map.100), calls=%async_computation.3 | async-start | bytes 98304 | tf_op jit(solution)/shard_map/all_to_all | solution.py:278
  50.1 2.0 %convolution_convert_fusion = bf16[1280,768]{1,0:T(8,128)(2,1)} fusion(bf16[1280,128]{1,0:T(8,128)(2,1)S(1)} %get-tuple-element.58, bf16[768,128]{1,0:T(8,128)(2,1)S(1)} %get-tuple-element.35.projection), kind=kOutput, calls=%fused_computation | convolution fusion | flops 252641280 | bytes 2490368 | tf_op jit(solution)/shard_map/dot_general | solution.py:32
  52.0 0.5 broadcast.3
  52.5 0.7 reduce.3
  53.2 0.1 reshape.23
  53.3 0.6 copy.11
  53.8 1.8 %all-to-all-done.3 = bf16[8,24,128]{2,1,0:T(8,128)(2,1)S(1)} async-done(((bf16[8,24,128]{2,1,0:T(8,128)(2,1)}), bf16[8,24,128]{2,1,0:T(8,128)(2,1)S(1)}, u32[]{:S(2)}, u32[]{:S(2)}) %all-to-all-start.3) | async-done | bytes 49184 | tf_op jit(solution)/shard_map/all_to_all | solution.py:278
  55.6 0.7 %shard_map.101 = bf16[4,192,128]{2,1,0:T(8,128)(2,1)} custom-call(bf16[192,128]{1,0:T(8,128)(2,1)S(1)} %bitcast.13), custom_call_target="tpu_custom_call" | custom-call | bytes 245760 | tf_op jit(solution)/shard_map/pallas_call | solution.py:38
  56.3 6.7 %all-to-all-start.4 = ((bf16[4,192,128]{2,1,0:T(8,128)(2,1)}), bf16[4,192,128]{2,1,0:T(8,128)(2,1)S(1)}, u32[]{:S(2)}, u32[]{:S(2)}) async-start(bf16[4,192,128]{2,1,0:T(8,128)(2,1)} %shard_map.101), calls=%async_computation.4 | async-start | bytes 393216 | tf_op jit(solution)/shard_map/all_to_all | solution.py:286
  63.0 1.0 %convolution_convert_fusion.1 = bf16[256,768]{1,0:T(8,128)(2,1)} fusion(bf16[256,128]{1,0:T(8,128)(2,1)S(1)} %get-tuple-element.57, bf16[768,128]{1,0:T(8,128)(2,1)S(1)} %get-tuple-element.35.projection), kind=kOutput, calls=%fused_computation.1 | convolution fusion | flops 50528256 | bytes 655360 | tf_op jit(solution)/shard_map/dot_general | solution.py:32
  64.0 3.5 %all-to-all-done.4 = bf16[4,192,128]{2,1,0:T(8,128)(2,1)S(1)} async-done(((bf16[4,192,128]{2,1,0:T(8,128)(2,1)}), bf16[4,192,128]{2,1,0:T(8,128)(2,1)S(1)}, u32[]{:S(2)}, u32[]{:S(2)}) %all-to-all-start.4) | async-done | bytes 196640 | tf_op jit(solution)/shard_map/all_to_all | solution.py:286
  67.5 0.8 %bitcast_convert_fusion = f32[768,128]{1,0:T(8,128)} fusion(bf16[4,192,128]{2,1,0:T(8,128)(2,1)S(1)} %all-to-all-done.4), kind=kLoop, calls=%fused_computation.2 | loop fusion | flops 98304 | bytes 589824 | tf_op jit(solution)/shard_map/convert_element_type | solution.py:287
  (1 shorter events, 0.0 us)
Async XLA Ops:
  2.5 6.8 %collective-permute-start = (bf16[272,128]{1,0:T(8,128)(2,1)S(1)}, bf16[272,128]{1,0:T(8,128)(2,1)S(1)}, u32[]{:S(2)}, u32[]{:S(2)}) collective-permute-start(bf16[272,128]{1,0:T(8,128)(2,1)S(1)} %get-tuple-element.36.sent.sent0), channel_id=1, source_target_pairs={{28,0},{0,4},{4,8},{8,12},{12,16},{16,20},{20,24},{24,28},{29,1},{... | collective-permute-start | bytes 208904 | tf_op jit(solution)/shard_map/ppermute | solution.py:28
  4.6 5.3 %collective-permute-start.1 = (bf16[272,128]{1,0:T(8,128)(2,1)S(1)}, bf16[272,128]{1,0:T(8,128)(2,1)S(1)}, u32[]{:S(2)}, u32[]{:S(2)}) collective-permute-start(bf16[272,128]{1,0:T(8,128)(2,1)S(1)} %get-tuple-element.36.sent.sent0), channel_id=1, source_target_pairs={{24,0},{28,4},{0,8},{4,12},{8,16},{12,20},{16,24},{20,28},{25,1},{... | collective-permute-start | bytes 208904 | tf_op jit(solution)/shard_map/ppermute | solution.py:28
  20.7 3.2 %collective-permute-start.2 = (bf16[128,256]{1,0:T(8,128)(2,1)S(1)}, bf16[128,256]{1,0:T(8,128)(2,1)S(1)}, u32[]{:S(2)}, u32[]{:S(2)}) collective-permute-start(bf16[128,256]{1,0:T(8,128)(2,1)S(1)} %get-tuple-element.54), channel_id=1, source_target_pairs={{4,0},{8,4},{12,8},{16,12},{20,16},{24,20},{28,24},{0,28},{5,1},{9... | collective-permute-start | bytes 196616 | tf_op jit(solution)/shard_map/ppermute | solution.py:28
  21.3 3.1 %collective-permute-start.3 = (bf16[128,256]{1,0:T(8,128)(2,1)S(1)}, bf16[128,256]{1,0:T(8,128)(2,1)S(1)}, u32[]{:S(2)}, u32[]{:S(2)}) collective-permute-start(bf16[128,256]{1,0:T(8,128)(2,1)S(1)} %get-tuple-element.55), channel_id=1, source_target_pairs={{8,0},{12,4},{16,8},{20,12},{24,16},{28,20},{0,24},{4,28},{9,1},{1... | collective-permute-start | bytes 196616 | tf_op jit(solution)/shard_map/ppermute | solution.py:28
  46.7 8.9 %all-to-all-start.3 = ((bf16[8,24,128]{2,1,0:T(8,128)(2,1)}), bf16[8,24,128]{2,1,0:T(8,128)(2,1)S(1)}, u32[]{:S(2)}, u32[]{:S(2)}) async-start(bf16[8,24,128]{2,1,0:T(8,128)(2,1)} %shard_map.100), calls=%async_computation.3 | async-start | bytes 98304 | tf_op jit(solution)/shard_map/all_to_all | solution.py:278
  56.3 11.1 %all-to-all-start.4 = ((bf16[4,192,128]{2,1,0:T(8,128)(2,1)}), bf16[4,192,128]{2,1,0:T(8,128)(2,1)S(1)}, u32[]{:S(2)}, u32[]{:S(2)}) async-start(bf16[4,192,128]{2,1,0:T(8,128)(2,1)} %shard_map.101), calls=%async_computation.4 | async-start | bytes 393216 | tf_op jit(solution)/shard_map/all_to_all | solution.py:286

commit v2 on v1

--- a/solution.py
+++ b/solution.py
@@ -118,6 +118,13 @@
     return jnp.concatenate([tail[i : i + 1, :] for i in range(rows // LANES)], axis=1)
 
 
+def split(values):
+    high = values.astype(jnp.bfloat16)
+    rest = values - high.astype(jnp.float32)
+    middle = rest.astype(jnp.bfloat16)
+    return high, middle, (rest - middle.astype(jnp.float32)).astype(jnp.bfloat16)
+
+
 def score_block(queries, passages, valid, embed, sent, powers, totals, scores, tops):
     rows = sent.shape[0] - ROWS
     tokens = embed.shape[0] // passages
@@ -139,11 +146,7 @@
     group = rows // queries
     same = lax.broadcasted_iota(jnp.int32, (rows, rows), 0) // group
     same = (same == lax.broadcasted_iota(jnp.int32, (rows, rows), 1) // group).astype(jnp.bfloat16)
-    high = best.astype(jnp.bfloat16)
-    rest = best - high.astype(jnp.float32)
-    middle = rest.astype(jnp.bfloat16)
-    low = (rest - middle.astype(jnp.float32)).astype(jnp.bfloat16)
-    total = dot32(high, same) + dot32(middle, same) + dot32(low, same)
+    total = sum(dot32(part, same) for part in split(best))
     c = lax.broadcasted_iota(jnp.int32, total.shape, 0)
     scores[...] = jnp.where(c < passages, outer_scale * total, -jnp.inf)
 
@@ -163,25 +166,17 @@
     return top + jnp.log(jnp.sum(jnp.exp(scores - top), axis=0, keepdims=True))
 
 
-def other_score_body(
-    queries, passages, valid, embed, sent1, sent2, scores0,
-    powers1, powers2, totals1, totals2, scores1, scores2, logs, tops,
-):
-    score_block(queries, passages, valid, embed, sent1, powers1, totals1, scores1, tops)
-    score_block(queries, passages, valid, embed, sent2, powers2, totals2, scores2, tops)
-    row = lax.broadcasted_iota(jnp.int32, logs.shape[1:], 0)
-    mine = jnp.zeros(logs.shape[1:], jnp.float32)
-    for part, scores in enumerate((scores0, scores1, scores2)):
-        mine = jnp.where(row == part, log_sum(scores[...]), mine)
-    for target in range(logs.shape[0]):
-        logs[target] = mine
-
-
-def all_logs(logs, block):
-    count = logs.shape[0]
-    parts = [logs[lax.rem(block + t, count)][t : t + 1, :] for t in range(3)]
+def log_add(parts):
     top = functools.reduce(jnp.maximum, parts)
     return top + jnp.log(sum(jnp.exp(part - top) for part in parts))
+
+
+def stack_rows(shape, rows):
+    index = lax.broadcasted_iota(jnp.int32, shape, 0)
+    tile = jnp.zeros(shape, jnp.float32)
+    for place, row in enumerate(rows):
+        tile = jnp.where(index == place, row, tile)
+    return tile
 
 
 def fill_grad_sim(passages, coefficient, powers, out, column):
@@ -194,53 +189,77 @@
         )
 
 
-def other_grad_body(
-    passages, embed, powers1, powers2, totals1, totals2, sent1, sent2,
-    scores1, scores2, logs, to_query1, to_query2, grad_sim,
+def other_score_body(
+    queries, passages, valid, embed, sent1, sent2, scores0,
+    powers1, powers2, totals1, totals2, scores1, scores2, logs, back1, back2, tops, grad_sim,
 ):
     rows = powers1.shape[1]
+    dim = embed.shape[1]
+    score_block(queries, passages, valid, embed, sent2, powers2, totals2, scores2, tops)
+    score_block(queries, passages, valid, embed, sent1, powers1, totals1, scores1, tops)
+    log0, log1, log2 = [log_sum(scores[...]) for scores in (scores0, scores1, scores2)]
+    logs[...] = stack_rows(logs.shape, (log0, log1, log2))
     turned = embed[...].T
-    count = logs.shape[0]
-    me = lax.axis_index("batch")
-    for distance, powers, totals, sent, own, out in (
-        (2, powers2, totals2, sent2, scores2, to_query2),
-        (1, powers1, totals1, sent1, scores1, to_query1),
+    for log, sent, powers, totals, scores, back, tail in (
+        (log2, sent2, powers2, totals2, scores2, back2, split(log2)),
+        (log1, sent1, powers1, totals1, scores1, back1, split(log1) + split(log2)),
     ):
-        column = (distance - 1) * rows
-        log_total = all_logs(logs, lax.rem(me + (count - distance), count))
-        dscore = loss_scale * jnp.exp(own[...] - log_total)
+        dscore = loss_scale * jnp.exp(scores[...] - log)
         coefficient = outer_scale * dscore * sent_keep(sent, rows) / totals[...]
-        fill_grad_sim(passages, coefficient, powers, grad_sim, column)
-        out[...] = dot32(turned, grad_sim[:, column : column + rows]).astype(jnp.bfloat16)
-
-
-def own_grad_body(
-    passages, wanted, hidden, embed, before, powers, totals, sent0, sent1, sent2,
-    own, logs, other_grad_sim,
-    losses, to_query, pre_grad, partial, grad_sim,
+        fill_grad_sim(passages, coefficient, powers, grad_sim, 0)
+        back[:dim, :] = dot32(turned, grad_sim[...]).astype(jnp.bfloat16)
+        tail = stack_rows((ROWS, rows), [part.astype(jnp.float32) for part in tail])
+        back[dim:, :] = tail.astype(jnp.bfloat16)
+
+
+def joined(back, dim, place):
+    tail = back[dim:, :].astype(jnp.float32)
+    high, middle, low = [tail[i : i + 1, :] for i in range(place, place + 3)]
+    return high + (middle + low)
+
+
+def grad_body(
+    queries, passages, wanted, query_hidden, passage_hidden, embed, query_before, passage_before,
+    powers0, powers1, powers2, totals0, totals1, totals2, scores0, scores1, scores2,
+    sent0, sent1, sent2, logs, logs1, logs2, back1, back2,
+    losses, query_pre_grad, passage_pre_grad, partial, grad_sim,
 ):
-    rows = powers.shape[1]
-    scores = own[...]
-    log_total = all_logs(logs, lax.axis_index("batch"))
+    rows = powers0.shape[1]
+    dim = embed.shape[1]
+    second, third = joined(back1, dim, 0), joined(back2, dim, 0)
+    total0 = log_add((logs[0:1, :], second, third))
+    total1 = log_add((logs1[0:1, :], logs[1:2, :], joined(back1, dim, 3)))
+    total2 = log_add((logs2[0:1, :], logs1[1:2, :], logs[2:3, :]))
+    scores = scores0[...]
     onehot = lax.broadcasted_iota(jnp.int32, scores.shape, 0) == wanted[...]
-    losses[...] = log_total - jnp.sum(jnp.where(onehot, scores, 0.0), axis=0, keepdims=True)
-    dscore = loss_scale * (jnp.exp(scores - log_total) - onehot.astype(jnp.float32))
-    coefficient = outer_scale * dscore * sent_keep(sent0, rows) / totals[...]
-    fill_grad_sim(passages, coefficient, powers, grad_sim, 0)
-    to_query[...] = dot32(embed[...].T, grad_sim[...])
-    grad = dot32(grad_sim[...], sent0[:rows, :])
-    grad += dot32(other_grad_sim[:, :rows], sent1[:rows, :])
-    grad += dot32(other_grad_sim[:, rows:], sent2[:rows, :])
-    pre = back_rows(grad, before[...])
-    pre_grad[...] = pre
-    partial[...] = dot32(pre.T, hidden[...])
-
-
-def query_grad_body(hidden, before, own, back1, back2, passage_partial, pre_grad, partial):
-    total = own[...] + back1[...].astype(jnp.float32) + back2[...].astype(jnp.float32)
-    pre = back_rows(total.T, before[...])
-    pre_grad[...] = pre
-    both = passage_partial[...] + dot32(pre.T, hidden[...])
+    loss = total0 - jnp.sum(jnp.where(onehot, scores, 0.0), axis=0, keepdims=True)
+    pick = lax.broadcasted_iota(jnp.int32, (rows, LANES), 1) * (rows // queries)
+    pick = (pick == lax.broadcasted_iota(jnp.int32, (rows, LANES), 0)).astype(jnp.bfloat16)
+    losses[...] = sum(dot32(part, pick) for part in split(loss))[:, :queries]
+
+    for block, (total, sent, powers, totals, scores) in enumerate((
+        (total0, sent0, powers0, totals0, scores0),
+        (total1, sent1, powers1, totals1, scores1),
+        (total2, sent2, powers2, totals2, scores2),
+    )):
+        dscore = jnp.exp(scores[...] - total)
+        if block == 0:
+            dscore = dscore - onehot.astype(jnp.float32)
+        coefficient = (outer_scale * loss_scale) * dscore * sent_keep(sent, rows) / totals[...]
+        fill_grad_sim(passages, coefficient, powers, grad_sim, block * rows)
+
+    to_query = dot32(embed[...].T, grad_sim[:, :rows])
+    to_query += back1[:dim, :].astype(jnp.float32) * jnp.exp(second - total0)
+    to_query += back2[:dim, :].astype(jnp.float32) * jnp.exp(third - total0)
+    pre = back_rows(to_query.T, query_before[...])
+    query_pre_grad[...] = pre
+    both = dot32(pre.T, query_hidden[...])
+    grad = dot32(grad_sim[:, :rows], sent0[:rows, :])
+    grad += dot32(grad_sim[:, rows : 2 * rows], sent1[:rows, :])
+    grad += dot32(grad_sim[:, 2 * rows :], sent2[:rows, :])
+    pre = back_rows(grad, passage_before[...])
+    passage_pre_grad[...] = pre
+    both += dot32(pre.T, passage_hidden[...])
     partial[...] = both.T.astype(jnp.bfloat16)
 
 
@@ -251,39 +270,20 @@
         out[copy] = total
 
 
-def copies_body(pieces, out):
-    for copy in range(out.shape[0]):
-        out[copy] = pieces[...]
-
-
-def sum_call(pieces, scale, copies):
-    return call(
-        functools.partial(sum_body, scale, copies),
-        (jax.ShapeDtypeStruct((copies,) + pieces.shape[1:], jnp.bfloat16),),
+def mean_over_devices(partial):
+    axes = ("batch", "mp")
+    devices = lax.axis_size("batch") * lax.axis_size("mp")
+    rows, columns = partial.shape
+    share = -(-rows // (devices * 8)) * 8
+    padded = jnp.pad(partial, ((0, share * devices - rows), (0, 0)))
+    pieces = lax.all_to_all(padded.reshape(devices, share, columns), axes, 0, 0)
+    means = call(
+        functools.partial(sum_body, 1.0 / devices, devices),
+        (jax.ShapeDtypeStruct(pieces.shape, jnp.bfloat16),),
         (vmem,),
         (pieces,),
     )[0]
-
-
-def mean_over_devices(partial):
-    outer, inner = lax.axis_size("batch"), lax.axis_size("mp")
-    devices = outer * inner
-    rows, columns = partial.shape
-    share = -(-rows // (devices * 8)) * 8
-    padded = jnp.pad(partial, ((0, share * devices - rows), (0, 0)))
-    pieces = padded.reshape(inner, outer * share, columns)
-    pieces = lax.all_to_all(pieces, "mp", 0, 0)
-    pieces = sum_call(pieces, 1.0, 1).reshape(outer, share, columns)
-    pieces = lax.all_to_all(pieces, "batch", 0, 0)
-    whole = lax.all_to_all(sum_call(pieces, 1.0 / devices, outer), "batch", 0, 0)
-    whole = whole.reshape(outer * share, columns)
-    whole = call(
-        copies_body,
-        (jax.ShapeDtypeStruct((inner,) + whole.shape, jnp.bfloat16),),
-        (vmem,),
-        (whole,),
-    )[0]
-    whole = lax.all_to_all(whole, "mp", 0, 0)
+    whole = lax.all_to_all(means, axes, 0, 0)
     return whole.reshape(devices * share, columns)[:rows].astype(jnp.float32)
 
 
@@ -297,7 +297,6 @@
     of = jax.ShapeDtypeStruct
     pair = of((ROWS, rows), f32)
     pairs = pltpu.VMEM((ROWS, rows), f32)
-    count = lax.axis_size("batch")
 
     taken = (
         query_lengths, passage_lengths, positives, query_hidden, passage_hidden, projection
@@ -331,45 +330,37 @@
         flops=2 * slots * dim * (width + rows),
         trans=slots * rows,
     )
-    powers1, powers2, totals1, totals2, scores1, scores2, logs = call(
+    powers1, powers2, totals1, totals2, scores1, scores2, logs, back1, back2 = call(
         functools.partial(other_score_body, queries, passages),
-        (of((slots, rows), f32),) * 2 + (pair,) * 4 + (of((count, 8, rows), f32),),
+        (of((slots, rows), f32),) * 2 + (pair,) * 4
+        + (of((8, rows), f32),) + (of((dim + ROWS, rows), bf16),) * 2,
         (vmem,) * 5,
         (valid, embed, sent1, sent2, scores0),
-        scratch=(pairs,),
-        flops=4 * slots * dim * rows,
+        scratch=(pairs, pltpu.VMEM((slots, rows), bf16)),
+        flops=8 * slots * dim * rows,
         trans=2 * slots * rows,
     )
-    logs = lax.all_to_all(logs, "batch", 0, 0)
-    to_query1, to_query2, grad_sim = call(
-        functools.partial(other_grad_body, passages),
-        (of((dim, rows), bf16),) * 2 + (of((slots, 2 * rows), bf16),),
-        (vmem,) * 10,
-        (embed, powers1, powers2, totals1, totals2, sent1, sent2, scores1, scores2, logs),
-        flops=4 * slots * dim * rows,
-    )
-    back1 = shifted(to_query1, "batch", -1)
-    back2 = shifted(to_query2, "batch", -2)
-    losses, to_query0, passage_pre_grad, passage_partial = call(
-        functools.partial(own_grad_body, passages),
-        (of((1, rows), f32), of((dim, rows), f32), of((slots, dim), bf16), of((dim, width), f32)),
-        (vmem,) * 12,
-        (wanted, passage_rows, embed, passage_before, powers0, totals0, sent0, sent1, sent2,
-         scores0, logs, grad_sim),
-        scratch=(pltpu.VMEM((slots, rows), bf16),),
-        flops=8 * slots * dim * rows + 2 * slots * width * dim,
-    )
-    query_pre_grad, partial = call(
-        query_grad_body,
-        (of((rows, dim), bf16), of((width, dim), bf16)),
-        (vmem,) * 6,
-        (query_rows, query_before, to_query0, back1, back2, passage_partial),
-        flops=2 * rows * width * dim,
+    back2 = shifted(back2, "batch", -2)
+    back1 = shifted(back1, "batch", -1)
+    logs1 = shifted(logs, "batch", 1)
+    logs2 = shifted(logs, "batch", 2)
+    losses, query_pre_grad, passage_pre_grad, partial = call(
+        functools.partial(grad_body, queries, passages),
+        (
+            of((1, queries), f32), of((rows, dim), bf16), of((slots, dim), bf16),
+            of((width, dim), bf16),
+        ),
+        (vmem,) * 23,
+        (wanted, query_rows, passage_rows, embed, query_before, passage_before,
+         powers0, powers1, powers2, totals0, totals1, totals2, scores0, scores1, scores2,
+         sent0, sent1, sent2, logs, logs1, logs2, back1, back2),
+        scratch=(pltpu.VMEM((slots, 3 * rows), bf16),),
+        flops=8 * slots * dim * rows + 2 * (slots + rows) * width * dim,
     )
     grad_projection = mean_over_devices(partial)
     grad_query_hidden = dot32(query_pre_grad, weight, NT).astype(bf16)
     grad_passage_hidden = dot32(passage_pre_grad, weight, NT).astype(bf16)
-    losses = losses.reshape(queries, rows // queries)[:, 0]
+    losses = losses.reshape(queries)
     return (losses, grad_query_hidden, grad_passage_hidden, grad_projection)
 
 

time: 69.5 us -> 50.8 us (0.73); the launches traced: 68.3 us -> 50.6 us
  blocking collectives: 30.1 us -> 15.4 us
  starting transfers between devices: 14.7 us -> 8.74 us
  waiting for transfers between devices: 8.48 us -> 13.9 us
  local copies, waits for them, and re-layouts: 1.18 us -> 0 us
    all_to_all x3 -> x1, blocking collectives: 30.1 us -> 15.4 us  [mean_over_devices(): pieces = lax.all_to_all(padded.reshape(devices, share, columns), axes, 0, 0)]
    all_to_all x2 -> x1, starting transfers between devices: 10 us -> 2.37 us  [mean_over_devices(): whole = lax.all_to_all(means, axes, 0, 0)]
    ppermute x4 -> x6, waiting for transfers between devices: 3.24 us -> 7.6 us  [shifted(): return lax.ppermute(block, axis, route)]
    ppermute x4 -> x6, starting transfers between devices: 4.65 us -> 6.37 us  [shifted(): return lax.ppermute(block, axis, route)]
    all_to_all x2 -> x1, waiting for transfers between devices: 5.24 us -> 6.28 us  [mean_over_devices(): whole = lax.all_to_all(means, axes, 0, 0)]
    pallas_call x9 -> x5, Pallas kernels: 8.74 us -> 8.11 us  [call(): pl.pallas_call(body, out_shape=tuple(outs), in_specs=list(in_specs), out_...]
  transfers between devices with their start and end apart: 6 -> 7, of which waited for: 6 -> 5; matrix products, arithmetic and copies ran while one was open for 7% -> 6% of each run, Pallas kernels for 5% -> 3%
where the time goes in v2:
time: 50.8 us; the launch traced here: 50.6 us
  blocking collectives  15.4 us (30%)
  waiting for transfers between devices  13.9 us (27%)
  starting transfers between devices  8.74 us (17%)
  Pallas kernels  8.11 us (16%)
  matrix products  2.95 us (6%)
  other arithmetic  0.78 us (2%)
  between operations  0.67 us (1%)
    all_to_all x1, blocking collectives, mean_over_devices(): pieces = lax.all_to_all(padded.reshape(devices, share, columns), axes, 0, 0)  15.4 us
    pallas_call x5, Pallas kernels, call(): pl.pallas_call(body, out_shape=tuple(outs), in_specs=list(in_specs), out_...  8.11 us
    ppermute x6, waiting for transfers between devices, shifted(): return lax.ppermute(block, axis, route)  7.6 us
    ppermute x6, starting transfers between devices, shifted(): return lax.ppermute(block, axis, route)  6.37 us
    all_to_all x1, waiting for transfers between devices, mean_over_devices(): whole = lax.all_to_all(means, axes, 0, 0)  6.28 us
    dot_general x2, matrix products, dot32(): lax.dot_general(left, right, dims, preferred_element_type=jnp.float32)  2.95 us
    all_to_all x1, starting transfers between devices, mean_over_devices(): whole = lax.all_to_all(means, axes, 0, 0)  2.37 us
  transfers between devices with their start and end apart: 7, of which 5 were waited for; matrix products, arithmetic and copies ran while one was open for 6% of the time, Pallas kernels for 3%

profile of v2, /device:TPU:1, one launch (start us, length us, event | category | flops | bytes accessed | tf_op | source)
XLA Modules:
  0.0 50.6 jit_solution(16122439031966926792)
XLA Ops:
  0.6 1.8 %shard_map.93 = (f32[256,128]{1,0:T(8,128)S(1)}, bf16[272,128]{1,0:T(8,128)(2,1)S(1)}, s32[16,256]{1,0:T(8,128)S(1)}, s32[1,256]{1,0:T(1,128)S(1)}, bf16[256,768...) custom-call(s32[8]{0:T(128)} %query_lengths_in.1, s32[10]{0:T(128)} %passage_lengths_in.1, ...), custom_call_target="tpu_custom_call" | custom-call | flops 50331648 | bytes 5330024 | tf_op jit(solution)/shard_map/pallas_call | solution.py:38
  2.5 2.2 %collective-permute-start.1 = (bf16[272,128]{1,0:T(8,128)(2,1)S(1)}, bf16[272,128]{1,0:T(8,128)(2,1)S(1)}, u32[]{:S(2)}, u32[]{:S(2)}) collective-permute-start(bf16[272,128]{1,0:T(8,128)(2,1)S(1)} %get-tuple-element.34.sent.sent0), channel_id=1, source_target_pairs={{24,0},{28,4},{0,8},{4,12},{8,16},{12,20},{16,24},{20,28},{25,1},{... | collective-permute-start | bytes 208904 | tf_op jit(solution)/shard_map/ppermute | solution.py:28
  4.7 1.2 %collective-permute-start = (bf16[272,128]{1,0:T(8,128)(2,1)S(1)}, bf16[272,128]{1,0:T(8,128)(2,1)S(1)}, u32[]{:S(2)}, u32[]{:S(2)}) collective-permute-start(bf16[272,128]{1,0:T(8,128)(2,1)S(1)} %get-tuple-element.34.sent.sent0), channel_id=1, source_target_pairs={{28,0},{0,4},{4,8},{8,12},{12,16},{16,20},{20,24},{24,28},{29,1},{... | collective-permute-start | bytes 208904 | tf_op jit(solution)/shard_map/ppermute | solution.py:28
  5.9 1.5 %shard_map.94 = (f32[1280,128]{1,0:T(8,128)S(1)}, bf16[1280,128]{1,0:T(8,128)(2,1)S(1)}, f32[1280,256]{1,0:T(8,128)S(1)}, f32[16,256]{1,0:T(8,128)S(1)}, f32[16,256]{1,0:T(8,128)S(1)}) custom-call(s32[16,256]{1,0:T(8,128)S(1)} %get-tuple-element.32.valid, bf16[1280,768]{1,0:T(8,128)(2,1)S(1)} %get-tuple-element.31.hidden.passage_hidden, ...), custom_call_target="tpu_custom_call" | custom-call | flops 335544320 | bytes 4575232 | tf_op jit(solution)/shard_map/pallas_call | solution.py:38
  7.4 1.0 %collective-permute-done.1.sent2 = bf16[272,128]{1,0:T(8,128)(2,1)S(1)} collective-permute-done((bf16[272,128]{1,0:T(8,128)(2,1)S(1)}, bf16[272,128]{1,0:T(8,128)(2,1)S(1)}, u32[]{:S(2)}, u32[]{:S(2)}) %collective-permute-start.1) | collective-permute-done | bytes 69664 | tf_op jit(solution)/shard_map/ppermute | solution.py:28
  8.4 2.7 %collective-permute-done.sent1 = bf16[272,128]{1,0:T(8,128)(2,1)S(1)} collective-permute-done((bf16[272,128]{1,0:T(8,128)(2,1)S(1)}, bf16[272,128]{1,0:T(8,128)(2,1)S(1)}, u32[]{:S(2)}, u32[]{:S(2)}) %collective-permute-start) | collective-permute-done | bytes 69664 | tf_op jit(solution)/shard_map/ppermute | solution.py:28
  11.1 1.8 %shard_map.95 = (f32[1280,256]{1,0:T(8,128)S(1)}, f32[1280,256]{1,0:T(8,128)S(1)}, f32[16,256]{1,0:T(8,128)S(1)}, f32[16,256]{1,0:T(8,128)S(1)}, f32[16,256]{1,0...) custom-call(s32[16,256]{1,0:T(8,128)S(1)} %get-tuple-element.32.vali, ...), custom_call_target="tpu_custom_call" | custom-call | flops 335544320 | bytes 3342336 | tf_op jit(solution)/shard_map/pallas_call | solution.py:38
  12.9 0.1 collective-permute-start.4
  13.0 1.4 %collective-permute-start.5 = (bf16[144,256]{1,0:T(8,128)(2,1)S(1)}, bf16[144,256]{1,0:T(8,128)(2,1)S(1)}, u32[]{:S(2)}, u32[]{:S(2)}) collective-permute-start(bf16[144,256]{1,0:T(8,128)(2,1)S(1)} %get-tuple-element.49), channel_id=1, source_target_pairs={{8,0},{12,4},{16,8},{20,12},{24,16},{28,20},{0,24},{4,28},{9,1},{1... | collective-permute-start | bytes 221192 | tf_op jit(solution)/shard_map/ppermute | solution.py:28
  14.4 0.1 collective-permute-start.3
  14.5 1.4 %collective-permute-start.2 = (f32[8,256]{1,0:T(8,128)S(1)}, f32[8,256]{1,0:T(8,128)S(1)}, u32[]{:S(2)}, u32[]{:S(2)}) collective-permute-start(f32[8,256]{1,0:T(8,128)S(1)} %get-tuple-element.47.logs), channel_id=1, source_target_pairs={{28,0},{0,4},{4,8},{8,12},{12,16},{16,20},{20,24},{24,28},{29,1},{... | collective-permute-start | bytes 24584 | tf_op jit(solution)/shard_map/ppermute | solution.py:28
  15.9 2.9 %collective-permute-done.3.logs2 = f32[8,256]{1,0:T(8,128)S(1)} collective-permute-done((f32[8,256]{1,0:T(8,128)S(1)}, f32[8,256]{1,0:T(8,128)S(1)}, u32[]{:S(2)}, u32[]{:S(2)}) %collective-permute-start.3) | collective-permute-done | bytes 8224 | tf_op jit(solution)/shard_map/ppermute | solution.py:28
  18.8 1.0 %collective-permute-done.2.logs1 = f32[8,256]{1,0:T(8,128)S(1)} collective-permute-done((f32[8,256]{1,0:T(8,128)S(1)}, f32[8,256]{1,0:T(8,128)S(1)}, u32[]{:S(2)}, u32[]{:S(2)}) %collective-permute-start.2) | collective-permute-done | bytes 8224 | tf_op jit(solution)/shard_map/ppermute | solution.py:28
  19.8 0.0 collective-permute-done.4.back1
  19.8 0.0 collective-permute-done.5.back2
  19.8 2.3 %shard_map.96 = (f32[1,8]{1,0:T(1,128)}, bf16[256,128]{1,0:T(8,128)(2,1)S(1)}, bf16[1280,128]{1,0:T(8,128)(2,1)S(1)}, bf16[768,128]{1,0:T(8,128)(2,1)S(1)}) custom-call(s32[1,256]{1,0:T(1,128)S(1)} %get-tuple-element.29.wanted, bf16[256,768]{1,0:T(8,128)(2,1)S(1)} %get-tuple-element.30.query_hidden, ...), custom_call_target="tpu_custom_call" | custom-call | flops 637534208 | bytes 8475680 | tf_op jit(solution)/shard_map/pallas_call | solution.py:38
  22.0 15.4 %all_to_all.10.pieces = bf16[32,24,128]{2,1,0:T(8,128)(2,1)S(1)} all-to-all(bf16[32,24,128]{2,1,0:T(8,128)(2,1)S(1)} %bitcast.9), channel_id=1, replica_groups=mesh['batch'=8,'mp'=4] {'batch','mp'}, dimensions={0} | all-to-all | bytes 393216 | tf_op jit(solution)/shard_map/all_to_all | solution.py:279
  37.5 0.7 %shard_map.97 = bf16[32,24,128]{2,1,0:T(8,128)(2,1)} custom-call(bf16[32,24,128]{2,1,0:T(8,128)(2,1)S(1)} %all_to_all.10.pieces), custom_call_target="tpu_custom_call" | custom-call | bytes 393216 | tf_op jit(solution)/shard_map/pallas_call | solution.py:38
  38.2 2.4 %all-to-all-start.1 = ((bf16[32,24,128]{2,1,0:T(8,128)(2,1)}), bf16[32,24,128]{2,1,0:T(8,128)(2,1)S(1)}, u32[]{:S(2)}, u32[]{:S(2)}) async-start(bf16[32,24,128]{2,1,0:T(8,128)(2,1)} %shard_map.97), calls=%async_computation.1 | async-start | bytes 393216 | tf_op jit(solution)/shard_map/all_to_all | solution.py:286
  40.6 1.0 %convolution_convert_fusion.1 = bf16[256,768]{1,0:T(8,128)(2,1)} fusion(bf16[256,128]{1,0:T(8,128)(2,1)S(1)} %get-tuple-element.51, bf16[768,128]{1,0:T(8,128)(2,1)S(1)} %get-tuple-element.33.projection), kind=kOutput, calls=%fused_computation.1 | convolution fusion | flops 50528256 | bytes 655360 | tf_op jit(solution)/shard_map/dot_general | solution.py:32
  41.6 1.9 %convolution_convert_fusion = bf16[1280,768]{1,0:T(8,128)(2,1)} fusion(bf16[1280,128]{1,0:T(8,128)(2,1)S(1)} %get-tuple-element.52, bf16[768,128]{1,0:T(8,128)(2,1)S(1)} %get-tuple-element.33.projection), kind=kOutput, calls=%fused_computation | convolution fusion | flops 252641280 | bytes 2490368 | tf_op jit(solution)/shard_map/dot_general | solution.py:32
  43.5 6.3 %all-to-all-done.1 = bf16[32,24,128]{2,1,0:T(8,128)(2,1)S(1)} async-done(((bf16[32,24,128]{2,1,0:T(8,128)(2,1)}), bf16[32,24,128]{2,1,0:T(8,128)(2,1)S(1)}, u32[]{:S(2)}, u32[]{:S(2)}) %all-to-all-start.1) | async-done | bytes 196640 | tf_op jit(solution)/shard_map/all_to_all | solution.py:286
  49.8 0.8 %bitcast_convert_fusion = f32[768,128]{1,0:T(8,128)} fusion(bf16[32,24,128]{2,1,0:T(8,128)(2,1)S(1)} %all-to-all-done.1), kind=kLoop, calls=%fused_computation.2 | loop fusion | flops 98304 | bytes 589824 | tf_op jit(solution)/shard_map/convert_element_type | solution.py:287
Async XLA Ops:
  2.5 5.9 %collective-permute-start.1 = (bf16[272,128]{1,0:T(8,128)(2,1)S(1)}, bf16[272,128]{1,0:T(8,128)(2,1)S(1)}, u32[]{:S(2)}, u32[]{:S(2)}) collective-permute-start(bf16[272,128]{1,0:T(8,128)(2,1)S(1)} %get-tuple-element.34.sent.sent0), channel_id=1, source_target_pairs={{24,0},{28,4},{0,8},{4,12},{8,16},{12,20},{16,24},{20,28},{25,1},{... | collective-permute-start | bytes 208904 | tf_op jit(solution)/shard_map/ppermute | solution.py:28
  4.7 6.5 %collective-permute-start = (bf16[272,128]{1,0:T(8,128)(2,1)S(1)}, bf16[272,128]{1,0:T(8,128)(2,1)S(1)}, u32[]{:S(2)}, u32[]{:S(2)}) collective-permute-start(bf16[272,128]{1,0:T(8,128)(2,1)S(1)} %get-tuple-element.34.sent.sent0), channel_id=1, source_target_pairs={{28,0},{0,4},{4,8},{8,12},{12,16},{16,20},{20,24},{24,28},{29,1},{... | collective-permute-start | bytes 208904 | tf_op jit(solution)/shard_map/ppermute | solution.py:28
  12.9 6.8 %collective-permute-start.4 = (bf16[144,256]{1,0:T(8,128)(2,1)S(1)}, bf16[144,256]{1,0:T(8,128)(2,1)S(1)}, u32[]{:S(2)}, u32[]{:S(2)}) collective-permute-start(bf16[144,256]{1,0:T(8,128)(2,1)S(1)} %get-tuple-element.48), channel_id=1, source_target_pairs={{4,0},{8,4},{12,8},{16,12},{20,16},{24,20},{28,24},{0,28},{5,1},{9... | collective-permute-start | bytes 221192 | tf_op jit(solution)/shard_map/ppermute | solution.py:28
  13.0 6.8 %collective-permute-start.5 = (bf16[144,256]{1,0:T(8,128)(2,1)S(1)}, bf16[144,256]{1,0:T(8,128)(2,1)S(1)}, u32[]{:S(2)}, u32[]{:S(2)}) collective-permute-start(bf16[144,256]{1,0:T(8,128)(2,1)S(1)} %get-tuple-element.49), channel_id=1, source_target_pairs={{8,0},{12,4},{16,8},{20,12},{24,16},{28,20},{0,24},{4,28},{9,1},{1... | collective-permute-start | bytes 221192 | tf_op jit(solution)/shard_map/ppermute | solution.py:28
  14.4 4.4 %collective-permute-start.3 = (f32[8,256]{1,0:T(8,128)S(1)}, f32[8,256]{1,0:T(8,128)S(1)}, u32[]{:S(2)}, u32[]{:S(2)}) collective-permute-start(f32[8,256]{1,0:T(8,128)S(1)} %get-tuple-element.47.logs), channel_id=1, source_target_pairs={{24,0},{28,4},{0,8},{4,12},{8,16},{12,20},{16,24},{20,28},{25,1},{... | collective-permute-start | bytes 24584 | tf_op jit(solution)/shard_map/ppermute | solution.py:28
  14.5 5.3 %collective-permute-start.2 = (f32[8,256]{1,0:T(8,128)S(1)}, f32[8,256]{1,0:T(8,128)S(1)}, u32[]{:S(2)}, u32[]{:S(2)}) collective-permute-start(f32[8,256]{1,0:T(8,128)S(1)} %get-tuple-element.47.logs), channel_id=1, source_target_pairs={{28,0},{0,4},{4,8},{8,12},{12,16},{16,20},{20,24},{24,28},{29,1},{... | collective-permute-start | bytes 24584 | tf_op jit(solution)/shard_map/ppermute | solution.py:28
  38.2 11.6 %all-to-all-start.1 = ((bf16[32,24,128]{2,1,0:T(8,128)(2,1)}), bf16[32,24,128]{2,1,0:T(8,128)(2,1)S(1)}, u32[]{:S(2)}, u32[]{:S(2)}) async-start(bf16[32,24,128]{2,1,0:T(8,128)(2,1)} %shard_map.97), calls=%async_computation.1 | async-start | bytes 393216 | tf_op jit(solution)/shard_map/all_to_all | solution.py:286

commit v3 on v2

--- a/solution.py
+++ b/solution.py
@@ -218,11 +218,79 @@
     return high + (middle + low)
 
 
+def half_at(bit, size, other):
+    side = lax.rem(lax.axis_index("mp") // bit, 2)
+    side = 1 - side if other else side
+    return pl.ds(pl.multiple_of(side * size, size), size)
+
+
+def share_halves(bit, whole, kept, sent):
+    size = kept.shape[0]
+    kept[...] = whole[half_at(bit, size, False), :]
+    sent[...] = whole[half_at(bit, size, True), :].astype(sent.dtype)
+
+
+def halve_body(bit, kept, taken, next_kept, next_sent, total):
+    total[...] = kept[...] + taken[...].astype(jnp.float32)
+    share_halves(bit, total, next_kept, next_sent)
+
+
+def last_half_body(scale, kept, taken, out):
+    out[...] = ((kept[...] + taken[...].astype(jnp.float32)) * scale).astype(out.dtype)
+
+
+def join_body(bit, mine, taken, out):
+    size = mine.shape[0]
+    out[half_at(bit, size, False), :] = mine[...].astype(out.dtype)
+    out[half_at(bit, size, True), :] = taken[...].astype(out.dtype)
+
+
+def swapped(block, bit):
+    return lax.ppermute(block, "mp", [(i, i ^ bit) for i in range(lax.axis_size("mp"))])
+
+
+def mean_over_devices(kept, sent):
+    of = jax.ShapeDtypeStruct
+    inner = lax.axis_size("mp")
+    scale = 1.0 / (lax.axis_size("batch") * inner)
+    bit = 1
+    while True:
+        taken = swapped(sent, bit)
+        size, columns = kept.shape
+        if 2 * bit == inner:
+            break
+        bit *= 2
+        kept, sent = call(
+            functools.partial(halve_body, bit),
+            (of((size // 2, columns), jnp.float32), of((size // 2, columns), jnp.bfloat16)),
+            (vmem,) * 2,
+            (kept, taken),
+            scratch=(pltpu.VMEM((size, columns), jnp.float32),),
+        )
+    share = call(
+        functools.partial(last_half_body, scale),
+        (of((size, columns), jnp.bfloat16),),
+        (vmem,) * 2,
+        (kept, taken),
+    )[0]
+    share = lax.psum(share, "batch")
+    while bit:
+        dtype = jnp.float32 if bit == 1 else jnp.bfloat16
+        share = call(
+            functools.partial(join_body, bit),
+            (of((2 * share.shape[0], columns), dtype),),
+            (vmem,) * 2,
+            (share, swapped(share, bit)),
+        )[0]
+        bit //= 2
+    return share
+
+
 def grad_body(
     queries, passages, wanted, query_hidden, passage_hidden, embed, query_before, passage_before,
     powers0, powers1, powers2, totals0, totals1, totals2, scores0, scores1, scores2,
     sent0, sent1, sent2, logs, logs1, logs2, back1, back2,
-    losses, query_pre_grad, passage_pre_grad, partial, grad_sim,
+    losses, query_pre_grad, passage_pre_grad, kept, sent, grad_sim, partial,
 ):
     rows = powers0.shape[1]
     dim = embed.shape[1]
@@ -237,7 +305,7 @@
     pick = (pick == lax.broadcasted_iota(jnp.int32, (rows, LANES), 0)).astype(jnp.bfloat16)
     losses[...] = sum(dot32(part, pick) for part in split(loss))[:, :queries]
 
-    for block, (total, sent, powers, totals, scores) in enumerate((
+    for block, (total, query, powers, totals, scores) in enumerate((
         (total0, sent0, powers0, totals0, scores0),
         (total1, sent1, powers1, totals1, scores1),
         (total2, sent2, powers2, totals2, scores2),
@@ -245,7 +313,7 @@
         dscore = jnp.exp(scores[...] - total)
         if block == 0:
             dscore = dscore - onehot.astype(jnp.float32)
-        coefficient = (outer_scale * loss_scale) * dscore * sent_keep(sent, rows) / totals[...]
+        coefficient = (outer_scale * loss_scale) * dscore * sent_keep(query, rows) / totals[...]
         fill_grad_sim(passages, coefficient, powers, grad_sim, block * rows)
 
     to_query = dot32(embed[...].T, grad_sim[:, :rows])
@@ -260,31 +328,8 @@
     pre = back_rows(grad, passage_before[...])
     passage_pre_grad[...] = pre
     both += dot32(pre.T, passage_hidden[...])
-    partial[...] = both.T.astype(jnp.bfloat16)
-
-
-def sum_body(scale, copies, pieces, out):
-    total = jnp.sum(pieces[...].astype(jnp.float32), axis=0) * scale
-    total = total.astype(jnp.bfloat16)
-    for copy in range(copies):
-        out[copy] = total
-
-
-def mean_over_devices(partial):
-    axes = ("batch", "mp")
-    devices = lax.axis_size("batch") * lax.axis_size("mp")
-    rows, columns = partial.shape
-    share = -(-rows // (devices * 8)) * 8
-    padded = jnp.pad(partial, ((0, share * devices - rows), (0, 0)))
-    pieces = lax.all_to_all(padded.reshape(devices, share, columns), axes, 0, 0)
-    means = call(
-        functools.partial(sum_body, 1.0 / devices, devices),
-        (jax.ShapeDtypeStruct(pieces.shape, jnp.bfloat16),),
-        (vmem,),
-        (pieces,),
-    )[0]
-    whole = lax.all_to_all(means, axes, 0, 0)
-    return whole.reshape(devices * share, columns)[:rows].astype(jnp.float32)
+    partial[...] = both.T
+    share_halves(1, partial, kept, sent)
 
 
 def per_device(query_hidden, passage_hidden, projection, query_lengths, passage_lengths, positives):
@@ -344,20 +389,20 @@
     back1 = shifted(back1, "batch", -1)
     logs1 = shifted(logs, "batch", 1)
     logs2 = shifted(logs, "batch", 2)
-    losses, query_pre_grad, passage_pre_grad, partial = call(
+    losses, query_pre_grad, passage_pre_grad, kept, sent = call(
         functools.partial(grad_body, queries, passages),
         (
             of((1, queries), f32), of((rows, dim), bf16), of((slots, dim), bf16),
-            of((width, dim), bf16),
+            of((width // 2, dim), f32), of((width // 2, dim), bf16),
         ),
         (vmem,) * 23,
         (wanted, query_rows, passage_rows, embed, query_before, passage_before,
          powers0, powers1, powers2, totals0, totals1, totals2, scores0, scores1, scores2,
          sent0, sent1, sent2, logs, logs1, logs2, back1, back2),
-        scratch=(pltpu.VMEM((slots, 3 * rows), bf16),),
+        scratch=(pltpu.VMEM((slots, 3 * rows), bf16), pltpu.VMEM((width, dim), f32)),
         flops=8 * slots * dim * rows + 2 * (slots + rows) * width * dim,
     )
-    grad_projection = mean_over_devices(partial)
+    grad_projection = mean_over_devices(kept, sent)
     grad_query_hidden = dot32(query_pre_grad, weight, NT).astype(bf16)
     grad_passage_hidden = dot32(passage_pre_grad, weight, NT).astype(bf16)
     losses = losses.reshape(queries)

time: 50.8 us -> 72.1 us (1.42)
  starting transfers between devices: 8.74 us -> 22 us
  blocking collectives: 15.4 us -> 27.8 us
  waiting for transfers between devices: 13.9 us -> 10.2 us
  other arithmetic: 0.78 us -> 0 us
    psum x0 -> x1, blocking collectives: none -> 27.8 us  [mean_over_devices(): share = lax.psum(share, 'batch')]
    ppermute x0 -> x4, starting transfers between devices: none -> 15.7 us  [swapped(): lax.ppermute(block, 'mp', [(i, i ^ bit) for i in range(lax.axis_size('mp'...]
    all_to_all x1 -> x0, blocking collectives: 15.4 us -> none  [mean_over_devices(): pieces = lax.all_to_all(padded.reshape(devices, share, columns), axes, 0, 0)]
    all_to_all x1 -> x0, waiting for transfers between devices: 6.28 us -> none  [mean_over_devices(): whole = lax.all_to_all(means, axes, 0, 0)]
    ppermute x0 -> x4, waiting for transfers between devices: none -> 2.65 us  [swapped(): lax.ppermute(block, 'mp', [(i, i ^ bit) for i in range(lax.axis_size('mp'...]
    all_to_all x1 -> x0, starting transfers between devices: 2.37 us -> none  [mean_over_devices(): whole = lax.all_to_all(means, axes, 0, 0)]
    convert_element_type x1 -> x0, other arithmetic: 0.78 us -> none  [mean_over_devices(): return whole.reshape(devices * share, columns)[:rows].astype(jnp.float32)]
    pallas_call x5 -> x8, Pallas kernels: 8.11 us -> 8.04 us  [call(): pl.pallas_call(body, out_shape=tuple(outs), in_specs=list(in_specs), out_...]
  transfers between devices with their start and end apart: 7 -> 10, of which waited for: 5 -> 6; matrix products, arithmetic and copies ran while one was open for 6% -> 4% of each run, Pallas kernels for 3% -> 2%
where the time goes in v3:
time: 72.1 us; the launch traced here: 71.7 us
  blocking collectives  27.8 us (39%)
  starting transfers between devices  22 us (31%)
  waiting for transfers between devices  10.2 us (14%)
  Pallas kernels  8.04 us (11%)
  matrix products  2.96 us (4%)
    psum x1, blocking collectives, mean_over_devices(): share = lax.psum(share, 'batch')  27.8 us
    ppermute x4, starting transfers between devices, swapped(): lax.ppermute(block, 'mp', [(i, i ^ bit) for i in range(lax.axis_size('mp'...  15.7 us
    pallas_call x8, Pallas kernels, call(): pl.pallas_call(body, out_shape=tuple(outs), in_specs=list(in_specs), out_...  8.04 us
    ppermute x6, waiting for transfers between devices, shifted(): return lax.ppermute(block, axis, route)  7.6 us
    ppermute x6, starting transfers between devices, shifted(): return lax.ppermute(block, axis, route)  6.37 us
    dot_general x2, matrix products, dot32(): lax.dot_general(left, right, dims, preferred_element_type=jnp.float32)  2.96 us
    ppermute x4, waiting for transfers between devices, swapped(): lax.ppermute(block, 'mp', [(i, i ^ bit) for i in range(lax.axis_size('mp'...  2.65 us
  transfers between devices with their start and end apart: 10, of which 6 were waited for; matrix products, arithmetic and copies ran while one was open for 4% of the time, Pallas kernels for 2%

profile of v3, /device:TPU:1, one launch (start us, length us, event | category | flops | bytes accessed | tf_op | source)
XLA Modules:
  0.0 71.7 jit_solution(15095964730679558838)
XLA Ops:
  0.6 1.8 %shard_map.93 = (f32[256,128]{1,0:T(8,128)S(1)}, bf16[272,128]{1,0:T(8,128)(2,1)S(1)}, s32[16,256]{1,0:T(8,128)S(1)}, s32[1,256]{1,0:T(1,128)S(1)}, bf16[256,768...) custom-call(s32[8]{0:T(128)} %query_lengths_in.1, s32[10]{0:T(128)} %passage_lengths_in.1, ...), custom_call_target="tpu_custom_call" | custom-call | flops 50331648 | bytes 5330024 | tf_op jit(solution)/shard_map/pallas_call | solution.py:38
  2.5 2.2 %collective-permute-start.1 = (bf16[272,128]{1,0:T(8,128)(2,1)S(1)}, bf16[272,128]{1,0:T(8,128)(2,1)S(1)}, u32[]{:S(2)}, u32[]{:S(2)}) collective-permute-start(bf16[272,128]{1,0:T(8,128)(2,1)S(1)} %get-tuple-element.37.sent.sent0), channel_id=1, source_target_pairs={{24,0},{28,4},{0,8},{4,12},{8,16},{12,20},{16,24},{20,28},{25,1},{... | collective-permute-start | bytes 208904 | tf_op jit(solution)/shard_map/ppermute | solution.py:28
  4.7 1.2 %collective-permute-start = (bf16[272,128]{1,0:T(8,128)(2,1)S(1)}, bf16[272,128]{1,0:T(8,128)(2,1)S(1)}, u32[]{:S(2)}, u32[]{:S(2)}) collective-permute-start(bf16[272,128]{1,0:T(8,128)(2,1)S(1)} %get-tuple-element.37.sent.sent0), channel_id=1, source_target_pairs={{28,0},{0,4},{4,8},{8,12},{12,16},{16,20},{20,24},{24,28},{29,1},{... | collective-permute-start | bytes 208904 | tf_op jit(solution)/shard_map/ppermute | solution.py:28
  5.9 1.5 %shard_map.94 = (f32[1280,128]{1,0:T(8,128)S(1)}, bf16[1280,128]{1,0:T(8,128)(2,1)S(1)}, f32[1280,256]{1,0:T(8,128)S(1)}, f32[16,256]{1,0:T(8,128)S(1)}, f32[16,256]{1,0:T(8,128)S(1)}) custom-call(s32[16,256]{1,0:T(8,128)S(1)} %get-tuple-element.35.valid, bf16[1280,768]{1,0:T(8,128)(2,1)S(1)} %get-tuple-element.34.hidden.passage_hidden, ...), custom_call_target="tpu_custom_call" | custom-call | flops 335544320 | bytes 4575232 | tf_op jit(solution)/shard_map/pallas_call | solution.py:38
  7.4 1.0 %collective-permute-done.1.sent2 = bf16[272,128]{1,0:T(8,128)(2,1)S(1)} collective-permute-done((bf16[272,128]{1,0:T(8,128)(2,1)S(1)}, bf16[272,128]{1,0:T(8,128)(2,1)S(1)}, u32[]{:S(2)}, u32[]{:S(2)}) %collective-permute-start.1) | collective-permute-done | bytes 69664 | tf_op jit(solution)/shard_map/ppermute | solution.py:28
  8.4 2.7 %collective-permute-done.sent1 = bf16[272,128]{1,0:T(8,128)(2,1)S(1)} collective-permute-done((bf16[272,128]{1,0:T(8,128)(2,1)S(1)}, bf16[272,128]{1,0:T(8,128)(2,1)S(1)}, u32[]{:S(2)}, u32[]{:S(2)}) %collective-permute-start) | collective-permute-done | bytes 69664 | tf_op jit(solution)/shard_map/ppermute | solution.py:28
  11.1 1.8 %shard_map.95 = (f32[1280,256]{1,0:T(8,128)S(1)}, f32[1280,256]{1,0:T(8,128)S(1)}, f32[16,256]{1,0:T(8,128)S(1)}, f32[16,256]{1,0:T(8,128)S(1)}, f32[16,256]{1,0...) custom-call(s32[16,256]{1,0:T(8,128)S(1)} %get-tuple-element.35.vali, ...), custom_call_target="tpu_custom_call" | custom-call | flops 335544320 | bytes 3342336 | tf_op jit(solution)/shard_map/pallas_call | solution.py:38
  12.9 0.1 collective-permute-start.4
  13.0 1.4 %collective-permute-start.5 = (bf16[144,256]{1,0:T(8,128)(2,1)S(1)}, bf16[144,256]{1,0:T(8,128)(2,1)S(1)}, u32[]{:S(2)}, u32[]{:S(2)}) collective-permute-start(bf16[144,256]{1,0:T(8,128)(2,1)S(1)} %get-tuple-element.52), channel_id=1, source_target_pairs={{8,0},{12,4},{16,8},{20,12},{24,16},{28,20},{0,24},{4,28},{9,1},{1... | collective-permute-start | bytes 221192 | tf_op jit(solution)/shard_map/ppermute | solution.py:28
  14.4 0.1 collective-permute-start.3
  14.5 1.4 %collective-permute-start.2 = (f32[8,256]{1,0:T(8,128)S(1)}, f32[8,256]{1,0:T(8,128)S(1)}, u32[]{:S(2)}, u32[]{:S(2)}) collective-permute-start(f32[8,256]{1,0:T(8,128)S(1)} %get-tuple-element.50.logs), channel_id=1, source_target_pairs={{28,0},{0,4},{4,8},{8,12},{12,16},{16,20},{20,24},{24,28},{29,1},{... | collective-permute-start | bytes 24584 | tf_op jit(solution)/shard_map/ppermute | solution.py:28
  15.9 2.9 %collective-permute-done.3.logs2 = f32[8,256]{1,0:T(8,128)S(1)} collective-permute-done((f32[8,256]{1,0:T(8,128)S(1)}, f32[8,256]{1,0:T(8,128)S(1)}, u32[]{:S(2)}, u32[]{:S(2)}) %collective-permute-start.3) | collective-permute-done | bytes 8224 | tf_op jit(solution)/shard_map/ppermute | solution.py:28
  18.8 1.0 %collective-permute-done.2.logs1 = f32[8,256]{1,0:T(8,128)S(1)} collective-permute-done((f32[8,256]{1,0:T(8,128)S(1)}, f32[8,256]{1,0:T(8,128)S(1)}, u32[]{:S(2)}, u32[]{:S(2)}) %collective-permute-start.2) | collective-permute-done | bytes 8224 | tf_op jit(solution)/shard_map/ppermute | solution.py:28
  19.8 0.0 collective-permute-done.4.back1
  19.8 0.0 collective-permute-done.5.back2
  19.8 2.1 %shard_map.96 = (f32[1,8]{1,0:T(1,128)}, bf16[256,128]{1,0:T(8,128)(2,1)S(1)}, bf16[1280,128]{1,0:T(8,128)(2,1)S(1)}, f32[384,128]{1,0:T(8,128)S(1)}, bf16[384,128]{1,0:T(8,128)(2,1)S(1)}) custom-call(s32[1,256]{1,0:T(1,128)S(1)} %get-tuple-element.32.wanted, bf16[256,768]{1,0:T(8,128)(2,1)S(1)} %get-tuple-element.33.query_hidden, ...), custom_call_target="tpu_custom_call" | custom-call | flops 637534208 | bytes 8573984 | tf_op jit(solution)/shard_map/pallas_call | solution.py:38
  21.8 3.8 %collective-permute-start.6 = (bf16[384,128]{1,0:T(8,128)(2,1)S(1)}, bf16[384,128]{1,0:T(8,128)(2,1)S(1)}, u32[]{:S(2)}, u32[]{:S(2)}) collective-permute-start(bf16[384,128]{1,0:T(8,128)(2,1)S(1)} %get-tuple-element.57), channel_id=1, source_target_pairs={{0,1},{1,0},{2,3},{3,2},{4,5},{5,4},{6,7},{7,6},{8,9},{9,8},{10,11... | collective-permute-start | bytes 294920 | tf_op jit(solution)/shard_map/ppermute | solution.py:249
  25.6 0.9 %collective-permute-done.6.taken = bf16[384,128]{1,0:T(8,128)(2,1)S(1)} collective-permute-done((bf16[384,128]{1,0:T(8,128)(2,1)S(1)}, bf16[384,128]{1,0:T(8,128)(2,1)S(1)}, u32[]{:S(2)}, u32[]{:S(2)}) %collective-permute-start.6) | collective-permute-done | bytes 98336 | tf_op jit(solution)/shard_map/ppermute | solution.py:249
  26.6 1.3 %collective-permute-start.7 = (bf16[192,128]{1,0:T(8,128)(2,1)S(1)}, bf16[192,128]{1,0:T(8,128)(2,1)S(1)}, u32[]{:S(2)}, u32[]{:S(2)}) collective-permute-start(bf16[192,128]{1,0:T(8,128)(2,1)S(1)} %get-tuple-element.59), channel_id=1, source_target_pairs={{0,2},{1,3},{2,0},{3,1},{4,6},{5,7},{6,4},{7,5},{8,10},{9,11},{10,... | collective-permute-start | bytes 147464 | tf_op jit(solution)/shard_map/ppermute | solution.py:249
  27.9 1.7 %collective-permute-done.7.taken = bf16[192,128]{1,0:T(8,128)(2,1)S(1)} collective-permute-done((bf16[192,128]{1,0:T(8,128)(2,1)S(1)}, bf16[192,128]{1,0:T(8,128)(2,1)S(1)}, u32[]{:S(2)}, u32[]{:S(2)}) %collective-permute-start.7) | collective-permute-done | bytes 49184 | tf_op jit(solution)/shard_map/ppermute | solution.py:249
  29.6 27.8 %psum.7.mine = bf16[192,128]{1,0:T(8,128)(2,1)S(1)} all-reduce(bf16[192,128]{1,0:T(8,128)(2,1)S(1)} %shard_map.98), channel_id=1, replica_groups=mesh['batch'=8,'mp'=4] {'batch'}, use_global_device_ids=true, to_apply=%region_0.0 | all-reduce | flops 24576 | bytes 98304 | tf_op jit(solution)/shard_map/psum | solution.py:276
  57.4 1.3 %collective-permute-start.8 = (bf16[192,128]{1,0:T(8,128)(2,1)S(1)}, bf16[192,128]{1,0:T(8,128)(2,1)S(1)}, u32[]{:S(2)}, u32[]{:S(2)}) collective-permute-start(bf16[192,128]{1,0:T(8,128)(2,1)S(1)} %psum.7.mine), channel_id=1, source_target_pairs={{0,2},{1,3},{2,0},{3,1},{4,6},{5,7},{6,4},{7,5},{8,10},{9,11},{10,... | collective-permute-start | bytes 147464 | tf_op jit(solution)/shard_map/ppermute | solution.py:249
  58.7 1.9 %convolution_convert_fusion = bf16[1280,768]{1,0:T(8,128)(2,1)} fusion(bf16[1280,128]{1,0:T(8,128)(2,1)S(1)} %get-tuple-element.55, bf16[768,128]{1,0:T(8,128)(2,1)S(1)} %get-tuple-element.36.projection), kind=kOutput, calls=%fused_computation | convolution fusion | flops 252641280 | bytes 2490368 | tf_op jit(solution)/shard_map/dot_general | solution.py:32
  60.6 0.0 collective-permute-done.8.taken
  60.7 9.3 %collective-permute-start.9 = (bf16[384,128]{1,0:T(8,128)(2,1)S(1)}, bf16[384,128]{1,0:T(8,128)(2,1)S(1)}, u32[]{:S(2)}, u32[]{:S(2)}) collective-permute-start(bf16[384,128]{1,0:T(8,128)(2,1)S(1)} %shard_map.99.mine), channel_id=1, source_target_pairs={{0,1},{1,0},{2,3},{3,2},{4,5},{5,4},{6,7},{7,6},{8,9},{9,8},{10,11... | collective-permute-start | bytes 294920 | tf_op jit(solution)/shard_map/ppermute | solution.py:249
  69.9 1.0 %convolution_convert_fusion.1 = bf16[256,768]{1,0:T(8,128)(2,1)} fusion(bf16[256,128]{1,0:T(8,128)(2,1)S(1)} %get-tuple-element.54, bf16[768,128]{1,0:T(8,128)(2,1)S(1)} %get-tuple-element.36.projection), kind=kOutput, calls=%fused_computation.1 | convolution fusion | flops 50528256 | bytes 655360 | tf_op jit(solution)/shard_map/dot_general | solution.py:32
  71.0 0.0 collective-permute-done.9.taken
  71.0 0.8 %shard_map.100 = f32[768,128]{1,0:T(8,128)} custom-call(bf16[384,128]{1,0:T(8,128)(2,1)S(1)} %shard_map.99.mine, bf16[384,128]{1,0:T(8,128)(2,1)S(1)} %collective-permute-done.9.taken), custom_call_target="tpu_custom_call" | custom-call | bytes 589824 | tf_op jit(solution)/shard_map/pallas_call | solution.py:38
  (3 shorter events, 0.1 us)
Async XLA Ops:
  2.5 5.9 %collective-permute-start.1 = (bf16[272,128]{1,0:T(8,128)(2,1)S(1)}, bf16[272,128]{1,0:T(8,128)(2,1)S(1)}, u32[]{:S(2)}, u32[]{:S(2)}) collective-permute-start(bf16[272,128]{1,0:T(8,128)(2,1)S(1)} %get-tuple-element.37.sent.sent0), channel_id=1, source_target_pairs={{24,0},{28,4},{0,8},{4,12},{8,16},{12,20},{16,24},{20,28},{25,1},{... | collective-permute-start | bytes 208904 | tf_op jit(solution)/shard_map/ppermute | solution.py:28
  4.7 6.5 %collective-permute-start = (bf16[272,128]{1,0:T(8,128)(2,1)S(1)}, bf16[272,128]{1,0:T(8,128)(2,1)S(1)}, u32[]{:S(2)}, u32[]{:S(2)}) collective-permute-start(bf16[272,128]{1,0:T(8,128)(2,1)S(1)} %get-tuple-element.37.sent.sent0), channel_id=1, source_target_pairs={{28,0},{0,4},{4,8},{8,12},{12,16},{16,20},{20,24},{24,28},{29,1},{... | collective-permute-start | bytes 208904 | tf_op jit(solution)/shard_map/ppermute | solution.py:28
  12.9 6.8 %collective-permute-start.4 = (bf16[144,256]{1,0:T(8,128)(2,1)S(1)}, bf16[144,256]{1,0:T(8,128)(2,1)S(1)}, u32[]{:S(2)}, u32[]{:S(2)}) collective-permute-start(bf16[144,256]{1,0:T(8,128)(2,1)S(1)} %get-tuple-element.51), channel_id=1, source_target_pairs={{4,0},{8,4},{12,8},{16,12},{20,16},{24,20},{28,24},{0,28},{5,1},{9... | collective-permute-start | bytes 221192 | tf_op jit(solution)/shard_map/ppermute | solution.py:28
  13.0 6.8 %collective-permute-start.5 = (bf16[144,256]{1,0:T(8,128)(2,1)S(1)}, bf16[144,256]{1,0:T(8,128)(2,1)S(1)}, u32[]{:S(2)}, u32[]{:S(2)}) collective-permute-start(bf16[144,256]{1,0:T(8,128)(2,1)S(1)} %get-tuple-element.52), channel_id=1, source_target_pairs={{8,0},{12,4},{16,8},{20,12},{24,16},{28,20},{0,24},{4,28},{9,1},{1... | collective-permute-start | bytes 221192 | tf_op jit(solution)/shard_map/ppermute | solution.py:28
  14.4 4.4 %collective-permute-start.3 = (f32[8,256]{1,0:T(8,128)S(1)}, f32[8,256]{1,0:T(8,128)S(1)}, u32[]{:S(2)}, u32[]{:S(2)}) collective-permute-start(f32[8,256]{1,0:T(8,128)S(1)} %get-tuple-element.50.logs), channel_id=1, source_target_pairs={{24,0},{28,4},{0,8},{4,12},{8,16},{12,20},{16,24},{20,28},{25,1},{... | collective-permute-start | bytes 24584 | tf_op jit(solution)/shard_map/ppermute | solution.py:28
  14.5 5.3 %collective-permute-start.2 = (f32[8,256]{1,0:T(8,128)S(1)}, f32[8,256]{1,0:T(8,128)S(1)}, u32[]{:S(2)}, u32[]{:S(2)}) collective-permute-start(f32[8,256]{1,0:T(8,128)S(1)} %get-tuple-element.50.logs), channel_id=1, source_target_pairs={{28,0},{0,4},{4,8},{8,12},{12,16},{16,20},{20,24},{24,28},{29,1},{... | collective-permute-start | bytes 24584 | tf_op jit(solution)/shard_map/ppermute | solution.py:28
  21.8 4.7 %collective-permute-start.6 = (bf16[384,128]{1,0:T(8,128)(2,1)S(1)}, bf16[384,128]{1,0:T(8,128)(2,1)S(1)}, u32[]{:S(2)}, u32[]{:S(2)}) collective-permute-start(bf16[384,128]{1,0:T(8,128)(2,1)S(1)} %get-tuple-element.57), channel_id=1, source_target_pairs={{0,1},{1,0},{2,3},{3,2},{4,5},{5,4},{6,7},{7,6},{8,9},{9,8},{10,11... | collective-permute-start | bytes 294920 | tf_op jit(solution)/shard_map/ppermute | solution.py:249
  26.6 3.0 %collective-permute-start.7 = (bf16[192,128]{1,0:T(8,128)(2,1)S(1)}, bf16[192,128]{1,0:T(8,128)(2,1)S(1)}, u32[]{:S(2)}, u32[]{:S(2)}) collective-permute-start(bf16[192,128]{1,0:T(8,128)(2,1)S(1)} %get-tuple-element.59), channel_id=1, source_target_pairs={{0,2},{1,3},{2,0},{3,1},{4,6},{5,7},{6,4},{7,5},{8,10},{9,11},{10,... | collective-permute-start | bytes 147464 | tf_op jit(solution)/shard_map/ppermute | solution.py:249
  57.4 3.3 %collective-permute-start.8 = (bf16[192,128]{1,0:T(8,128)(2,1)S(1)}, bf16[192,128]{1,0:T(8,128)(2,1)S(1)}, u32[]{:S(2)}, u32[]{:S(2)}) collective-permute-start(bf16[192,128]{1,0:T(8,128)(2,1)S(1)} %psum.7.mine), channel_id=1, source_target_pairs={{0,2},{1,3},{2,0},{3,1},{4,6},{5,7},{6,4},{7,5},{8,10},{9,11},{10,... | collective-permute-start | bytes 147464 | tf_op jit(solution)/shard_map/ppermute | solution.py:249
  60.7 10.3 %collective-permute-start.9 = (bf16[384,128]{1,0:T(8,128)(2,1)S(1)}, bf16[384,128]{1,0:T(8,128)(2,1)S(1)}, u32[]{:S(2)}, u32[]{:S(2)}) collective-permute-start(bf16[384,128]{1,0:T(8,128)(2,1)S(1)} %shard_map.99.mine), channel_id=1, source_target_pairs={{0,1},{1,0},{2,3},{3,2},{4,5},{5,4},{6,7},{7,6},{8,9},{9,8},{10,11... | collective-permute-start | bytes 294920 | tf_op jit(solution)/shard_map/ppermute | solution.py:249

commit v4 on v2

--- a/solution.py
+++ b/solution.py
@@ -34,7 +34,7 @@
 
 def call(body, outs, in_specs, args, scratch=(), flops=0, trans=0):
     moved = sum(a.size * a.dtype.itemsize for a in args)
-    moved += sum(math.prod(o.shape) * o.dtype.itemsize for o in outs)
+    moved += sum(math.prod(o.shape) * jnp.dtype(o.dtype).itemsize for o in outs)
     return pl.pallas_call(
         body,
         out_shape=tuple(outs),
@@ -129,18 +129,24 @@
     rows = sent.shape[0] - ROWS
     tokens = embed.shape[0] // passages
     query = sent[:rows, :]
-    slot = lax.broadcasted_iota(jnp.int32, (tokens, rows), 0)
+    half = tokens // 2
+    slot = lax.broadcasted_iota(jnp.int32, (tokens - half, rows), 0) + half
     totals[...] = jnp.ones(totals.shape, jnp.float32)
     tops[...] = jnp.zeros(tops.shape, jnp.float32)
     for c in range(passages):
-        part = slice(c * tokens, (c + 1) * tokens)
-        sims = dot32(embed[part, :], query, NT)
-        sims = jnp.where(slot < valid[c : c + 1, :], sims, -jnp.inf)
-        top = jnp.max(sims, axis=0, keepdims=True)
-        power = jnp.exp2((sims - top) * (inner_scale * LOG2E))
-        powers[part, :] = power
+        sims = dot32(embed[c * tokens : (c + 1) * tokens, :], query, NT)
+        low, high = sims[:half], jnp.where(slot < valid[c : c + 1, :], sims[half:], -jnp.inf)
+        top = jnp.maximum(
+            jnp.max(low, axis=0, keepdims=True), jnp.max(high, axis=0, keepdims=True)
+        )
+        low = jnp.exp2((low - top) * (inner_scale * LOG2E))
+        high = jnp.exp2((high - top) * (inner_scale * LOG2E))
+        powers[c * tokens : c * tokens + half, :] = low
+        powers[c * tokens + half : (c + 1) * tokens, :] = high
         tops[c : c + 1, :] = top
-        totals[c : c + 1, :] = jnp.sum(power, axis=0, keepdims=True)
+        totals[c : c + 1, :] = jnp.sum(low, axis=0, keepdims=True) + jnp.sum(
+            high, axis=0, keepdims=True
+        )
     best = tops[...] + jnp.log(totals[...]) / inner_scale
     best = best * sent_keep(sent, rows)
     group = rows // queries
@@ -153,12 +159,13 @@
 
 def own_score_body(
     queries, passages, valid, hidden, projection, sent,
-    before_out, embed_out, powers, totals, scores, tops,
+    before_out, embed_out, powers, totals, scores, log_out, tops,
 ):
     before = dot32(hidden[...], projection[...])
     before_out[...] = before
     embed_out[...] = unit_rows(before)[0].astype(jnp.bfloat16)
     score_block(queries, passages, valid, embed_out, sent, powers, totals, scores, tops)
+    log_out[...] = stack_rows(log_out.shape, (log_sum(scores[...]),))
 
 
 def log_sum(scores):
@@ -190,24 +197,24 @@
 
 
 def other_score_body(
-    queries, passages, valid, embed, sent1, sent2, scores0,
-    powers1, powers2, totals1, totals2, scores1, scores2, logs, back1, back2, tops, grad_sim,
+    queries, passages, valid, embed, sent1, sent2, log0, far0,
+    grad_sim, logs, back1, back2, powers1, powers2, totals1, totals2, scores1, scores2, tops,
 ):
     rows = powers1.shape[1]
     dim = embed.shape[1]
     score_block(queries, passages, valid, embed, sent2, powers2, totals2, scores2, tops)
     score_block(queries, passages, valid, embed, sent1, powers1, totals1, scores1, tops)
-    log0, log1, log2 = [log_sum(scores[...]) for scores in (scores0, scores1, scores2)]
-    logs[...] = stack_rows(logs.shape, (log0, log1, log2))
+    log1, log2 = log_sum(scores1[...]), log_sum(scores2[...])
+    logs[...] = stack_rows(logs.shape, (log0[0:1, :], log1, log2, far0[0:1, :]))
     turned = embed[...].T
-    for log, sent, powers, totals, scores, back, tail in (
-        (log2, sent2, powers2, totals2, scores2, back2, split(log2)),
-        (log1, sent1, powers1, totals1, scores1, back1, split(log1) + split(log2)),
+    for column, log, sent, powers, totals, scores, back, tail in (
+        (rows, log2, sent2, powers2, totals2, scores2, back2, split(log2)),
+        (0, log1, sent1, powers1, totals1, scores1, back1, split(log1) + split(log2)),
     ):
         dscore = loss_scale * jnp.exp(scores[...] - log)
         coefficient = outer_scale * dscore * sent_keep(sent, rows) / totals[...]
-        fill_grad_sim(passages, coefficient, powers, grad_sim, 0)
-        back[:dim, :] = dot32(turned, grad_sim[...]).astype(jnp.bfloat16)
+        fill_grad_sim(passages, coefficient, powers, grad_sim, column)
+        back[:dim, :] = dot32(turned, grad_sim[:, column : column + rows]).astype(jnp.bfloat16)
         tail = stack_rows((ROWS, rows), [part.astype(jnp.float32) for part in tail])
         back[dim:, :] = tail.astype(jnp.bfloat16)
 
@@ -220,16 +227,15 @@
 
 def grad_body(
     queries, passages, wanted, query_hidden, passage_hidden, embed, query_before, passage_before,
-    powers0, powers1, powers2, totals0, totals1, totals2, scores0, scores1, scores2,
-    sent0, sent1, sent2, logs, logs1, logs2, back1, back2,
+    powers, totals, scores0, sent0, sent1, sent2, other_grad_sim, logs, logs1, back1, back2,
     losses, query_pre_grad, passage_pre_grad, partial, grad_sim,
 ):
-    rows = powers0.shape[1]
+    rows = powers.shape[1]
     dim = embed.shape[1]
     second, third = joined(back1, dim, 0), joined(back2, dim, 0)
     total0 = log_add((logs[0:1, :], second, third))
     total1 = log_add((logs1[0:1, :], logs[1:2, :], joined(back1, dim, 3)))
-    total2 = log_add((logs2[0:1, :], logs1[1:2, :], logs[2:3, :]))
+    total2 = log_add((logs[3:4, :], logs1[1:2, :], logs[2:3, :]))
     scores = scores0[...]
     onehot = lax.broadcasted_iota(jnp.int32, scores.shape, 0) == wanted[...]
     loss = total0 - jnp.sum(jnp.where(onehot, scores, 0.0), axis=0, keepdims=True)
@@ -237,26 +243,23 @@
     pick = (pick == lax.broadcasted_iota(jnp.int32, (rows, LANES), 0)).astype(jnp.bfloat16)
     losses[...] = sum(dot32(part, pick) for part in split(loss))[:, :queries]
 
-    for block, (total, sent, powers, totals, scores) in enumerate((
-        (total0, sent0, powers0, totals0, scores0),
-        (total1, sent1, powers1, totals1, scores1),
-        (total2, sent2, powers2, totals2, scores2),
-    )):
-        dscore = jnp.exp(scores[...] - total)
-        if block == 0:
-            dscore = dscore - onehot.astype(jnp.float32)
-        coefficient = (outer_scale * loss_scale) * dscore * sent_keep(sent, rows) / totals[...]
-        fill_grad_sim(passages, coefficient, powers, grad_sim, block * rows)
-
-    to_query = dot32(embed[...].T, grad_sim[:, :rows])
+    shares = (jnp.exp(logs[1:2, :] - total1), jnp.exp(logs[2:3, :] - total2))
+    shares = stack_rows((8, rows), shares).T
+    first = (sent1[:rows, :].astype(jnp.float32) * shares[:, 0:1]).astype(jnp.bfloat16)
+    grad = dot32(other_grad_sim[:, :rows], first)
+    first = (sent2[:rows, :].astype(jnp.float32) * shares[:, 1:2]).astype(jnp.bfloat16)
+    grad += dot32(other_grad_sim[:, rows:], first)
+
+    dscore = loss_scale * (jnp.exp(scores - total0) - onehot.astype(jnp.float32))
+    coefficient = outer_scale * dscore * sent_keep(sent0, rows) / totals[...]
+    fill_grad_sim(passages, coefficient, powers, grad_sim, 0)
+    to_query = dot32(embed[...].T, grad_sim[...])
     to_query += back1[:dim, :].astype(jnp.float32) * jnp.exp(second - total0)
     to_query += back2[:dim, :].astype(jnp.float32) * jnp.exp(third - total0)
     pre = back_rows(to_query.T, query_before[...])
     query_pre_grad[...] = pre
     both = dot32(pre.T, query_hidden[...])
-    grad = dot32(grad_sim[:, :rows], sent0[:rows, :])
-    grad += dot32(grad_sim[:, rows : 2 * rows], sent1[:rows, :])
-    grad += dot32(grad_sim[:, 2 * rows :], sent2[:rows, :])
+    grad += dot32(grad_sim[...], sent0[:rows, :])
     pre = back_rows(grad, passage_before[...])
     passage_pre_grad[...] = pre
     both += dot32(pre.T, passage_hidden[...])
@@ -279,7 +282,7 @@
     pieces = lax.all_to_all(padded.reshape(devices, share, columns), axes, 0, 0)
     means = call(
         functools.partial(sum_body, 1.0 / devices, devices),
-        (jax.ShapeDtypeStruct(pieces.shape, jnp.bfloat16),),
+        (pltpu.VMEM(pieces.shape, jnp.bfloat16),),
         (vmem,),
         (pieces,),
     )[0]
@@ -321,40 +324,41 @@
     )
     sent1 = shifted(sent0, "batch", 1)
     sent2 = shifted(sent0, "batch", 2)
-    passage_before, embed, powers0, totals0, scores0 = call(
+    passage_before, embed, powers0, totals0, scores0, log0 = call(
         functools.partial(own_score_body, queries, passages),
-        (of((slots, dim), f32), of((slots, dim), bf16), of((slots, rows), f32), pair, pair),
+        (
+            of((slots, dim), f32), of((slots, dim), bf16), of((slots, rows), f32), pair, pair,
+            of((8, rows), f32),
+        ),
         (vmem,) * 4,
         (valid, passage_rows, weight, sent0),
         scratch=(pairs,),
         flops=2 * slots * dim * (width + rows),
         trans=slots * rows,
     )
-    powers1, powers2, totals1, totals2, scores1, scores2, logs, back1, back2 = call(
+    far0 = shifted(log0, "batch", 2)
+    other_grad_sim, logs, back1, back2 = call(
         functools.partial(other_score_body, queries, passages),
-        (of((slots, rows), f32),) * 2 + (pair,) * 4
-        + (of((8, rows), f32),) + (of((dim + ROWS, rows), bf16),) * 2,
-        (vmem,) * 5,
-        (valid, embed, sent1, sent2, scores0),
-        scratch=(pairs, pltpu.VMEM((slots, rows), bf16)),
+        (of((slots, 2 * rows), bf16), of((8, rows), f32)) + (of((dim + ROWS, rows), bf16),) * 2,
+        (vmem,) * 6,
+        (valid, embed, sent1, sent2, log0, far0),
+        scratch=(pltpu.VMEM((slots, rows), f32),) * 2 + (pairs,) * 5,
         flops=8 * slots * dim * rows,
         trans=2 * slots * rows,
     )
     back2 = shifted(back2, "batch", -2)
     back1 = shifted(back1, "batch", -1)
     logs1 = shifted(logs, "batch", 1)
-    logs2 = shifted(logs, "batch", 2)
     losses, query_pre_grad, passage_pre_grad, partial = call(
         functools.partial(grad_body, queries, passages),
         (
             of((1, queries), f32), of((rows, dim), bf16), of((slots, dim), bf16),
             of((width, dim), bf16),
         ),
-        (vmem,) * 23,
+        (vmem,) * 17,
         (wanted, query_rows, passage_rows, embed, query_before, passage_before,
-         powers0, powers1, powers2, totals0, totals1, totals2, scores0, scores1, scores2,
-         sent0, sent1, sent2, logs, logs1, logs2, back1, back2),
-        scratch=(pltpu.VMEM((slots, 3 * rows), bf16),),
+         powers0, totals0, scores0, sent0, sent1, sent2, other_grad_sim, logs, logs1, back1, back2),
+        scratch=(pltpu.VMEM((slots, rows), bf16),),
         flops=8 * slots * dim * rows + 2 * (slots + rows) * width * dim,
     )
     grad_projection = mean_over_devices(partial)

time: 50.8 us -> 50.8 us (level)
  blocking collectives: 15.4 us -> 14.4 us
  waiting for transfers between devices: 13.9 us -> 14.9 us
    all_to_all x1, blocking collectives: 15.4 us -> 14.4 us  [mean_over_devices(): pieces = lax.all_to_all(padded.reshape(devices, share, columns), axes, 0, 0)]
    ppermute x6, waiting for transfers between devices: 7.6 us -> 8.61 us  [shifted(): return lax.ppermute(block, axis, route)]
  transfers between devices with their start and end apart: 7 -> 7, of which waited for: 5 -> 3; matrix products, arithmetic and copies ran while one was open for 6% -> 6% of each run, Pallas kernels for 3% -> 3%
where the time goes in v4:
time: 50.8 us; the launch traced here: 50.5 us
  waiting for transfers between devices  14.9 us (29%)
  blocking collectives  14.4 us (28%)
  starting transfers between devices  8.71 us (17%)
  Pallas kernels  8.19 us (16%)
  matrix products  2.96 us (6%)
  other arithmetic  0.78 us (2%)
  between operations  0.67 us (1%)
    all_to_all x1, blocking collectives, mean_over_devices(): pieces = lax.all_to_all(padded.reshape(devices, share, columns), axes, 0, 0)  14.4 us
    ppermute x6, waiting for transfers between devices, shifted(): return lax.ppermute(block, axis, route)  8.61 us
    pallas_call x5, Pallas kernels, call(): pl.pallas_call(body, out_shape=tuple(outs), in_specs=list(in_specs), out_...  8.19 us
    ppermute x6, starting transfers between devices, shifted(): return lax.ppermute(block, axis, route)  6.34 us
    all_to_all x1, waiting for transfers between devices, mean_over_devices(): whole = lax.all_to_all(means, axes, 0, 0)  6.27 us
    dot_general x2, matrix products, dot32(): lax.dot_general(left, right, dims, preferred_element_type=jnp.float32)  2.96 us
    all_to_all x1, starting transfers between devices, mean_over_devices(): whole = lax.all_to_all(means, axes, 0, 0)  2.37 us
  transfers between devices with their start and end apart: 7, of which 3 were waited for; matrix products, arithmetic and copies ran while one was open for 6% of the time, Pallas kernels for 3%

profile of v4, /device:TPU:1, one launch (start us, length us, event | category | flops | bytes accessed | tf_op | source)
XLA Modules:
  0.0 50.5 jit_solution(7911392860070659873)
XLA Ops:
  0.6 1.8 %shard_map.93 = (f32[256,128]{1,0:T(8,128)S(1)}, bf16[272,128]{1,0:T(8,128)(2,1)S(1)}, s32[16,256]{1,0:T(8,128)S(1)}, s32[1,256]{1,0:T(1,128)S(1)}, bf16[256,768...) custom-call(s32[8]{0:T(128)} %query_lengths_in.1, s32[10]{0:T(128)} %passage_lengths_in.1, ...), custom_call_target="tpu_custom_call" | custom-call | flops 50331648 | bytes 5330024 | tf_op jit(solution)/shard_map/pallas_call | solution.py:38
  2.5 2.2 %collective-permute-start.1 = (bf16[272,128]{1,0:T(8,128)(2,1)S(1)}, bf16[272,128]{1,0:T(8,128)(2,1)S(1)}, u32[]{:S(2)}, u32[]{:S(2)}) collective-permute-start(bf16[272,128]{1,0:T(8,128)(2,1)S(1)} %get-tuple-element.30.sent.sent0), channel_id=1, source_target_pairs={{24,0},{28,4},{0,8},{4,12},{8,16},{12,20},{16,24},{20,28},{25,1},{... | collective-permute-start | bytes 208904 | tf_op jit(solution)/shard_map/ppermute | solution.py:28
  4.7 1.2 %collective-permute-start = (bf16[272,128]{1,0:T(8,128)(2,1)S(1)}, bf16[272,128]{1,0:T(8,128)(2,1)S(1)}, u32[]{:S(2)}, u32[]{:S(2)}) collective-permute-start(bf16[272,128]{1,0:T(8,128)(2,1)S(1)} %get-tuple-element.30.sent.sent0), channel_id=1, source_target_pairs={{28,0},{0,4},{4,8},{8,12},{12,16},{16,20},{20,24},{24,28},{29,1},{... | collective-permute-start | bytes 208904 | tf_op jit(solution)/shard_map/ppermute | solution.py:28
  5.9 1.5 %shard_map.94 = (f32[1280,128]{1,0:T(8,128)S(1)}, bf16[1280,128]{1,0:T(8,128)(2,1)S(1)}, f32[1280,256]{1,0:T(8,128)S(1)}, f32[16,256]{1,0:T(8,128)S(1)}, f32[16,256]{1,0:T(8,128)S(1)}, /*index=5*/f32[8,256]{1,0:T(8,128)S(1)}) custom-call(s32[16,256]{1,0:T(8,128)S(1)} %get-tuple-element.28.valid, ...), custom_call_target="tpu_custom_call" | custom-call | flops 335544320 | bytes 4583424 | tf_op jit(solution)/shard_map/pallas_call | solution.py:38
  7.4 1.3 %collective-permute-start.2 = (f32[8,256]{1,0:T(8,128)S(1)}, f32[8,256]{1,0:T(8,128)S(1)}, u32[]{:S(2)}, u32[]{:S(2)}) collective-permute-start(f32[8,256]{1,0:T(8,128)S(1)} %get-tuple-element.37.log0), channel_id=1, source_target_pairs={{24,0},{28,4},{0,8},{4,12},{8,16},{12,20},{16,24},{20,28},{25,1},{... | collective-permute-start | bytes 24584 | tf_op jit(solution)/shard_map/ppermute | solution.py:28
  8.7 3.3 %collective-permute-done.2.far0 = f32[8,256]{1,0:T(8,128)S(1)} collective-permute-done((f32[8,256]{1,0:T(8,128)S(1)}, f32[8,256]{1,0:T(8,128)S(1)}, u32[]{:S(2)}, u32[]{:S(2)}) %collective-permute-start.2) | collective-permute-done | bytes 8224 | tf_op jit(solution)/shard_map/ppermute | solution.py:28
  12.0 0.0 collective-permute-done.1.sent2
  12.0 0.0 collective-permute-done.sent1
  12.0 1.7 %shard_map.95 = (bf16[1280,512]{1,0:T(8,128)(2,1)S(1)}, f32[8,256]{1,0:T(8,128)S(1)}, bf16[144,256]{1,0:T(8,128)(2,1)S(1)}, bf16[144,256]{1,0:T(8,128)(2,1)S(1)}) custom-call(s32[16,256]{1,0:T(8,128)S(1)} %get-tuple-element.28.valid, bf16[1280,128]{1,0:T(8,128)(2,1)S(1)} %get-tuple-element.31.embed, bf16[272,128]{1,0:T(8,128)(2,1)S(1)} %collective-permute-done.sent1, ...), custom_call_target="tpu_custom_call" | custom-call | flops 335544320 | bytes 1966080 | tf_op jit(solution)/shard_map/pallas_call | solution.py:38
  13.8 1.1 %collective-permute-start.4 = (bf16[144,256]{1,0:T(8,128)(2,1)S(1)}, bf16[144,256]{1,0:T(8,128)(2,1)S(1)}, u32[]{:S(2)}, u32[]{:S(2)}) collective-permute-start(bf16[144,256]{1,0:T(8,128)(2,1)S(1)} %get-tuple-element.40), channel_id=1, source_target_pairs={{4,0},{8,4},{12,8},{16,12},{20,16},{24,20},{28,24},{0,28},{5,1},{9... | collective-permute-start | bytes 221192 | tf_op jit(solution)/shard_map/ppermute | solution.py:28
  14.8 0.5 %collective-permute-start.5 = (bf16[144,256]{1,0:T(8,128)(2,1)S(1)}, bf16[144,256]{1,0:T(8,128)(2,1)S(1)}, u32[]{:S(2)}, u32[]{:S(2)}) collective-permute-start(bf16[144,256]{1,0:T(8,128)(2,1)S(1)} %get-tuple-element.41), channel_id=1, source_target_pairs={{8,0},{12,4},{16,8},{20,12},{24,16},{28,20},{0,24},{4,28},{9,1},{1... | collective-permute-start | bytes 221192 | tf_op jit(solution)/shard_map/ppermute | solution.py:28
  15.4 0.0 collective-permute-start.3
  15.4 5.3 %collective-permute-done.3.logs1 = f32[8,256]{1,0:T(8,128)S(1)} collective-permute-done((f32[8,256]{1,0:T(8,128)S(1)}, f32[8,256]{1,0:T(8,128)S(1)}, u32[]{:S(2)}, u32[]{:S(2)}) %collective-permute-start.3) | collective-permute-done | bytes 8224 | tf_op jit(solution)/shard_map/ppermute | solution.py:28
  20.7 0.0 collective-permute-done.4.back1
  20.7 0.0 collective-permute-done.5.back2
  20.7 2.4 %shard_map.96 = (f32[1,8]{1,0:T(1,128)}, bf16[256,128]{1,0:T(8,128)(2,1)S(1)}, bf16[1280,128]{1,0:T(8,128)(2,1)S(1)}, bf16[768,128]{1,0:T(8,128)(2,1)S(1)}) custom-call(s32[1,256]{1,0:T(1,128)S(1)} %get-tuple-element.25.wanted, bf16[256,768]{1,0:T(8,128)(2,1)S(1)} %get-tuple-element.26.query_hidden, ...), custom_call_target="tpu_custom_call" | custom-call | flops 637534208 | bytes 7091232 | tf_op jit(solution)/shard_map/pallas_call | solution.py:38
  23.1 14.4 %all_to_all.10.pieces = bf16[32,24,128]{2,1,0:T(8,128)(2,1)S(1)} all-to-all(bf16[32,24,128]{2,1,0:T(8,128)(2,1)S(1)} %bitcast.9), channel_id=1, replica_groups=mesh['batch'=8,'mp'=4] {'batch','mp'}, dimensions={0} | all-to-all | bytes 393216 | tf_op jit(solution)/shard_map/all_to_all | solution.py:282
  37.4 0.7 %shard_map.97 = bf16[32,24,128]{2,1,0:T(8,128)(2,1)} custom-call(bf16[32,24,128]{2,1,0:T(8,128)(2,1)S(1)} %all_to_all.10.pieces), custom_call_target="tpu_custom_call" | custom-call | bytes 393216 | tf_op jit(solution)/shard_map/pallas_call | solution.py:38
  38.2 2.4 %all-to-all-start.1 = ((bf16[32,24,128]{2,1,0:T(8,128)(2,1)}), bf16[32,24,128]{2,1,0:T(8,128)(2,1)S(1)}, u32[]{:S(2)}, u32[]{:S(2)}) async-start(bf16[32,24,128]{2,1,0:T(8,128)(2,1)} %shard_map.97), calls=%async_computation.1 | async-start | bytes 393216 | tf_op jit(solution)/shard_map/all_to_all | solution.py:289
  40.5 1.0 %convolution_convert_fusion.1 = bf16[256,768]{1,0:T(8,128)(2,1)} fusion(bf16[256,128]{1,0:T(8,128)(2,1)S(1)} %get-tuple-element.43, bf16[768,128]{1,0:T(8,128)(2,1)S(1)} %get-tuple-element.29.projection), kind=kOutput, calls=%fused_computation.1 | convolution fusion | flops 50528256 | bytes 655360 | tf_op jit(solution)/shard_map/dot_general | solution.py:32
  41.5 1.9 %convolution_convert_fusion = bf16[1280,768]{1,0:T(8,128)(2,1)} fusion(bf16[1280,128]{1,0:T(8,128)(2,1)S(1)} %get-tuple-element.44, bf16[768,128]{1,0:T(8,128)(2,1)S(1)} %get-tuple-element.29.projection), kind=kOutput, calls=%fused_computation | convolution fusion | flops 252641280 | bytes 2490368 | tf_op jit(solution)/shard_map/dot_general | solution.py:32
  43.5 6.3 %all-to-all-done.1 = bf16[32,24,128]{2,1,0:T(8,128)(2,1)S(1)} async-done(((bf16[32,24,128]{2,1,0:T(8,128)(2,1)}), bf16[32,24,128]{2,1,0:T(8,128)(2,1)S(1)}, u32[]{:S(2)}, u32[]{:S(2)}) %all-to-all-start.1) | async-done | bytes 196640 | tf_op jit(solution)/shard_map/all_to_all | solution.py:289
  49.8 0.8 %bitcast_convert_fusion = f32[768,128]{1,0:T(8,128)} fusion(bf16[32,24,128]{2,1,0:T(8,128)(2,1)S(1)} %all-to-all-done.1), kind=kLoop, calls=%fused_computation.2 | loop fusion | flops 98304 | bytes 589824 | tf_op jit(solution)/shard_map/convert_element_type | solution.py:290
Async XLA Ops:
  2.5 9.6 %collective-permute-start.1 = (bf16[272,128]{1,0:T(8,128)(2,1)S(1)}, bf16[272,128]{1,0:T(8,128)(2,1)S(1)}, u32[]{:S(2)}, u32[]{:S(2)}) collective-permute-start(bf16[272,128]{1,0:T(8,128)(2,1)S(1)} %get-tuple-element.30.sent.sent0), channel_id=1, source_target_pairs={{24,0},{28,4},{0,8},{4,12},{8,16},{12,20},{16,24},{20,28},{25,1},{... | collective-permute-start | bytes 208904 | tf_op jit(solution)/shard_map/ppermute | solution.py:28
  4.7 7.4 %collective-permute-start = (bf16[272,128]{1,0:T(8,128)(2,1)S(1)}, bf16[272,128]{1,0:T(8,128)(2,1)S(1)}, u32[]{:S(2)}, u32[]{:S(2)}) collective-permute-start(bf16[272,128]{1,0:T(8,128)(2,1)S(1)} %get-tuple-element.30.sent.sent0), channel_id=1, source_target_pairs={{28,0},{0,4},{4,8},{8,12},{12,16},{16,20},{20,24},{24,28},{29,1},{... | collective-permute-start | bytes 208904 | tf_op jit(solution)/shard_map/ppermute | solution.py:28
  7.4 4.6 %collective-permute-start.2 = (f32[8,256]{1,0:T(8,128)S(1)}, f32[8,256]{1,0:T(8,128)S(1)}, u32[]{:S(2)}, u32[]{:S(2)}) collective-permute-start(f32[8,256]{1,0:T(8,128)S(1)} %get-tuple-element.37.log0), channel_id=1, source_target_pairs={{24,0},{28,4},{0,8},{4,12},{8,16},{12,20},{16,24},{20,28},{25,1},{... | collective-permute-start | bytes 24584 | tf_op jit(solution)/shard_map/ppermute | solution.py:28
  13.8 6.9 %collective-permute-start.4 = (bf16[144,256]{1,0:T(8,128)(2,1)S(1)}, bf16[144,256]{1,0:T(8,128)(2,1)S(1)}, u32[]{:S(2)}, u32[]{:S(2)}) collective-permute-start(bf16[144,256]{1,0:T(8,128)(2,1)S(1)} %get-tuple-element.40), channel_id=1, source_target_pairs={{4,0},{8,4},{12,8},{16,12},{20,16},{24,20},{28,24},{0,28},{5,1},{9... | collective-permute-start | bytes 221192 | tf_op jit(solution)/shard_map/ppermute | solution.py:28
  14.8 5.8 %collective-permute-start.5 = (bf16[144,256]{1,0:T(8,128)(2,1)S(1)}, bf16[144,256]{1,0:T(8,128)(2,1)S(1)}, u32[]{:S(2)}, u32[]{:S(2)}) collective-permute-start(bf16[144,256]{1,0:T(8,128)(2,1)S(1)} %get-tuple-element.41), channel_id=1, source_target_pairs={{8,0},{12,4},{16,8},{20,12},{24,16},{28,20},{0,24},{4,28},{9,1},{1... | collective-permute-start | bytes 221192 | tf_op jit(solution)/shard_map/ppermute | solution.py:28
  15.4 5.3 %collective-permute-start.3 = (f32[8,256]{1,0:T(8,128)S(1)}, f32[8,256]{1,0:T(8,128)S(1)}, u32[]{:S(2)}, u32[]{:S(2)}) collective-permute-start(f32[8,256]{1,0:T(8,128)S(1)} %get-tuple-element.39.logs), channel_id=1, source_target_pairs={{28,0},{0,4},{4,8},{8,12},{12,16},{16,20},{20,24},{24,28},{29,1},{... | collective-permute-start | bytes 24584 | tf_op jit(solution)/shard_map/ppermute | solution.py:28
  38.2 11.6 %all-to-all-start.1 = ((bf16[32,24,128]{2,1,0:T(8,128)(2,1)}), bf16[32,24,128]{2,1,0:T(8,128)(2,1)S(1)}, u32[]{:S(2)}, u32[]{:S(2)}) async-start(bf16[32,24,128]{2,1,0:T(8,128)(2,1)} %shard_map.97), calls=%async_computation.1 | async-start | bytes 393216 | tf_op jit(solution)/shard_map/all_to_all | solution.py:289

commit v5 on v4

--- a/solution.py
+++ b/solution.py
@@ -64,8 +64,7 @@
     return before * inverse, inverse
 
 
-def back_rows(grad, before):
-    unit, inverse = unit_rows(before)
+def back_rows(grad, unit, inverse):
     inner = jnp.sum(unit * grad, axis=1, keepdims=True)
     return ((grad - unit * inner) * inverse).astype(jnp.bfloat16)
 
@@ -80,7 +79,7 @@
 def query_embed_body(
     queries, query_lengths_in, passage_lengths_in, positives_in, query_hidden_in, passage_hidden_in,
     projection_in,
-    before_out, sent_out, slots_out, wanted_out, query_hidden, passage_hidden, projection,
+    unit_out, inverse_out, sent_out, slots_out, wanted_out, query_hidden, passage_hidden, projection,
     query_lengths, passage_lengths, positives, sems,
 ):
     pairs = (
@@ -93,8 +92,10 @@
     copies[1].wait()
     rows = query_hidden.shape[0]
     before = dot32(query_hidden[...], projection[...])
-    before_out[...] = before
-    sent_out[:rows, :] = unit_rows(before)[0].astype(jnp.bfloat16)
+    unit, inverse = unit_rows(before)
+    unit_out[...] = unit
+    inverse_out[...] = jnp.broadcast_to(inverse, unit.shape)
+    sent_out[:rows, :] = unit.astype(jnp.bfloat16)
     copies[2].wait()
     keep = keep_row(query_lengths, queries, rows // queries)
     row = lax.broadcasted_iota(jnp.int32, (ROWS, LANES), 0)
@@ -159,13 +160,16 @@
 
 def own_score_body(
     queries, passages, valid, hidden, projection, sent,
-    before_out, embed_out, powers, totals, scores, log_out, tops,
+    unit_out, inverse_out, embed_out, turned_out, powers, totals, scores, log_out, tops,
 ):
-    before = dot32(hidden[...], projection[...])
-    before_out[...] = before
-    embed_out[...] = unit_rows(before)[0].astype(jnp.bfloat16)
+    unit, inverse = unit_rows(dot32(hidden[...], projection[...]))
+    unit_out[...] = unit
+    inverse_out[...] = jnp.broadcast_to(inverse, unit.shape)
+    embed = unit.astype(jnp.bfloat16)
+    embed_out[...] = embed
     score_block(queries, passages, valid, embed_out, sent, powers, totals, scores, tops)
     log_out[...] = stack_rows(log_out.shape, (log_sum(scores[...]),))
+    turned_out[...] = embed.T
 
 
 def log_sum(scores):
@@ -196,27 +200,36 @@
         )
 
 
-def other_score_body(
-    queries, passages, valid, embed, sent1, sent2, log0, far0,
-    grad_sim, logs, back1, back2, powers1, powers2, totals1, totals2, scores1, scores2, tops,
+def send_back(passages, turned, sent, powers, totals, scores, log, tail, back, grad_sim):
+    dim, rows = turned.shape[0], powers.shape[1]
+    dscore = loss_scale * jnp.exp(scores[...] - log)
+    coefficient = outer_scale * dscore * sent_keep(sent, rows) / totals[...]
+    fill_grad_sim(passages, coefficient, powers, grad_sim, 0)
+    back[:dim, :] = dot32(turned[...], grad_sim[...]).astype(jnp.bfloat16)
+    tail = stack_rows((ROWS, rows), [part.astype(jnp.float32) for part in tail])
+    back[dim:, :] = tail.astype(jnp.bfloat16)
+
+
+def far_score_body(
+    queries, passages, valid, embed, turned, sent,
+    powers, totals, scores, log_out, back, tops, grad_sim,
 ):
-    rows = powers1.shape[1]
-    dim = embed.shape[1]
-    score_block(queries, passages, valid, embed, sent2, powers2, totals2, scores2, tops)
-    score_block(queries, passages, valid, embed, sent1, powers1, totals1, scores1, tops)
-    log1, log2 = log_sum(scores1[...]), log_sum(scores2[...])
-    logs[...] = stack_rows(logs.shape, (log0[0:1, :], log1, log2, far0[0:1, :]))
-    turned = embed[...].T
-    for column, log, sent, powers, totals, scores, back, tail in (
-        (rows, log2, sent2, powers2, totals2, scores2, back2, split(log2)),
-        (0, log1, sent1, powers1, totals1, scores1, back1, split(log1) + split(log2)),
-    ):
-        dscore = loss_scale * jnp.exp(scores[...] - log)
-        coefficient = outer_scale * dscore * sent_keep(sent, rows) / totals[...]
-        fill_grad_sim(passages, coefficient, powers, grad_sim, column)
-        back[:dim, :] = dot32(turned, grad_sim[:, column : column + rows]).astype(jnp.bfloat16)
-        tail = stack_rows((ROWS, rows), [part.astype(jnp.float32) for part in tail])
-        back[dim:, :] = tail.astype(jnp.bfloat16)
+    score_block(queries, passages, valid, embed, sent, powers, totals, scores, tops)
+    log = log_sum(scores[...])
+    log_out[...] = stack_rows(log_out.shape, (log,))
+    send_back(passages, turned, sent, powers, totals, scores, log, split(log), back, grad_sim)
+
+
+def near_score_body(
+    queries, passages, valid, embed, turned, sent, log0, log2, far0,
+    powers, totals, scores, logs, back, tops, grad_sim,
+):
+    score_block(queries, passages, valid, embed, sent, powers, totals, scores, tops)
+    log = log_sum(scores[...])
+    other = log2[0:1, :]
+    logs[...] = stack_rows(logs.shape, (log0[0:1, :], log, other, far0[0:1, :]))
+    tail = split(log) + split(other)
+    send_back(passages, turned, sent, powers, totals, scores, log, tail, back, grad_sim)
 
 
 def joined(back, dim, place):
@@ -226,12 +239,14 @@
 
 
 def grad_body(
-    queries, passages, wanted, query_hidden, passage_hidden, embed, query_before, passage_before,
-    powers, totals, scores0, sent0, sent1, sent2, other_grad_sim, logs, logs1, back1, back2,
-    losses, query_pre_grad, passage_pre_grad, partial, grad_sim,
+    queries, passages, wanted, query_hidden, passage_hidden, turned,
+    query_unit, query_inverse, passage_unit, passage_inverse,
+    powers0, powers1, powers2, totals0, totals1, totals2, scores0, scores1, scores2,
+    sent0, sent1, sent2, logs, logs1, back1, back2,
+    losses, query_pre_grad, passage_pre_grad, partial, grad_sim, query_rows,
 ):
-    rows = powers.shape[1]
-    dim = embed.shape[1]
+    rows = powers0.shape[1]
+    dim = turned.shape[0]
     second, third = joined(back1, dim, 0), joined(back2, dim, 0)
     total0 = log_add((logs[0:1, :], second, third))
     total1 = log_add((logs1[0:1, :], logs[1:2, :], joined(back1, dim, 3)))
@@ -243,26 +258,28 @@
     pick = (pick == lax.broadcasted_iota(jnp.int32, (rows, LANES), 0)).astype(jnp.bfloat16)
     losses[...] = sum(dot32(part, pick) for part in split(loss))[:, :queries]
 
-    shares = (jnp.exp(logs[1:2, :] - total1), jnp.exp(logs[2:3, :] - total2))
-    shares = stack_rows((8, rows), shares).T
-    first = (sent1[:rows, :].astype(jnp.float32) * shares[:, 0:1]).astype(jnp.bfloat16)
-    grad = dot32(other_grad_sim[:, :rows], first)
-    first = (sent2[:rows, :].astype(jnp.float32) * shares[:, 1:2]).astype(jnp.bfloat16)
-    grad += dot32(other_grad_sim[:, rows:], first)
-
-    dscore = loss_scale * (jnp.exp(scores - total0) - onehot.astype(jnp.float32))
-    coefficient = outer_scale * dscore * sent_keep(sent0, rows) / totals[...]
-    fill_grad_sim(passages, coefficient, powers, grad_sim, 0)
-    to_query = dot32(embed[...].T, grad_sim[...])
+    for block, (total, query, powers, totals, scores) in enumerate((
+        (total0, sent0, powers0, totals0, scores0),
+        (total1, sent1, powers1, totals1, scores1),
+        (total2, sent2, powers2, totals2, scores2),
+    )):
+        dscore = jnp.exp(scores[...] - total)
+        if block == 0:
+            dscore = dscore - onehot.astype(jnp.float32)
+        coefficient = (outer_scale * loss_scale) * dscore * sent_keep(query, rows) / totals[...]
+        fill_grad_sim(passages, coefficient, powers, grad_sim, block * rows)
+        query_rows[block * rows : (block + 1) * rows, :] = query[:rows, :]
+
+    grad = dot32(grad_sim[...], query_rows[...])
+    pre = back_rows(grad, passage_unit[...], passage_inverse[...])
+    passage_pre_grad[...] = pre
+    both = dot32(pre.T, passage_hidden[...])
+    to_query = dot32(turned[...], grad_sim[:, :rows])
     to_query += back1[:dim, :].astype(jnp.float32) * jnp.exp(second - total0)
     to_query += back2[:dim, :].astype(jnp.float32) * jnp.exp(third - total0)
-    pre = back_rows(to_query.T, query_before[...])
+    pre = back_rows(to_query.T, query_unit[...], query_inverse[...])
     query_pre_grad[...] = pre
-    both = dot32(pre.T, query_hidden[...])
-    grad += dot32(grad_sim[...], sent0[:rows, :])
-    pre = back_rows(grad, passage_before[...])
-    passage_pre_grad[...] = pre
-    both += dot32(pre.T, passage_hidden[...])
+    both += dot32(pre.T, query_hidden[...])
     partial[...] = both.T.astype(jnp.bfloat16)
 
 
@@ -282,7 +299,7 @@
     pieces = lax.all_to_all(padded.reshape(devices, share, columns), axes, 0, 0)
     means = call(
         functools.partial(sum_body, 1.0 / devices, devices),
-        (pltpu.VMEM(pieces.shape, jnp.bfloat16),),
+        (jax.ShapeDtypeStruct(pieces.shape, jnp.bfloat16),),
         (vmem,),
         (pieces,),
     )[0]
@@ -305,10 +322,11 @@
         query_lengths, passage_lengths, positives, query_hidden, passage_hidden, projection
     )
     taken = tuple(pltpu.with_memory_space_constraint(x, pltpu.HBM) for x in taken)
-    query_before, sent0, valid, wanted, query_rows, passage_rows, weight = call(
+    query_unit, query_inverse, sent0, valid, wanted, query_rows, passage_rows, weight = call(
         functools.partial(query_embed_body, queries),
         (
-            of((rows, dim), f32), of((rows + ROWS, dim), bf16), of((ROWS, rows), jnp.int32),
+            of((rows, dim), f32), of((rows, dim), f32), of((rows + ROWS, dim), bf16),
+            of((ROWS, rows), jnp.int32),
             of((1, rows), jnp.int32), of((rows, width), bf16), of((slots, width), bf16),
             of((width, dim), bf16),
         ),
@@ -324,11 +342,13 @@
     )
     sent1 = shifted(sent0, "batch", 1)
     sent2 = shifted(sent0, "batch", 2)
-    passage_before, embed, powers0, totals0, scores0, log0 = call(
+    (
+        passage_unit, passage_inverse, embed, turned, powers0, totals0, scores0, log0
+    ) = call(
         functools.partial(own_score_body, queries, passages),
         (
-            of((slots, dim), f32), of((slots, dim), bf16), of((slots, rows), f32), pair, pair,
-            of((8, rows), f32),
+            of((slots, dim), f32), of((slots, dim), f32), of((slots, dim), bf16),
+            of((dim, slots), bf16), of((slots, rows), f32), pair, pair, of((8, rows), f32),
         ),
         (vmem,) * 4,
         (valid, passage_rows, weight, sent0),
@@ -337,16 +357,28 @@
         trans=slots * rows,
     )
     far0 = shifted(log0, "batch", 2)
-    other_grad_sim, logs, back1, back2 = call(
-        functools.partial(other_score_body, queries, passages),
-        (of((slots, 2 * rows), bf16), of((8, rows), f32)) + (of((dim + ROWS, rows), bf16),) * 2,
-        (vmem,) * 6,
-        (valid, embed, sent1, sent2, log0, far0),
-        scratch=(pltpu.VMEM((slots, rows), f32),) * 2 + (pairs,) * 5,
-        flops=8 * slots * dim * rows,
-        trans=2 * slots * rows,
+    block_outs = (
+        of((slots, rows), f32), pair, pair, of((8, rows), f32), of((dim + ROWS, rows), bf16)
+    )
+    powers2, totals2, scores2, log2, back2 = call(
+        functools.partial(far_score_body, queries, passages),
+        block_outs,
+        (vmem,) * 4,
+        (valid, embed, turned, sent2),
+        scratch=(pairs, pltpu.VMEM((slots, rows), bf16)),
+        flops=4 * slots * dim * rows,
+        trans=slots * rows,
     )
     back2 = shifted(back2, "batch", -2)
+    powers1, totals1, scores1, logs, back1 = call(
+        functools.partial(near_score_body, queries, passages),
+        block_outs,
+        (vmem,) * 7,
+        (valid, embed, turned, sent1, log0, log2, far0),
+        scratch=(pairs, pltpu.VMEM((slots, rows), bf16)),
+        flops=4 * slots * dim * rows,
+        trans=slots * rows,
+    )
     back1 = shifted(back1, "batch", -1)
     logs1 = shifted(logs, "batch", 1)
     losses, query_pre_grad, passage_pre_grad, partial = call(
@@ -355,10 +387,12 @@
             of((1, queries), f32), of((rows, dim), bf16), of((slots, dim), bf16),
             of((width, dim), bf16),
         ),
-        (vmem,) * 17,
-        (wanted, query_rows, passage_rows, embed, query_before, passage_before,
-         powers0, totals0, scores0, sent0, sent1, sent2, other_grad_sim, logs, logs1, back1, back2),
-        scratch=(pltpu.VMEM((slots, rows), bf16),),
+        (vmem,) * 24,
+        (wanted, query_rows, passage_rows, turned,
+         query_unit, query_inverse, passage_unit, passage_inverse,
+         powers0, powers1, powers2, totals0, totals1, totals2, scores0, scores1, scores2,
+         sent0, sent1, sent2, logs, logs1, back1, back2),
+        scratch=(pltpu.VMEM((slots, 3 * rows), bf16), pltpu.VMEM((3 * rows, dim), bf16)),
         flops=8 * slots * dim * rows + 2 * (slots + rows) * width * dim,
     )
     grad_projection = mean_over_devices(partial)

time: 50.8 us -> 49.1 us (0.967)
  waiting for transfers between devices: 14.9 us -> 11.2 us
  starting transfers between devices: 8.71 us -> 10.7 us
    ppermute x6, waiting for transfers between devices: 8.61 us -> 4.91 us  [shifted(): return lax.ppermute(block, axis, route)]
    ppermute x6, starting transfers between devices: 6.34 us -> 8.28 us  [shifted(): return lax.ppermute(block, axis, route)]
    pallas_call x5 -> x6, Pallas kernels: 8.19 us -> 8.19 us  [call(): pl.pallas_call(body, out_shape=tuple(outs), in_specs=list(in_specs), out_...]
  transfers between devices with their start and end apart: 7 -> 7, of which waited for: 3 -> 3; matrix products, arithmetic and copies ran while one was open for 6% -> 6% of each run, Pallas kernels for 3% -> 8%
where the time goes in v5:
time: 49.1 us; the launch traced here: 48.9 us
  blocking collectives  14.5 us (30%)
  waiting for transfers between devices  11.2 us (23%)
  starting transfers between devices  10.7 us (22%)
  Pallas kernels  8.19 us (17%)
  matrix products  2.95 us (6%)
  other arithmetic  0.78 us (2%)
  between operations  0.69 us (1%)
    all_to_all x1, blocking collectives, mean_over_devices(): pieces = lax.all_to_all(padded.reshape(devices, share, columns), axes, 0, 0)  14.5 us
    ppermute x6, starting transfers between devices, shifted(): return lax.ppermute(block, axis, route)  8.28 us
    pallas_call x6, Pallas kernels, call(): pl.pallas_call(body, out_shape=tuple(outs), in_specs=list(in_specs), out_...  8.19 us
    all_to_all x1, waiting for transfers between devices, mean_over_devices(): whole = lax.all_to_all(means, axes, 0, 0)  6.28 us
    ppermute x6, waiting for transfers between devices, shifted(): return lax.ppermute(block, axis, route)  4.91 us
    dot_general x2, matrix products, dot32(): lax.dot_general(left, right, dims, preferred_element_type=jnp.float32)  2.95 us
    all_to_all x1, starting transfers between devices, mean_over_devices(): whole = lax.all_to_all(means, axes, 0, 0)  2.37 us
  transfers between devices with their start and end apart: 7, of which 3 were waited for; matrix products, arithmetic and copies ran while one was open for 6% of the time, Pallas kernels for 8%

profile of v5, /device:TPU:1, one launch (start us, length us, event | category | flops | bytes accessed | tf_op | source)
XLA Modules:
  0.0 48.9 jit_solution(18340250095833894035)
XLA Ops:
  0.6 1.8 %shard_map.93 = (f32[256,128]{1,0:T(8,128)S(1)}, f32[256,128]{1,0:T(8,128)S(1)}, bf16[272,128]{1,0:T(8,128)(2,1)S(1)}, s32[16,256]{1,0:T(8,128)S(1)}, s32[1,256]...) custom-call(s32[8]{0:T(128)} %query_lengths_in.1, ...), custom_call_target="tpu_custom_call" | custom-call | flops 50331648 | bytes 5461096 | tf_op jit(solution)/shard_map/pallas_call | solution.py:38
  2.5 2.2 %collective-permute-start.1 = (bf16[272,128]{1,0:T(8,128)(2,1)S(1)}, bf16[272,128]{1,0:T(8,128)(2,1)S(1)}, u32[]{:S(2)}, u32[]{:S(2)}) collective-permute-start(bf16[272,128]{1,0:T(8,128)(2,1)S(1)} %get-tuple-element.39.sent.sent0), channel_id=1, source_target_pairs={{24,0},{28,4},{0,8},{4,12},{8,16},{12,20},{16,24},{20,28},{25,1},{... | collective-permute-start | bytes 208904 | tf_op jit(solution)/shard_map/ppermute | solution.py:28
  4.7 1.2 %collective-permute-start = (bf16[272,128]{1,0:T(8,128)(2,1)S(1)}, bf16[272,128]{1,0:T(8,128)(2,1)S(1)}, u32[]{:S(2)}, u32[]{:S(2)}) collective-permute-start(bf16[272,128]{1,0:T(8,128)(2,1)S(1)} %get-tuple-element.39.sent.sent0), channel_id=1, source_target_pairs={{28,0},{0,4},{4,8},{8,12},{12,16},{16,20},{20,24},{24,28},{29,1},{... | collective-permute-start | bytes 208904 | tf_op jit(solution)/shard_map/ppermute | solution.py:28
  5.9 1.5 %shard_map.94 = (f32[1280,128]{1,0:T(8,128)S(1)}, f32[1280,128]{1,0:T(8,128)S(1)}, bf16[1280,128]{1,0:T(8,128)(2,1)S(1)}, bf16[128,1280]{1,0:T(8,128)(2,1)S(1)},...) custom-call(s32[16,256]{1,0:T(8,128)S(1)} %get-tuple-element.37.valid, ...), custom_call_target="tpu_custom_call" | custom-call | flops 335544320 | bytes 5566464 | tf_op jit(solution)/shard_map/pallas_call | solution.py:38
  7.4 1.3 %collective-permute-start.2 = (f32[8,256]{1,0:T(8,128)S(1)}, f32[8,256]{1,0:T(8,128)S(1)}, u32[]{:S(2)}, u32[]{:S(2)}) collective-permute-start(f32[8,256]{1,0:T(8,128)S(1)} %get-tuple-element.47.log0), channel_id=1, source_target_pairs={{24,0},{28,4},{0,8},{4,12},{8,16},{12,20},{16,24},{20,28},{25,1},{... | collective-permute-start | bytes 24584 | tf_op jit(solution)/shard_map/ppermute | solution.py:28
  8.8 0.0 collective-permute-done.1.sent.sent2
  8.8 1.1 %shard_map.95 = (f32[1280,256]{1,0:T(8,128)S(1)}, f32[16,256]{1,0:T(8,128)S(1)}, f32[16,256]{1,0:T(8,128)S(1)}, f32[8,256]{1,0:T(8,128)S(1)}, bf16[144,256]{1,0:T(8,128)(2,1)S(1)}) custom-call(s32[16,256]{1,0:T(8,128)S(1)} %get-tuple-element.37.valid, bf16[1280,128]{1,0:T(8,128)(2,1)S(1)} %get-tuple-element.46.embed, ...), custom_call_target="tpu_custom_call" | custom-call | flops 167772160 | bytes 2166784 | tf_op jit(solution)/shard_map/pallas_call | solution.py:38
  9.9 2.0 %collective-permute-start.5 = (bf16[144,256]{1,0:T(8,128)(2,1)S(1)}, bf16[144,256]{1,0:T(8,128)(2,1)S(1)}, u32[]{:S(2)}, u32[]{:S(2)}) collective-permute-start(bf16[144,256]{1,0:T(8,128)(2,1)S(1)} %get-tuple-element.59), channel_id=1, source_target_pairs={{8,0},{12,4},{16,8},{20,12},{24,16},{28,20},{0,24},{4,28},{9,1},{1... | collective-permute-start | bytes 221192 | tf_op jit(solution)/shard_map/ppermute | solution.py:28
  11.9 0.2 collective-permute-done.2.far0
  12.1 0.0 collective-permute-done.sent.sent1
  12.1 1.1 %shard_map.96 = (f32[1280,256]{1,0:T(8,128)S(1)}, f32[16,256]{1,0:T(8,128)S(1)}, f32[16,256]{1,0:T(8,128)S(1)}, f32[8,256]{1,0:T(8,128)S(1)}, bf16[144,256]{1,0:T(8,128)(2,1)S(1)}) custom-call(s32[16,256]{1,0:T(8,128)S(1)} %get-tuple-element.37.valid, bf16[1280,128]{1,0:T(8,128)(2,1)S(1)} %get-tuple-element.46.embed, ...), custom_call_target="tpu_custom_call" | custom-call | flops 167772160 | bytes 2191360 | tf_op jit(solution)/shard_map/pallas_call | solution.py:38
  13.2 1.1 %collective-permute-start.4 = (bf16[144,256]{1,0:T(8,128)(2,1)S(1)}, bf16[144,256]{1,0:T(8,128)(2,1)S(1)}, u32[]{:S(2)}, u32[]{:S(2)}) collective-permute-start(bf16[144,256]{1,0:T(8,128)(2,1)S(1)} %get-tuple-element.58), channel_id=1, source_target_pairs={{4,0},{8,4},{12,8},{16,12},{20,16},{24,20},{28,24},{0,28},{5,1},{9... | collective-permute-start | bytes 221192 | tf_op jit(solution)/shard_map/ppermute | solution.py:28
  14.2 0.5 collective-permute-start.3
  14.7 4.7 %collective-permute-done.3.logs1 = f32[8,256]{1,0:T(8,128)S(1)} collective-permute-done((f32[8,256]{1,0:T(8,128)S(1)}, f32[8,256]{1,0:T(8,128)S(1)}, u32[]{:S(2)}, u32[]{:S(2)}) %collective-permute-start.3) | collective-permute-done | bytes 8224 | tf_op jit(solution)/shard_map/ppermute | solution.py:28
  19.4 0.0 collective-permute-done.5.back2
  19.4 0.0 collective-permute-done.4.back1
  19.4 1.9 %shard_map.97 = (f32[1,8]{1,0:T(1,128)}, bf16[256,128]{1,0:T(8,128)(2,1)S(1)}, bf16[1280,128]{1,0:T(8,128)(2,1)S(1)}, bf16[768,128]{1,0:T(8,128)(2,1)S(1)}) custom-call(s32[1,256]{1,0:T(1,128)S(1)} %get-tuple-element.34.wanted, bf16[256,768]{1,0:T(8,128)(2,1)S(1)} %get-tuple-element.35.query_hidden, ...), custom_call_target="tpu_custom_call" | custom-call | flops 637534208 | bytes 9253920 | tf_op jit(solution)/shard_map/pallas_call | solution.py:38
  21.3 14.5 %all_to_all.10.pieces = bf16[32,24,128]{2,1,0:T(8,128)(2,1)S(1)} all-to-all(bf16[32,24,128]{2,1,0:T(8,128)(2,1)S(1)} %bitcast.9), channel_id=1, replica_groups=mesh['batch'=8,'mp'=4] {'batch','mp'}, dimensions={0} | all-to-all | bytes 393216 | tf_op jit(solution)/shard_map/all_to_all | solution.py:299
  35.8 0.7 %shard_map.98 = bf16[32,24,128]{2,1,0:T(8,128)(2,1)} custom-call(bf16[32,24,128]{2,1,0:T(8,128)(2,1)S(1)} %all_to_all.10.pieces), custom_call_target="tpu_custom_call" | custom-call | bytes 393216 | tf_op jit(solution)/shard_map/pallas_call | solution.py:38
  36.5 2.4 %all-to-all-start.1 = ((bf16[32,24,128]{2,1,0:T(8,128)(2,1)}), bf16[32,24,128]{2,1,0:T(8,128)(2,1)S(1)}, u32[]{:S(2)}, u32[]{:S(2)}) async-start(bf16[32,24,128]{2,1,0:T(8,128)(2,1)} %shard_map.98), calls=%async_computation.1 | async-start | bytes 393216 | tf_op jit(solution)/shard_map/all_to_all | solution.py:306
  38.9 1.0 %convolution_convert_fusion.1 = bf16[256,768]{1,0:T(8,128)(2,1)} fusion(bf16[256,128]{1,0:T(8,128)(2,1)S(1)} %get-tuple-element.61, bf16[768,128]{1,0:T(8,128)(2,1)S(1)} %get-tuple-element.38.projection), kind=kOutput, calls=%fused_computation.1 | convolution fusion | flops 50528256 | bytes 655360 | tf_op jit(solution)/shard_map/dot_general | solution.py:32
  39.9 1.9 %convolution_convert_fusion = bf16[1280,768]{1,0:T(8,128)(2,1)} fusion(bf16[1280,128]{1,0:T(8,128)(2,1)S(1)} %get-tuple-element.62, bf16[768,128]{1,0:T(8,128)(2,1)S(1)} %get-tuple-element.38.projection), kind=kOutput, calls=%fused_computation | convolution fusion | flops 252641280 | bytes 2490368 | tf_op jit(solution)/shard_map/dot_general | solution.py:32
  41.8 6.3 %all-to-all-done.1 = bf16[32,24,128]{2,1,0:T(8,128)(2,1)S(1)} async-done(((bf16[32,24,128]{2,1,0:T(8,128)(2,1)}), bf16[32,24,128]{2,1,0:T(8,128)(2,1)S(1)}, u32[]{:S(2)}, u32[]{:S(2)}) %all-to-all-start.1) | async-done | bytes 196640 | tf_op jit(solution)/shard_map/all_to_all | solution.py:306
  48.1 0.8 %bitcast_convert_fusion = f32[768,128]{1,0:T(8,128)} fusion(bf16[32,24,128]{2,1,0:T(8,128)(2,1)S(1)} %all-to-all-done.1), kind=kLoop, calls=%fused_computation.2 | loop fusion | flops 98304 | bytes 589824 | tf_op jit(solution)/shard_map/convert_element_type | solution.py:307
Async XLA Ops:
  2.5 6.3 %collective-permute-start.1 = (bf16[272,128]{1,0:T(8,128)(2,1)S(1)}, bf16[272,128]{1,0:T(8,128)(2,1)S(1)}, u32[]{:S(2)}, u32[]{:S(2)}) collective-permute-start(bf16[272,128]{1,0:T(8,128)(2,1)S(1)} %get-tuple-element.39.sent.sent0), channel_id=1, source_target_pairs={{24,0},{28,4},{0,8},{4,12},{8,16},{12,20},{16,24},{20,28},{25,1},{... | collective-permute-start | bytes 208904 | tf_op jit(solution)/shard_map/ppermute | solution.py:28
  4.7 7.4 %collective-permute-start = (bf16[272,128]{1,0:T(8,128)(2,1)S(1)}, bf16[272,128]{1,0:T(8,128)(2,1)S(1)}, u32[]{:S(2)}, u32[]{:S(2)}) collective-permute-start(bf16[272,128]{1,0:T(8,128)(2,1)S(1)} %get-tuple-element.39.sent.sent0), channel_id=1, source_target_pairs={{28,0},{0,4},{4,8},{8,12},{12,16},{16,20},{20,24},{24,28},{29,1},{... | collective-permute-start | bytes 208904 | tf_op jit(solution)/shard_map/ppermute | solution.py:28
  7.4 4.6 %collective-permute-start.2 = (f32[8,256]{1,0:T(8,128)S(1)}, f32[8,256]{1,0:T(8,128)S(1)}, u32[]{:S(2)}, u32[]{:S(2)}) collective-permute-start(f32[8,256]{1,0:T(8,128)S(1)} %get-tuple-element.47.log0), channel_id=1, source_target_pairs={{24,0},{28,4},{0,8},{4,12},{8,16},{12,20},{16,24},{20,28},{25,1},{... | collective-permute-start | bytes 24584 | tf_op jit(solution)/shard_map/ppermute | solution.py:28
  9.9 9.6 %collective-permute-start.5 = (bf16[144,256]{1,0:T(8,128)(2,1)S(1)}, bf16[144,256]{1,0:T(8,128)(2,1)S(1)}, u32[]{:S(2)}, u32[]{:S(2)}) collective-permute-start(bf16[144,256]{1,0:T(8,128)(2,1)S(1)} %get-tuple-element.59), channel_id=1, source_target_pairs={{8,0},{12,4},{16,8},{20,12},{24,16},{28,20},{0,24},{4,28},{9,1},{1... | collective-permute-start | bytes 221192 | tf_op jit(solution)/shard_map/ppermute | solution.py:28
  13.2 6.3 %collective-permute-start.4 = (bf16[144,256]{1,0:T(8,128)(2,1)S(1)}, bf16[144,256]{1,0:T(8,128)(2,1)S(1)}, u32[]{:S(2)}, u32[]{:S(2)}) collective-permute-start(bf16[144,256]{1,0:T(8,128)(2,1)S(1)} %get-tuple-element.58), channel_id=1, source_target_pairs={{4,0},{8,4},{12,8},{16,12},{20,16},{24,20},{28,24},{0,28},{5,1},{9... | collective-permute-start | bytes 221192 | tf_op jit(solution)/shard_map/ppermute | solution.py:28
  14.2 5.2 %collective-permute-start.3 = (f32[8,256]{1,0:T(8,128)S(1)}, f32[8,256]{1,0:T(8,128)S(1)}, u32[]{:S(2)}, u32[]{:S(2)}) collective-permute-start(f32[8,256]{1,0:T(8,128)S(1)} %get-tuple-element.57.logs), channel_id=1, source_target_pairs={{28,0},{0,4},{4,8},{8,12},{12,16},{16,20},{20,24},{24,28},{29,1},{... | collective-permute-start | bytes 24584 | tf_op jit(solution)/shard_map/ppermute | solution.py:28
  36.5 11.6 %all-to-all-start.1 = ((bf16[32,24,128]{2,1,0:T(8,128)(2,1)}), bf16[32,24,128]{2,1,0:T(8,128)(2,1)S(1)}, u32[]{:S(2)}, u32[]{:S(2)}) async-start(bf16[32,24,128]{2,1,0:T(8,128)(2,1)} %shard_map.98), calls=%async_computation.1 | async-start | bytes 393216 | tf_op jit(solution)/shard_map/all_to_all | solution.py:306

commit v6 on v5

--- a/solution.py
+++ b/solution.py
@@ -200,14 +200,12 @@
         )
 
 
-def send_back(passages, turned, sent, powers, totals, scores, log, tail, back, grad_sim):
-    dim, rows = turned.shape[0], powers.shape[1]
+def query_gradient(passages, turned, sent, powers, totals, scores, log, grad_sim):
+    rows = powers.shape[1]
     dscore = loss_scale * jnp.exp(scores[...] - log)
     coefficient = outer_scale * dscore * sent_keep(sent, rows) / totals[...]
     fill_grad_sim(passages, coefficient, powers, grad_sim, 0)
-    back[:dim, :] = dot32(turned[...], grad_sim[...]).astype(jnp.bfloat16)
-    tail = stack_rows((ROWS, rows), [part.astype(jnp.float32) for part in tail])
-    back[dim:, :] = tail.astype(jnp.bfloat16)
+    return dot32(turned[...], grad_sim[...]).astype(jnp.bfloat16)
 
 
 def far_score_body(
@@ -217,40 +215,43 @@
     score_block(queries, passages, valid, embed, sent, powers, totals, scores, tops)
     log = log_sum(scores[...])
     log_out[...] = stack_rows(log_out.shape, (log,))
-    send_back(passages, turned, sent, powers, totals, scores, log, split(log), back, grad_sim)
+    dim, rows = turned.shape[0], powers.shape[1]
+    back[:dim, :] = query_gradient(passages, turned, sent, powers, totals, scores, log, grad_sim)
+    tail = stack_rows((ROWS, rows), [part.astype(jnp.float32) for part in split(log)])
+    back[dim:, :] = tail.astype(jnp.bfloat16)
 
 
 def near_score_body(
-    queries, passages, valid, embed, turned, sent, log0, log2, far0,
-    powers, totals, scores, logs, back, tops, grad_sim,
+    queries, passages, valid, embed, sent, log0, log2, powers, totals, scores, logs, tops
 ):
     score_block(queries, passages, valid, embed, sent, powers, totals, scores, tops)
     log = log_sum(scores[...])
-    other = log2[0:1, :]
-    logs[...] = stack_rows(logs.shape, (log0[0:1, :], log, other, far0[0:1, :]))
-    tail = split(log) + split(other)
-    send_back(passages, turned, sent, powers, totals, scores, log, tail, back, grad_sim)
-
-
-def joined(back, dim, place):
+    logs[...] = stack_rows(logs.shape, (log0[0:1, :], log, log2[0:1, :]))
+
+
+def near_grad_body(passages, turned, sent, powers, totals, scores, logs, back, grad_sim):
+    back[...] = query_gradient(
+        passages, turned, sent, powers, totals, scores, logs[1:2, :], grad_sim
+    )
+
+
+def joined(back, dim):
     tail = back[dim:, :].astype(jnp.float32)
-    high, middle, low = [tail[i : i + 1, :] for i in range(place, place + 3)]
-    return high + (middle + low)
-
-
-def grad_body(
-    queries, passages, wanted, query_hidden, passage_hidden, turned,
-    query_unit, query_inverse, passage_unit, passage_inverse,
+    return tail[0:1, :] + (tail[1:2, :] + tail[2:3, :])
+
+
+def passage_grad_body(
+    queries, passages, wanted, hidden, turned, unit, inverse,
     powers0, powers1, powers2, totals0, totals1, totals2, scores0, scores1, scores2,
-    sent0, sent1, sent2, logs, logs1, back1, back2,
-    losses, query_pre_grad, passage_pre_grad, partial, grad_sim, query_rows,
+    sent0, sent1, sent2, logs, below, far_below, above, back2,
+    losses, pre_grad, partial, to_query, shares, grad_sim, query_rows,
 ):
     rows = powers0.shape[1]
-    dim = turned.shape[0]
-    second, third = joined(back1, dim, 0), joined(back2, dim, 0)
+    second, third = above[1:2, :], joined(back2, turned.shape[0])
     total0 = log_add((logs[0:1, :], second, third))
-    total1 = log_add((logs1[0:1, :], logs[1:2, :], joined(back1, dim, 3)))
-    total2 = log_add((logs[3:4, :], logs1[1:2, :], logs[2:3, :]))
+    total1 = log_add((below[0:1, :], logs[1:2, :], above[2:3, :]))
+    total2 = log_add((far_below[0:1, :], below[1:2, :], logs[2:3, :]))
+    shares[...] = stack_rows(shares.shape, (jnp.exp(second - total0), jnp.exp(third - total0)))
     scores = scores0[...]
     onehot = lax.broadcasted_iota(jnp.int32, scores.shape, 0) == wanted[...]
     loss = total0 - jnp.sum(jnp.where(onehot, scores, 0.0), axis=0, keepdims=True)
@@ -270,16 +271,22 @@
         fill_grad_sim(passages, coefficient, powers, grad_sim, block * rows)
         query_rows[block * rows : (block + 1) * rows, :] = query[:rows, :]
 
+    to_query[...] = dot32(turned[...], grad_sim[:, :rows])
     grad = dot32(grad_sim[...], query_rows[...])
-    pre = back_rows(grad, passage_unit[...], passage_inverse[...])
-    passage_pre_grad[...] = pre
-    both = dot32(pre.T, passage_hidden[...])
-    to_query = dot32(turned[...], grad_sim[:, :rows])
-    to_query += back1[:dim, :].astype(jnp.float32) * jnp.exp(second - total0)
-    to_query += back2[:dim, :].astype(jnp.float32) * jnp.exp(third - total0)
-    pre = back_rows(to_query.T, query_unit[...], query_inverse[...])
-    query_pre_grad[...] = pre
-    both += dot32(pre.T, query_hidden[...])
+    pre = back_rows(grad, unit[...], inverse[...])
+    pre_grad[...] = pre
+    partial[...] = dot32(pre.T, hidden[...])
+
+
+def query_grad_body(
+    hidden, unit, inverse, own, shares, back1, back2, passage_partial, pre_grad, partial
+):
+    dim = own.shape[0]
+    total = own[...] + back1[...].astype(jnp.float32) * shares[0:1, :]
+    total += back2[:dim, :].astype(jnp.float32) * shares[1:2, :]
+    pre = back_rows(total.T, unit[...], inverse[...])
+    pre_grad[...] = pre
+    both = passage_partial[...] + dot32(pre.T, hidden[...])
     partial[...] = both.T.astype(jnp.bfloat16)
 
 
@@ -356,44 +363,58 @@
         flops=2 * slots * dim * (width + rows),
         trans=slots * rows,
     )
-    far0 = shifted(log0, "batch", 2)
-    block_outs = (
-        of((slots, rows), f32), pair, pair, of((8, rows), f32), of((dim + ROWS, rows), bf16)
-    )
+    block_outs = (of((slots, rows), f32), pair, pair, of((8, rows), f32))
+    matrix = pltpu.VMEM((slots, rows), bf16)
     powers2, totals2, scores2, log2, back2 = call(
         functools.partial(far_score_body, queries, passages),
-        block_outs,
+        block_outs + (of((dim + ROWS, rows), bf16),),
         (vmem,) * 4,
         (valid, embed, turned, sent2),
-        scratch=(pairs, pltpu.VMEM((slots, rows), bf16)),
+        scratch=(pairs, matrix),
         flops=4 * slots * dim * rows,
         trans=slots * rows,
     )
     back2 = shifted(back2, "batch", -2)
-    powers1, totals1, scores1, logs, back1 = call(
+    powers1, totals1, scores1, logs = call(
         functools.partial(near_score_body, queries, passages),
         block_outs,
-        (vmem,) * 7,
-        (valid, embed, turned, sent1, log0, log2, far0),
-        scratch=(pairs, pltpu.VMEM((slots, rows), bf16)),
-        flops=4 * slots * dim * rows,
+        (vmem,) * 5,
+        (valid, embed, sent1, log0, log2),
+        scratch=(pairs,),
+        flops=2 * slots * dim * rows,
         trans=slots * rows,
     )
+    below = shifted(logs, "batch", 1)
+    far_below = shifted(logs, "batch", 2)
+    above = shifted(logs, "batch", -1)
+    back1 = call(
+        functools.partial(near_grad_body, passages),
+        (of((dim, rows), bf16),),
+        (vmem,) * 6,
+        (turned, sent1, powers1, totals1, scores1, logs),
+        scratch=(matrix,),
+        flops=2 * slots * dim * rows,
+    )[0]
     back1 = shifted(back1, "batch", -1)
-    logs1 = shifted(logs, "batch", 1)
-    losses, query_pre_grad, passage_pre_grad, partial = call(
-        functools.partial(grad_body, queries, passages),
+    losses, passage_pre_grad, passage_partial, to_query, shares = call(
+        functools.partial(passage_grad_body, queries, passages),
         (
-            of((1, queries), f32), of((rows, dim), bf16), of((slots, dim), bf16),
-            of((width, dim), bf16),
+            of((1, queries), f32), of((slots, dim), bf16), of((dim, width), f32),
+            of((dim, rows), f32), of((8, rows), f32),
         ),
-        (vmem,) * 24,
-        (wanted, query_rows, passage_rows, turned,
-         query_unit, query_inverse, passage_unit, passage_inverse,
+        (vmem,) * 22,
+        (wanted, passage_rows, turned, passage_unit, passage_inverse,
          powers0, powers1, powers2, totals0, totals1, totals2, scores0, scores1, scores2,
-         sent0, sent1, sent2, logs, logs1, back1, back2),
+         sent0, sent1, sent2, logs, below, far_below, above, back2),
         scratch=(pltpu.VMEM((slots, 3 * rows), bf16), pltpu.VMEM((3 * rows, dim), bf16)),
-        flops=8 * slots * dim * rows + 2 * (slots + rows) * width * dim,
+        flops=20 * (8 * slots * dim * rows + 2 * slots * width * dim),
+    )
+    query_pre_grad, partial = call(
+        query_grad_body,
+        (of((rows, dim), bf16), of((width, dim), bf16)),
+        (vmem,) * 8,
+        (query_rows, query_unit, query_inverse, to_query, shares, back1, back2, passage_partial),
+        flops=2 * rows * width * dim,
     )
     grad_projection = mean_over_devices(partial)
     grad_query_hidden = dot32(query_pre_grad, weight, NT).astype(bf16)

time: 49.1 us -> 53.2 us (1.084)
  blocking collectives: 14.5 us -> 17.8 us
  waiting for transfers between devices: 11.2 us -> 8.07 us
  starting transfers between devices: 10.7 us -> 13.8 us
  Pallas kernels: 8.19 us -> 8.84 us
    all_to_all x1, blocking collectives: 14.5 us -> 17.8 us  [mean_over_devices(): pieces = lax.all_to_all(padded.reshape(devices, share, columns), axes, 0, 0)]
    ppermute x6 -> x7, starting transfers between devices: 8.28 us -> 11.5 us  [shifted(): return lax.ppermute(block, axis, route)]
    ppermute x6 -> x7, waiting for transfers between devices: 4.91 us -> 1.8 us  [shifted(): return lax.ppermute(block, axis, route)]
    pallas_call x6 -> x8, Pallas kernels: 8.19 us -> 8.84 us  [call(): pl.pallas_call(body, out_shape=tuple(outs), in_specs=list(in_specs), out_...]
  transfers between devices with their start and end apart: 7 -> 8, of which waited for: 3 -> 4; matrix products, arithmetic and copies ran while one was open for 6% -> 6% of each run, Pallas kernels for 8% -> 11%
where the time goes in v6:
time: 53.2 us; the launch traced here: 53 us
  blocking collectives  17.8 us (33%)
  starting transfers between devices  13.8 us (26%)
  Pallas kernels  8.84 us (17%)
  waiting for transfers between devices  8.07 us (15%)
  matrix products  2.96 us (6%)
  other arithmetic  0.78 us (1%)
  between operations  0.69 us (1%)
    all_to_all x1, blocking collectives, mean_over_devices(): pieces = lax.all_to_all(padded.reshape(devices, share, columns), axes, 0, 0)  17.8 us
    ppermute x7, starting transfers between devices, shifted(): return lax.ppermute(block, axis, route)  11.5 us
    pallas_call x8, Pallas kernels, call(): pl.pallas_call(body, out_shape=tuple(outs), in_specs=list(in_specs), out_...  8.84 us
    all_to_all x1, waiting for transfers between devices, mean_over_devices(): whole = lax.all_to_all(means, axes, 0, 0)  6.27 us
    dot_general x2, matrix products, dot32(): lax.dot_general(left, right, dims, preferred_element_type=jnp.float32)  2.96 us
    all_to_all x1, starting transfers between devices, mean_over_devices(): whole = lax.all_to_all(means, axes, 0, 0)  2.37 us
    ppermute x7, waiting for transfers between devices, shifted(): return lax.ppermute(block, axis, route)  1.8 us
  transfers between devices with their start and end apart: 8, of which 4 were waited for; matrix products, arithmetic and copies ran while one was open for 6% of the time, Pallas kernels for 11%

profile of v6, /device:TPU:1, one launch (start us, length us, event | category | flops | bytes accessed | tf_op | source)
XLA Modules:
  0.0 53.0 jit_solution(7021461985023736539)
XLA Ops:
  0.6 1.8 %shard_map.93 = (f32[256,128]{1,0:T(8,128)S(1)}, f32[256,128]{1,0:T(8,128)S(1)}, bf16[272,128]{1,0:T(8,128)(2,1)S(1)}, s32[16,256]{1,0:T(8,128)S(1)}, s32[1,256]...) custom-call(s32[8]{0:T(128)} %query_lengths_in.1, ...), custom_call_target="tpu_custom_call" | custom-call | flops 50331648 | bytes 5461096 | tf_op jit(solution)/shard_map/pallas_call | solution.py:38
  2.5 2.2 %collective-permute-start.1 = (bf16[272,128]{1,0:T(8,128)(2,1)S(1)}, bf16[272,128]{1,0:T(8,128)(2,1)S(1)}, u32[]{:S(2)}, u32[]{:S(2)}) collective-permute-start(bf16[272,128]{1,0:T(8,128)(2,1)S(1)} %get-tuple-element.40.sent.sent0), channel_id=1, source_target_pairs={{24,0},{28,4},{0,8},{4,12},{8,16},{12,20},{16,24},{20,28},{25,1},{... | collective-permute-start | bytes 208904 | tf_op jit(solution)/shard_map/ppermute | solution.py:28
  4.7 1.2 %collective-permute-start = (bf16[272,128]{1,0:T(8,128)(2,1)S(1)}, bf16[272,128]{1,0:T(8,128)(2,1)S(1)}, u32[]{:S(2)}, u32[]{:S(2)}) collective-permute-start(bf16[272,128]{1,0:T(8,128)(2,1)S(1)} %get-tuple-element.40.sent.sent0), channel_id=1, source_target_pairs={{28,0},{0,4},{4,8},{8,12},{12,16},{16,20},{20,24},{24,28},{29,1},{... | collective-permute-start | bytes 208904 | tf_op jit(solution)/shard_map/ppermute | solution.py:28
  5.9 1.5 %shard_map.94 = (f32[1280,128]{1,0:T(8,128)S(1)}, f32[1280,128]{1,0:T(8,128)S(1)}, bf16[1280,128]{1,0:T(8,128)(2,1)S(1)}, bf16[128,1280]{1,0:T(8,128)(2,1)S(1)},...) custom-call(s32[16,256]{1,0:T(8,128)S(1)} %get-tuple-element.38.valid, ...), custom_call_target="tpu_custom_call" | custom-call | flops 335544320 | bytes 5566464 | tf_op jit(solution)/shard_map/pallas_call | solution.py:38
  7.4 1.0 %collective-permute-done.1.sent.sent2 = bf16[272,128]{1,0:T(8,128)(2,1)S(1)} collective-permute-done((bf16[272,128]{1,0:T(8,128)(2,1)S(1)}, bf16[272,128]{1,0:T(8,128)(2,1)S(1)}, u32[]{:S(2)}, u32[]{:S(2)}) %collective-permute-start.1) | collective-permute-done | bytes 69664 | tf_op jit(solution)/shard_map/ppermute | solution.py:28
  8.4 1.1 %shard_map.95 = (f32[1280,256]{1,0:T(8,128)S(1)}, f32[16,256]{1,0:T(8,128)S(1)}, f32[16,256]{1,0:T(8,128)S(1)}, f32[8,256]{1,0:T(8,128)S(1)}, bf16[144,256]{1,0:T(8,128)(2,1)S(1)}) custom-call(s32[16,256]{1,0:T(8,128)S(1)} %get-tuple-element.38.valid, bf16[1280,128]{1,0:T(8,128)(2,1)S(1)} %get-tuple-element.45.embed, ...), custom_call_target="tpu_custom_call" | custom-call | flops 167772160 | bytes 2166784 | tf_op jit(solution)/shard_map/pallas_call | solution.py:38
  9.5 1.5 %collective-permute-start.5 = (bf16[144,256]{1,0:T(8,128)(2,1)S(1)}, bf16[144,256]{1,0:T(8,128)(2,1)S(1)}, u32[]{:S(2)}, u32[]{:S(2)}) collective-permute-start(bf16[144,256]{1,0:T(8,128)(2,1)S(1)} %get-tuple-element.57), channel_id=1, source_target_pairs={{8,0},{12,4},{16,8},{20,12},{24,16},{28,20},{0,24},{4,28},{9,1},{1... | collective-permute-start | bytes 221192 | tf_op jit(solution)/shard_map/ppermute | solution.py:28
  11.0 0.1 collective-permute-done.sent.sent1
  11.1 0.8 %shard_map.96 = (f32[1280,256]{1,0:T(8,128)S(1)}, f32[16,256]{1,0:T(8,128)S(1)}, f32[16,256]{1,0:T(8,128)S(1)}, f32[8,256]{1,0:T(8,128)S(1)}) custom-call(s32[16,256]{1,0:T(8,128)S(1)} %get-tuple-element.38.valid, bf16[1280,128]{1,0:T(8,128)(2,1)S(1)} %get-tuple-element.45.embed, bf16[272,128]{1,0:T(8,128)(2,1)S(1)} %collective-permute-done.sent.sent1, ...), custom_call_target="tpu_custom_call" | custom-call | flops 83886080 | bytes 1781760 | tf_op jit(solution)/shard_map/pallas_call | solution.py:38
  11.9 1.0 %collective-permute-start.4 = (f32[8,256]{1,0:T(8,128)S(1)}, f32[8,256]{1,0:T(8,128)S(1)}, u32[]{:S(2)}, u32[]{:S(2)}) collective-permute-start(f32[8,256]{1,0:T(8,128)S(1)} %get-tuple-element.56.logs), channel_id=1, source_target_pairs={{4,0},{8,4},{12,8},{16,12},{20,16},{24,20},{28,24},{0,28},{5,1},{9... | collective-permute-start | bytes 24584 | tf_op jit(solution)/shard_map/ppermute | solution.py:28
  12.9 1.3 %collective-permute-start.3 = (f32[8,256]{1,0:T(8,128)S(1)}, f32[8,256]{1,0:T(8,128)S(1)}, u32[]{:S(2)}, u32[]{:S(2)}) collective-permute-start(f32[8,256]{1,0:T(8,128)S(1)} %get-tuple-element.56.logs), channel_id=1, source_target_pairs={{24,0},{28,4},{0,8},{4,12},{8,16},{12,20},{16,24},{20,28},{25,1},{... | collective-permute-start | bytes 24584 | tf_op jit(solution)/shard_map/ppermute | solution.py:28
  14.2 0.0 collective-permute-start.2
  14.2 0.3 shard_map.98
  14.5 4.2 %collective-permute-start.6 = (bf16[128,256]{1,0:T(8,128)(2,1)S(1)}, bf16[128,256]{1,0:T(8,128)(2,1)S(1)}, u32[]{:S(2)}, u32[]{:S(2)}) collective-permute-start(bf16[128,256]{1,0:T(8,128)(2,1)S(1)} %shard_map.98), channel_id=1, source_target_pairs={{4,0},{8,4},{12,8},{16,12},{20,16},{24,20},{28,24},{0,28},{5,1},{9... | collective-permute-start | bytes 196616 | tf_op jit(solution)/shard_map/ppermute | solution.py:28
  18.7 0.0 collective-permute-done.4.above
  18.7 0.0 collective-permute-done.3.far_below
  18.7 0.7 %collective-permute-done.2.below = f32[8,256]{1,0:T(8,128)S(1)} collective-permute-done((f32[8,256]{1,0:T(8,128)S(1)}, f32[8,256]{1,0:T(8,128)S(1)}, u32[]{:S(2)}, u32[]{:S(2)}) %collective-permute-start.2) | collective-permute-done | bytes 8224 | tf_op jit(solution)/shard_map/ppermute | solution.py:28
  19.4 0.0 collective-permute-done.5.back2
  19.4 2.1 %shard_map.97 = (f32[1,8]{1,0:T(1,128)}, bf16[1280,128]{1,0:T(8,128)(2,1)S(1)}, f32[128,768]{1,0:T(8,128)S(1)}, f32[128,256]{1,0:T(8,128)S(1)}, f32[8,256]{1,0:T(8,128)S(1)}) custom-call(s32[1,256]{1,0:T(1,128)S(1)} %get-tuple-element.36.wanted, bf16[1280,768]{1,0:T(8,128)(2,1)S(1)} %get-tuple-element.37.hidden, ...), custom_call_target="tpu_custom_call" | custom-call | flops 11744051200 | bytes 8811552 | tf_op jit(solution)/shard_map/pallas_call | solution.py:38
  21.5 0.0 collective-permute-done.6.back1
  21.5 0.5 shard_map.99
  22.0 17.8 %all_to_all.10.pieces = bf16[32,24,128]{2,1,0:T(8,128)(2,1)S(1)} all-to-all(bf16[32,24,128]{2,1,0:T(8,128)(2,1)S(1)} %bitcast.9), channel_id=1, replica_groups=mesh['batch'=8,'mp'=4] {'batch','mp'}, dimensions={0} | all-to-all | bytes 393216 | tf_op jit(solution)/shard_map/all_to_all | solution.py:306
  39.9 0.7 %shard_map.100 = bf16[32,24,128]{2,1,0:T(8,128)(2,1)} custom-call(bf16[32,24,128]{2,1,0:T(8,128)(2,1)S(1)} %all_to_all.10.pieces), custom_call_target="tpu_custom_call" | custom-call | bytes 393216 | tf_op jit(solution)/shard_map/pallas_call | solution.py:38
  40.6 2.4 %all-to-all-start.1 = ((bf16[32,24,128]{2,1,0:T(8,128)(2,1)}), bf16[32,24,128]{2,1,0:T(8,128)(2,1)S(1)}, u32[]{:S(2)}, u32[]{:S(2)}) async-start(bf16[32,24,128]{2,1,0:T(8,128)(2,1)} %shard_map.100), calls=%async_computation.1 | async-start | bytes 393216 | tf_op jit(solution)/shard_map/all_to_all | solution.py:313
  43.0 1.0 %convolution_convert_fusion.1 = bf16[256,768]{1,0:T(8,128)(2,1)} fusion(bf16[256,128]{1,0:T(8,128)(2,1)S(1)} %get-tuple-element.65, bf16[768,128]{1,0:T(8,128)(2,1)S(1)} %get-tuple-element.39.projection), kind=kOutput, calls=%fused_computation.1 | convolution fusion | flops 50528256 | bytes 655360 | tf_op jit(solution)/shard_map/dot_general | solution.py:32
  44.0 1.9 %convolution_convert_fusion = bf16[1280,768]{1,0:T(8,128)(2,1)} fusion(bf16[1280,128]{1,0:T(8,128)(2,1)S(1)} %get-tuple-element.66, bf16[768,128]{1,0:T(8,128)(2,1)S(1)} %get-tuple-element.39.projection), kind=kOutput, calls=%fused_computation | convolution fusion | flops 252641280 | bytes 2490368 | tf_op jit(solution)/shard_map/dot_general | solution.py:32
  45.9 6.3 %all-to-all-done.1 = bf16[32,24,128]{2,1,0:T(8,128)(2,1)S(1)} async-done(((bf16[32,24,128]{2,1,0:T(8,128)(2,1)}), bf16[32,24,128]{2,1,0:T(8,128)(2,1)S(1)}, u32[]{:S(2)}, u32[]{:S(2)}) %all-to-all-start.1) | async-done | bytes 196640 | tf_op jit(solution)/shard_map/all_to_all | solution.py:313
  52.2 0.8 %bitcast_convert_fusion = f32[768,128]{1,0:T(8,128)} fusion(bf16[32,24,128]{2,1,0:T(8,128)(2,1)S(1)} %all-to-all-done.1), kind=kLoop, calls=%fused_computation.2 | loop fusion | flops 98304 | bytes 589824 | tf_op jit(solution)/shard_map/convert_element_type | solution.py:314
Async XLA Ops:
  2.5 5.9 %collective-permute-start.1 = (bf16[272,128]{1,0:T(8,128)(2,1)S(1)}, bf16[272,128]{1,0:T(8,128)(2,1)S(1)}, u32[]{:S(2)}, u32[]{:S(2)}) collective-permute-start(bf16[272,128]{1,0:T(8,128)(2,1)S(1)} %get-tuple-element.40.sent.sent0), channel_id=1, source_target_pairs={{24,0},{28,4},{0,8},{4,12},{8,16},{12,20},{16,24},{20,28},{25,1},{... | collective-permute-start | bytes 208904 | tf_op jit(solution)/shard_map/ppermute | solution.py:28
  4.7 6.5 %collective-permute-start = (bf16[272,128]{1,0:T(8,128)(2,1)S(1)}, bf16[272,128]{1,0:T(8,128)(2,1)S(1)}, u32[]{:S(2)}, u32[]{:S(2)}) collective-permute-start(bf16[272,128]{1,0:T(8,128)(2,1)S(1)} %get-tuple-element.40.sent.sent0), channel_id=1, source_target_pairs={{28,0},{0,4},{4,8},{8,12},{12,16},{16,20},{20,24},{24,28},{29,1},{... | collective-permute-start | bytes 208904 | tf_op jit(solution)/shard_map/ppermute | solution.py:28
  9.5 9.9 %collective-permute-start.5 = (bf16[144,256]{1,0:T(8,128)(2,1)S(1)}, bf16[144,256]{1,0:T(8,128)(2,1)S(1)}, u32[]{:S(2)}, u32[]{:S(2)}) collective-permute-start(bf16[144,256]{1,0:T(8,128)(2,1)S(1)} %get-tuple-element.57), channel_id=1, source_target_pairs={{8,0},{12,4},{16,8},{20,12},{24,16},{28,20},{0,24},{4,28},{9,1},{1... | collective-permute-start | bytes 221192 | tf_op jit(solution)/shard_map/ppermute | solution.py:28
  11.9 6.8 %collective-permute-start.4 = (f32[8,256]{1,0:T(8,128)S(1)}, f32[8,256]{1,0:T(8,128)S(1)}, u32[]{:S(2)}, u32[]{:S(2)}) collective-permute-start(f32[8,256]{1,0:T(8,128)S(1)} %get-tuple-element.56.logs), channel_id=1, source_target_pairs={{4,0},{8,4},{12,8},{16,12},{20,16},{24,20},{28,24},{0,28},{5,1},{9... | collective-permute-start | bytes 24584 | tf_op jit(solution)/shard_map/ppermute | solution.py:28
  12.9 5.8 %collective-permute-start.3 = (f32[8,256]{1,0:T(8,128)S(1)}, f32[8,256]{1,0:T(8,128)S(1)}, u32[]{:S(2)}, u32[]{:S(2)}) collective-permute-start(f32[8,256]{1,0:T(8,128)S(1)} %get-tuple-element.56.logs), channel_id=1, source_target_pairs={{24,0},{28,4},{0,8},{4,12},{8,16},{12,20},{16,24},{20,28},{25,1},{... | collective-permute-start | bytes 24584 | tf_op jit(solution)/shard_map/ppermute | solution.py:28
  14.2 5.2 %collective-permute-start.2 = (f32[8,256]{1,0:T(8,128)S(1)}, f32[8,256]{1,0:T(8,128)S(1)}, u32[]{:S(2)}, u32[]{:S(2)}) collective-permute-start(f32[8,256]{1,0:T(8,128)S(1)} %get-tuple-element.56.logs), channel_id=1, source_target_pairs={{28,0},{0,4},{4,8},{8,12},{12,16},{16,20},{20,24},{24,28},{29,1},{... | collective-permute-start | bytes 24584 | tf_op jit(solution)/shard_map/ppermute | solution.py:28
  14.5 7.0 %collective-permute-start.6 = (bf16[128,256]{1,0:T(8,128)(2,1)S(1)}, bf16[128,256]{1,0:T(8,128)(2,1)S(1)}, u32[]{:S(2)}, u32[]{:S(2)}) collective-permute-start(bf16[128,256]{1,0:T(8,128)(2,1)S(1)} %shard_map.98), channel_id=1, source_target_pairs={{4,0},{8,4},{12,8},{16,12},{20,16},{24,20},{28,24},{0,28},{5,1},{9... | collective-permute-start | bytes 196616 | tf_op jit(solution)/shard_map/ppermute | solution.py:28
  40.6 11.6 %all-to-all-start.1 = ((bf16[32,24,128]{2,1,0:T(8,128)(2,1)}), bf16[32,24,128]{2,1,0:T(8,128)(2,1)S(1)}, u32[]{:S(2)}, u32[]{:S(2)}) async-start(bf16[32,24,128]{2,1,0:T(8,128)(2,1)} %shard_map.100), calls=%async_computation.1 | async-start | bytes 393216 | tf_op jit(solution)/shard_map/all_to_all | solution.py:313

commit v7 on v5

--- a/solution.py
+++ b/solution.py
@@ -32,14 +32,14 @@
     return lax.dot_general(left, right, dims, preferred_element_type=jnp.float32)
 
 
-def call(body, outs, in_specs, args, scratch=(), flops=0, trans=0):
+def call(body, outs, in_specs, args, scratch=(), flops=0, trans=0, out_specs=None):
     moved = sum(a.size * a.dtype.itemsize for a in args)
     moved += sum(math.prod(o.shape) * jnp.dtype(o.dtype).itemsize for o in outs)
     return pl.pallas_call(
         body,
         out_shape=tuple(outs),
         in_specs=list(in_specs),
-        out_specs=tuple(vmem for _ in outs),
+        out_specs=out_specs or tuple(vmem for _ in outs),
         scratch_shapes=list(scratch),
         compiler_params=pltpu.CompilerParams(vmem_limit_bytes=24 * 2**20),
         cost_estimate=pl.CostEstimate(flops=flops, bytes_accessed=moved, transcendentals=trans),
@@ -239,11 +239,12 @@
 
 
 def grad_body(
-    queries, passages, wanted, query_hidden, passage_hidden, turned,
+    queries, passages, pieces, wanted, query_hidden, passage_hidden, turned,
     query_unit, query_inverse, passage_unit, passage_inverse,
     powers0, powers1, powers2, totals0, totals1, totals2, scores0, scores1, scores2,
-    sent0, sent1, sent2, logs, logs1, back1, back2,
-    losses, query_pre_grad, passage_pre_grad, partial, grad_sim, query_rows,
+    sent0, sent1, sent2, logs, logs1, back1, back2, weight,
+    losses, partial, query_out, passage_out,
+    grad_sim, query_rows, pre_rows, query_grad, passage_grad, sems,
 ):
     rows = powers0.shape[1]
     dim = turned.shape[0]
@@ -270,17 +271,30 @@
         fill_grad_sim(passages, coefficient, powers, grad_sim, block * rows)
         query_rows[block * rows : (block + 1) * rows, :] = query[:rows, :]
 
-    grad = dot32(grad_sim[...], query_rows[...])
-    pre = back_rows(grad, passage_unit[...], passage_inverse[...])
-    passage_pre_grad[...] = pre
-    both = dot32(pre.T, passage_hidden[...])
+    size = passage_hidden.shape[0] // pieces
+    copies = []
+    for piece in range(pieces):
+        part = pl.ds(piece * size, size)
+        grad = dot32(grad_sim[part, :], query_rows[...])
+        pre = back_rows(grad, passage_unit[part, :], passage_inverse[part, :])
+        pre_rows[part, :] = pre
+        passage_grad[part, :] = dot32(pre, weight[...], NT).astype(jnp.bfloat16)
+        copies.append(
+            pltpu.make_async_copy(passage_grad.at[part], passage_out.at[part], sems.at[piece])
+        )
+        copies[-1].start()
     to_query = dot32(turned[...], grad_sim[:, :rows])
     to_query += back1[:dim, :].astype(jnp.float32) * jnp.exp(second - total0)
     to_query += back2[:dim, :].astype(jnp.float32) * jnp.exp(third - total0)
     pre = back_rows(to_query.T, query_unit[...], query_inverse[...])
-    query_pre_grad[...] = pre
-    both += dot32(pre.T, query_hidden[...])
+    query_grad[...] = dot32(pre, weight[...], NT).astype(jnp.bfloat16)
+    copies.append(pltpu.make_async_copy(query_grad, query_out, sems.at[pieces]))
+    copies[-1].start()
+    both = dot32(pre.T, query_hidden[...])
+    both += dot32(pre_rows[...].T, passage_hidden[...])
     partial[...] = both.T.astype(jnp.bfloat16)
+    for copy in copies:
+        copy.wait()
 
 
 def sum_body(scale, copies, pieces, out):
@@ -381,23 +395,30 @@
     )
     back1 = shifted(back1, "batch", -1)
     logs1 = shifted(logs, "batch", 1)
-    losses, query_pre_grad, passage_pre_grad, partial = call(
-        functools.partial(grad_body, queries, passages),
+    pieces = passages // 2 if passages % 2 == 0 else passages
+    losses, partial, grad_query_hidden, grad_passage_hidden = call(
+        functools.partial(grad_body, queries, passages, pieces),
         (
-            of((1, queries), f32), of((rows, dim), bf16), of((slots, dim), bf16),
-            of((width, dim), bf16),
+            of((1, queries), f32), of((width, dim), bf16),
+            of((rows, width), bf16), of((slots, width), bf16),
         ),
-        (vmem,) * 24,
+        (vmem,) * 25,
         (wanted, query_rows, passage_rows, turned,
          query_unit, query_inverse, passage_unit, passage_inverse,
          powers0, powers1, powers2, totals0, totals1, totals2, scores0, scores1, scores2,
-         sent0, sent1, sent2, logs, logs1, back1, back2),
-        scratch=(pltpu.VMEM((slots, 3 * rows), bf16), pltpu.VMEM((3 * rows, dim), bf16)),
-        flops=8 * slots * dim * rows + 2 * (slots + rows) * width * dim,
+         sent0, sent1, sent2, logs, logs1, back1, back2, weight),
+        scratch=(
+            pltpu.VMEM((slots, 3 * rows), bf16),
+            pltpu.VMEM((3 * rows, dim), bf16),
+            pltpu.VMEM((slots, dim), bf16),
+            pltpu.VMEM((rows, width), bf16),
+            pltpu.VMEM((slots, width), bf16),
+            pltpu.SemaphoreType.DMA((pieces + 1,)),
+        ),
+        flops=8 * slots * dim * rows + 4 * (slots + rows) * width * dim,
+        out_specs=(vmem, vmem, hbm, hbm),
     )
     grad_projection = mean_over_devices(partial)
-    grad_query_hidden = dot32(query_pre_grad, weight, NT).astype(bf16)
-    grad_passage_hidden = dot32(passage_pre_grad, weight, NT).astype(bf16)
     losses = losses.reshape(queries)
     return (losses, grad_query_hidden, grad_passage_hidden, grad_projection)
 

time: 49.1 us -> 50.4 us (1.026)
  blocking collectives: 14.5 us -> 25.9 us
  waiting for transfers between devices: 11.2 us -> 4.92 us
  matrix products: 2.95 us -> 0 us
  starting transfers between devices: 10.7 us -> 8.27 us
  Pallas kernels: 8.19 us -> 9.67 us
    all_to_all x0 -> x1, blocking collectives: none -> 11.4 us  [mean_over_devices(): whole = lax.all_to_all(means, axes, 0, 0)]
    all_to_all x1 -> x0, waiting for transfers between devices: 6.28 us -> none  [mean_over_devices(): whole = lax.all_to_all(means, axes, 0, 0)]
    dot_general x2 -> x0, matrix products: 2.95 us -> none  [dot32(): lax.dot_general(left, right, dims, preferred_element_type=jnp.float32)]
    all_to_all x1 -> x0, starting transfers between devices: 2.37 us -> none  [mean_over_devices(): whole = lax.all_to_all(means, axes, 0, 0)]
    pallas_call x6, Pallas kernels: 8.19 us -> 9.67 us  [call(): pl.pallas_call(body, out_shape=tuple(outs), in_specs=list(in_specs), out_...]
  transfers between devices with their start and end apart: 7 -> 6, of which waited for: 3 -> 2; matrix products, arithmetic and copies ran while one was open for 6% -> 0% of each run, Pallas kernels for 8% -> 7%
where the time goes in v7:
time: 50.4 us; the launch traced here: 50.2 us
  blocking collectives  25.9 us (51%)
  Pallas kernels  9.67 us (19%)
  starting transfers between devices  8.27 us (16%)
  waiting for transfers between devices  4.92 us (10%)
  other arithmetic  0.79 us (2%)
  between operations  0.68 us (1%)
    all_to_all x1, blocking collectives, mean_over_devices(): pieces = lax.all_to_all(padded.reshape(devices, share, columns), axes, 0, 0)  14.5 us
    all_to_all x1, blocking collectives, mean_over_devices(): whole = lax.all_to_all(means, axes, 0, 0)  11.4 us
    pallas_call x6, Pallas kernels, call(): pl.pallas_call(body, out_shape=tuple(outs), in_specs=list(in_specs), out_...  9.67 us
    ppermute x6, starting transfers between devices, shifted(): return lax.ppermute(block, axis, route)  8.27 us
    ppermute x6, waiting for transfers between devices, shifted(): return lax.ppermute(block, axis, route)  4.92 us
  transfers between devices with their start and end apart: 6, of which 2 were waited for; matrix products, arithmetic and copies ran while one was open for 0% of the time, Pallas kernels for 7%

profile of v7, /device:TPU:1, one launch (start us, length us, event | category | flops | bytes accessed | tf_op | source)
XLA Modules:
  0.0 50.2 jit_solution(14924653026783830210)
XLA Ops:
  0.6 1.8 %shard_map.93 = (f32[256,128]{1,0:T(8,128)S(1)}, f32[256,128]{1,0:T(8,128)S(1)}, bf16[272,128]{1,0:T(8,128)(2,1)S(1)}, s32[16,256]{1,0:T(8,128)S(1)}, s32[1,256]...) custom-call(s32[8]{0:T(128)} %query_lengths_in.1, ...), custom_call_target="tpu_custom_call" | custom-call | flops 50331648 | bytes 5461096 | tf_op jit(solution)/shard_map/pallas_call | solution.py:38
  2.5 2.2 %collective-permute-start.1 = (bf16[272,128]{1,0:T(8,128)(2,1)S(1)}, bf16[272,128]{1,0:T(8,128)(2,1)S(1)}, u32[]{:S(2)}, u32[]{:S(2)}) collective-permute-start(bf16[272,128]{1,0:T(8,128)(2,1)S(1)} %get-tuple-element.39.sent.sent0), channel_id=1, source_target_pairs={{24,0},{28,4},{0,8},{4,12},{8,16},{12,20},{16,24},{20,28},{25,1},{... | collective-permute-start | bytes 208904 | tf_op jit(solution)/shard_map/ppermute | solution.py:28
  4.7 1.2 %collective-permute-start = (bf16[272,128]{1,0:T(8,128)(2,1)S(1)}, bf16[272,128]{1,0:T(8,128)(2,1)S(1)}, u32[]{:S(2)}, u32[]{:S(2)}) collective-permute-start(bf16[272,128]{1,0:T(8,128)(2,1)S(1)} %get-tuple-element.39.sent.sent0), channel_id=1, source_target_pairs={{28,0},{0,4},{4,8},{8,12},{12,16},{16,20},{20,24},{24,28},{29,1},{... | collective-permute-start | bytes 208904 | tf_op jit(solution)/shard_map/ppermute | solution.py:28
  5.9 1.5 %shard_map.94 = (f32[1280,128]{1,0:T(8,128)S(1)}, f32[1280,128]{1,0:T(8,128)S(1)}, bf16[1280,128]{1,0:T(8,128)(2,1)S(1)}, bf16[128,1280]{1,0:T(8,128)(2,1)S(1)},...) custom-call(s32[16,256]{1,0:T(8,128)S(1)} %get-tuple-element.37.valid, ...), custom_call_target="tpu_custom_call" | custom-call | flops 335544320 | bytes 5566464 | tf_op jit(solution)/shard_map/pallas_call | solution.py:38
  7.4 1.3 %collective-permute-start.2 = (f32[8,256]{1,0:T(8,128)S(1)}, f32[8,256]{1,0:T(8,128)S(1)}, u32[]{:S(2)}, u32[]{:S(2)}) collective-permute-start(f32[8,256]{1,0:T(8,128)S(1)} %get-tuple-element.47.log0), channel_id=1, source_target_pairs={{24,0},{28,4},{0,8},{4,12},{8,16},{12,20},{16,24},{20,28},{25,1},{... | collective-permute-start | bytes 24584 | tf_op jit(solution)/shard_map/ppermute | solution.py:28
  8.8 0.0 collective-permute-done.1.sent.sent2
  8.8 1.1 %shard_map.95 = (f32[1280,256]{1,0:T(8,128)S(1)}, f32[16,256]{1,0:T(8,128)S(1)}, f32[16,256]{1,0:T(8,128)S(1)}, f32[8,256]{1,0:T(8,128)S(1)}, bf16[144,256]{1,0:T(8,128)(2,1)S(1)}) custom-call(s32[16,256]{1,0:T(8,128)S(1)} %get-tuple-element.37.valid, bf16[1280,128]{1,0:T(8,128)(2,1)S(1)} %get-tuple-element.46.embed, ...), custom_call_target="tpu_custom_call" | custom-call | flops 167772160 | bytes 2166784 | tf_op jit(solution)/shard_map/pallas_call | solution.py:38
  9.9 2.0 %collective-permute-start.5 = (bf16[144,256]{1,0:T(8,128)(2,1)S(1)}, bf16[144,256]{1,0:T(8,128)(2,1)S(1)}, u32[]{:S(2)}, u32[]{:S(2)}) collective-permute-start(bf16[144,256]{1,0:T(8,128)(2,1)S(1)} %get-tuple-element.59), channel_id=1, source_target_pairs={{8,0},{12,4},{16,8},{20,12},{24,16},{28,20},{0,24},{4,28},{9,1},{1... | collective-permute-start | bytes 221192 | tf_op jit(solution)/shard_map/ppermute | solution.py:28
  11.9 0.2 collective-permute-done.2.far0
  12.1 0.0 collective-permute-done.sent.sent1
  12.1 1.1 %shard_map.96 = (f32[1280,256]{1,0:T(8,128)S(1)}, f32[16,256]{1,0:T(8,128)S(1)}, f32[16,256]{1,0:T(8,128)S(1)}, f32[8,256]{1,0:T(8,128)S(1)}, bf16[144,256]{1,0:T(8,128)(2,1)S(1)}) custom-call(s32[16,256]{1,0:T(8,128)S(1)} %get-tuple-element.37.valid, bf16[1280,128]{1,0:T(8,128)(2,1)S(1)} %get-tuple-element.46.embed, ...), custom_call_target="tpu_custom_call" | custom-call | flops 167772160 | bytes 2191360 | tf_op jit(solution)/shard_map/pallas_call | solution.py:38
  13.2 1.1 %collective-permute-start.4 = (bf16[144,256]{1,0:T(8,128)(2,1)S(1)}, bf16[144,256]{1,0:T(8,128)(2,1)S(1)}, u32[]{:S(2)}, u32[]{:S(2)}) collective-permute-start(bf16[144,256]{1,0:T(8,128)(2,1)S(1)} %get-tuple-element.58), channel_id=1, source_target_pairs={{4,0},{8,4},{12,8},{16,12},{20,16},{24,20},{28,24},{0,28},{5,1},{9... | collective-permute-start | bytes 221192 | tf_op jit(solution)/shard_map/ppermute | solution.py:28
  14.2 0.4 collective-permute-start.3
  14.7 4.8 %collective-permute-done.3.logs1 = f32[8,256]{1,0:T(8,128)S(1)} collective-permute-done((f32[8,256]{1,0:T(8,128)S(1)}, f32[8,256]{1,0:T(8,128)S(1)}, u32[]{:S(2)}, u32[]{:S(2)}) %collective-permute-start.3) | collective-permute-done | bytes 8224 | tf_op jit(solution)/shard_map/ppermute | solution.py:28
  19.4 0.0 collective-permute-done.5.back2
  19.4 0.0 collective-permute-done.4.back1
  19.4 4.0 %shard_map.97 = (f32[1,8]{1,0:T(1,128)}, bf16[768,128]{1,0:T(8,128)(2,1)S(1)}, bf16[256,768]{1,0:T(8,128)(2,1)}, bf16[1280,768]{1,0:T(8,128)(2,1)}) custom-call(s32[1,256]{1,0:T(1,128)S(1)} %get-tuple-element.34.wanted, bf16[256,768]{1,0:T(8,128)(2,1)S(1)} %get-tuple-element.35.query_hidden, bf16[1280,768]{1,0:T(8,128)(2,1)S(1)} %get-tuple-element.36.hidden.passage_hidden, ...), custom_call_target="tpu_custom_call" | custom-call | flops 939524096 | bytes 11416608 | tf_op jit(solution)/shard_map/pallas_call | solution.py:38
  23.5 14.5 %all_to_all.10.pieces = bf16[32,24,128]{2,1,0:T(8,128)(2,1)S(1)} all-to-all(bf16[32,24,128]{2,1,0:T(8,128)(2,1)S(1)} %bitcast.5), channel_id=1, replica_groups=mesh['batch'=8,'mp'=4] {'batch','mp'}, dimensions={0} | all-to-all | bytes 393216 | tf_op jit(solution)/shard_map/all_to_all | solution.py:313
  38.0 11.4 %all_to_all.11 = bf16[32,24,128]{2,1,0:T(8,128)(2,1)S(1)} all-to-all(bf16[32,24,128]{2,1,0:T(8,128)(2,1)S(1)} %shard_map.98), channel_id=1, replica_groups=mesh['batch'=8,'mp'=4] {'batch','mp'}, dimensions={0} | all-to-all | bytes 393216 | tf_op jit(solution)/shard_map/all_to_all | solution.py:320
  49.4 0.8 %bitcast_convert_fusion = f32[768,128]{1,0:T(8,128)} fusion(bf16[32,24,128]{2,1,0:T(8,128)(2,1)S(1)} %all_to_all.11), kind=kLoop, calls=%fused_computation | loop fusion | flops 98304 | bytes 589824 | tf_op jit(solution)/shard_map/convert_element_type | solution.py:321
  (1 shorter events, 0.0 us)
Async XLA Ops:
  2.5 6.3 %collective-permute-start.1 = (bf16[272,128]{1,0:T(8,128)(2,1)S(1)}, bf16[272,128]{1,0:T(8,128)(2,1)S(1)}, u32[]{:S(2)}, u32[]{:S(2)}) collective-permute-start(bf16[272,128]{1,0:T(8,128)(2,1)S(1)} %get-tuple-element.39.sent.sent0), channel_id=1, source_target_pairs={{24,0},{28,4},{0,8},{4,12},{8,16},{12,20},{16,24},{20,28},{25,1},{... | collective-permute-start | bytes 208904 | tf_op jit(solution)/shard_map/ppermute | solution.py:28
  4.7 7.4 %collective-permute-start = (bf16[272,128]{1,0:T(8,128)(2,1)S(1)}, bf16[272,128]{1,0:T(8,128)(2,1)S(1)}, u32[]{:S(2)}, u32[]{:S(2)}) collective-permute-start(bf16[272,128]{1,0:T(8,128)(2,1)S(1)} %get-tuple-element.39.sent.sent0), channel_id=1, source_target_pairs={{28,0},{0,4},{4,8},{8,12},{12,16},{16,20},{20,24},{24,28},{29,1},{... | collective-permute-start | bytes 208904 | tf_op jit(solution)/shard_map/ppermute | solution.py:28
  7.4 4.6 %collective-permute-start.2 = (f32[8,256]{1,0:T(8,128)S(1)}, f32[8,256]{1,0:T(8,128)S(1)}, u32[]{:S(2)}, u32[]{:S(2)}) collective-permute-start(f32[8,256]{1,0:T(8,128)S(1)} %get-tuple-element.47.log0), channel_id=1, source_target_pairs={{24,0},{28,4},{0,8},{4,12},{8,16},{12,20},{16,24},{20,28},{25,1},{... | collective-permute-start | bytes 24584 | tf_op jit(solution)/shard_map/ppermute | solution.py:28
  9.9 9.6 %collective-permute-start.5 = (bf16[144,256]{1,0:T(8,128)(2,1)S(1)}, bf16[144,256]{1,0:T(8,128)(2,1)S(1)}, u32[]{:S(2)}, u32[]{:S(2)}) collective-permute-start(bf16[144,256]{1,0:T(8,128)(2,1)S(1)} %get-tuple-element.59), channel_id=1, source_target_pairs={{8,0},{12,4},{16,8},{20,12},{24,16},{28,20},{0,24},{4,28},{9,1},{1... | collective-permute-start | bytes 221192 | tf_op jit(solution)/shard_map/ppermute | solution.py:28
  13.2 6.3 %collective-permute-start.4 = (bf16[144,256]{1,0:T(8,128)(2,1)S(1)}, bf16[144,256]{1,0:T(8,128)(2,1)S(1)}, u32[]{:S(2)}, u32[]{:S(2)}) collective-permute-start(bf16[144,256]{1,0:T(8,128)(2,1)S(1)} %get-tuple-element.58), channel_id=1, source_target_pairs={{4,0},{8,4},{12,8},{16,12},{20,16},{24,20},{28,24},{0,28},{5,1},{9... | collective-permute-start | bytes 221192 | tf_op jit(solution)/shard_map/ppermute | solution.py:28
  14.2 5.2 %collective-permute-start.3 = (f32[8,256]{1,0:T(8,128)S(1)}, f32[8,256]{1,0:T(8,128)S(1)}, u32[]{:S(2)}, u32[]{:S(2)}) collective-permute-start(f32[8,256]{1,0:T(8,128)S(1)} %get-tuple-element.57.logs), channel_id=1, source_target_pairs={{28,0},{0,4},{4,8},{8,12},{12,16},{16,20},{20,24},{24,28},{29,1},{... | collective-permute-start | bytes 24584 | tf_op jit(solution)/shard_map/ppermute | solution.py:28

commit v8 on v5

--- a/solution.py
+++ b/solution.py
@@ -76,11 +76,13 @@
     return copies
 
 
-def query_embed_body(
+def own_body(
     queries, query_lengths_in, passage_lengths_in, positives_in, query_hidden_in, passage_hidden_in,
     projection_in,
-    unit_out, inverse_out, sent_out, slots_out, wanted_out, query_hidden, passage_hidden, projection,
-    query_lengths, passage_lengths, positives, sems,
+    query_unit_out, query_inverse_out, passage_unit_out, passage_inverse_out, sent_out, embed_out,
+    turned_out, slots_out, wanted_out, powers, totals, scores, log_out,
+    query_hidden, passage_hidden, projection,
+    tops, query_lengths, passage_lengths, positives, sems,
 ):
     pairs = (
         (projection_in, projection), (query_hidden_in, query_hidden),
@@ -91,32 +93,54 @@
     copies[0].wait()
     copies[1].wait()
     rows = query_hidden.shape[0]
-    before = dot32(query_hidden[...], projection[...])
-    unit, inverse = unit_rows(before)
-    unit_out[...] = unit
-    inverse_out[...] = jnp.broadcast_to(inverse, unit.shape)
+    unit, inverse = unit_rows(dot32(query_hidden[...], projection[...]))
+    query_unit_out[...] = unit
+    query_inverse_out[...] = jnp.broadcast_to(inverse, unit.shape)
     sent_out[:rows, :] = unit.astype(jnp.bfloat16)
     copies[2].wait()
     keep = keep_row(query_lengths, queries, rows // queries)
-    row = lax.broadcasted_iota(jnp.int32, (ROWS, LANES), 0)
-    tail = jnp.zeros((ROWS, LANES), jnp.float32)
-    for piece in range(rows // LANES):
-        tail = jnp.where(row == piece, keep[:, piece * LANES : (piece + 1) * LANES], tail)
-    sent_out[rows:, :] = tail.astype(jnp.bfloat16)
     copies[3].wait()
     wanted_out[...] = spread(positives, queries, rows // queries)
     copies[4].wait()
+    passages = passage_lengths.shape[0]
     c = lax.broadcasted_iota(jnp.int32, slots_out.shape, 0)
     valid = jnp.zeros(slots_out.shape, jnp.int32)
-    for item in range(passage_lengths.shape[0]):
+    for item in range(passages):
         valid = jnp.where(c == item, passage_lengths[item], valid)
     slots_out[...] = valid
     copies[5].wait()
+    unit, inverse = unit_rows(dot32(passage_hidden[...], projection[...]))
+    passage_unit_out[...] = unit
+    passage_inverse_out[...] = jnp.broadcast_to(inverse, unit.shape)
+    embed = unit.astype(jnp.bfloat16)
+    embed_out[...] = embed
+    score_block(
+        queries, passages, slots_out, embed_out, sent_out, powers, totals, scores, tops, keep
+    )
+    log = log_sum(scores[...])
+    log_out[...] = stack_rows(log_out.shape, (log,))
+    lines = [keep] + [part.astype(jnp.float32) for part in split(log)]
+    lines = [
+        line[:, i * LANES : (i + 1) * LANES] for line in lines for i in range(rows // LANES)
+    ]
+    sent_out[rows:, :] = stack_rows((ROWS, LANES), lines).astype(jnp.bfloat16)
+    turned_out[...] = embed.T
+
+
+def sent_row(sent, rows, place):
+    tail = sent[rows:, :].astype(jnp.float32)
+    count = rows // LANES
+    return jnp.concatenate(
+        [tail[i : i + 1, :] for i in range(place * count, (place + 1) * count)], axis=1
+    )
 
 
 def sent_keep(sent, rows):
-    tail = sent[rows:, :].astype(jnp.float32)
-    return jnp.concatenate([tail[i : i + 1, :] for i in range(rows // LANES)], axis=1)
+    return sent_row(sent, rows, 0)
+
+
+def sent_log(sent, rows):
+    return sent_row(sent, rows, 1) + (sent_row(sent, rows, 2) + sent_row(sent, rows, 3))
 
 
 def split(values):
@@ -126,7 +150,7 @@
     return high, middle, (rest - middle.astype(jnp.float32)).astype(jnp.bfloat16)
 
 
-def score_block(queries, passages, valid, embed, sent, powers, totals, scores, tops):
+def score_block(queries, passages, valid, embed, sent, powers, totals, scores, tops, keep=None):
     rows = sent.shape[0] - ROWS
     tokens = embed.shape[0] // passages
     query = sent[:rows, :]
@@ -134,8 +158,9 @@
     slot = lax.broadcasted_iota(jnp.int32, (tokens - half, rows), 0) + half
     totals[...] = jnp.ones(totals.shape, jnp.float32)
     tops[...] = jnp.zeros(tops.shape, jnp.float32)
+    powers[...] = dot32(embed[...], query, NT)
     for c in range(passages):
-        sims = dot32(embed[c * tokens : (c + 1) * tokens, :], query, NT)
+        sims = powers[c * tokens : (c + 1) * tokens, :]
         low, high = sims[:half], jnp.where(slot < valid[c : c + 1, :], sims[half:], -jnp.inf)
         top = jnp.maximum(
             jnp.max(low, axis=0, keepdims=True), jnp.max(high, axis=0, keepdims=True)
@@ -149,27 +174,13 @@
             high, axis=0, keepdims=True
         )
     best = tops[...] + jnp.log(totals[...]) / inner_scale
-    best = best * sent_keep(sent, rows)
+    best = best * (sent_keep(sent, rows) if keep is None else keep)
     group = rows // queries
     same = lax.broadcasted_iota(jnp.int32, (rows, rows), 0) // group
     same = (same == lax.broadcasted_iota(jnp.int32, (rows, rows), 1) // group).astype(jnp.bfloat16)
     total = sum(dot32(part, same) for part in split(best))
     c = lax.broadcasted_iota(jnp.int32, total.shape, 0)
     scores[...] = jnp.where(c < passages, outer_scale * total, -jnp.inf)
-
-
-def own_score_body(
-    queries, passages, valid, hidden, projection, sent,
-    unit_out, inverse_out, embed_out, turned_out, powers, totals, scores, log_out, tops,
-):
-    unit, inverse = unit_rows(dot32(hidden[...], projection[...]))
-    unit_out[...] = unit
-    inverse_out[...] = jnp.broadcast_to(inverse, unit.shape)
-    embed = unit.astype(jnp.bfloat16)
-    embed_out[...] = embed
-    score_block(queries, passages, valid, embed_out, sent, powers, totals, scores, tops)
-    log_out[...] = stack_rows(log_out.shape, (log_sum(scores[...]),))
-    turned_out[...] = embed.T
 
 
 def log_sum(scores):
@@ -221,13 +232,13 @@
 
 
 def near_score_body(
-    queries, passages, valid, embed, turned, sent, log0, log2, far0,
+    queries, passages, valid, embed, turned, sent, log0, log2,
     powers, totals, scores, logs, back, tops, grad_sim,
 ):
     score_block(queries, passages, valid, embed, sent, powers, totals, scores, tops)
     log = log_sum(scores[...])
     other = log2[0:1, :]
-    logs[...] = stack_rows(logs.shape, (log0[0:1, :], log, other, far0[0:1, :]))
+    logs[...] = stack_rows(logs.shape, (log0[0:1, :], log, other))
     tail = split(log) + split(other)
     send_back(passages, turned, sent, powers, totals, scores, log, tail, back, grad_sim)
 
@@ -249,8 +260,8 @@
     dim = turned.shape[0]
     second, third = joined(back1, dim, 0), joined(back2, dim, 0)
     total0 = log_add((logs[0:1, :], second, third))
-    total1 = log_add((logs1[0:1, :], logs[1:2, :], joined(back1, dim, 3)))
-    total2 = log_add((logs[3:4, :], logs1[1:2, :], logs[2:3, :]))
+    total1 = log_add((sent_log(sent1, rows), logs[1:2, :], joined(back1, dim, 3)))
+    total2 = log_add((sent_log(sent2, rows), logs1[1:2, :], logs[2:3, :]))
     scores = scores0[...]
     onehot = lax.broadcasted_iota(jnp.int32, scores.shape, 0) == wanted[...]
     loss = total0 - jnp.sum(jnp.where(onehot, scores, 0.0), axis=0, keepdims=True)
@@ -322,41 +333,32 @@
         query_lengths, passage_lengths, positives, query_hidden, passage_hidden, projection
     )
     taken = tuple(pltpu.with_memory_space_constraint(x, pltpu.HBM) for x in taken)
-    query_unit, query_inverse, sent0, valid, wanted, query_rows, passage_rows, weight = call(
-        functools.partial(query_embed_body, queries),
+    (
+        query_unit, query_inverse, passage_unit, passage_inverse, sent0, embed, turned,
+        valid, wanted, powers0, totals0, scores0, log0, query_rows, passage_rows, weight,
+    ) = call(
+        functools.partial(own_body, queries),
         (
-            of((rows, dim), f32), of((rows, dim), f32), of((rows + ROWS, dim), bf16),
-            of((ROWS, rows), jnp.int32),
-            of((1, rows), jnp.int32), of((rows, width), bf16), of((slots, width), bf16),
-            of((width, dim), bf16),
+            of((rows, dim), f32), of((rows, dim), f32), of((slots, dim), f32),
+            of((slots, dim), f32), of((rows + ROWS, dim), bf16), of((slots, dim), bf16),
+            of((dim, slots), bf16), of((ROWS, rows), jnp.int32), of((1, rows), jnp.int32),
+            of((slots, rows), f32), pair, pair, of((8, rows), f32),
+            of((rows, width), bf16), of((slots, width), bf16), of((width, dim), bf16),
         ),
         (hbm,) * 6,
         taken,
         scratch=(
+            pairs,
             pltpu.SMEM((queries,), jnp.int32),
             pltpu.SMEM((passages,), jnp.int32),
             pltpu.SMEM((queries,), jnp.int32),
             pltpu.SemaphoreType.DMA((6,)),
         ),
-        flops=2 * rows * width * dim,
+        flops=2 * (slots + rows) * width * dim + 2 * slots * rows * dim,
+        trans=slots * rows,
     )
     sent1 = shifted(sent0, "batch", 1)
     sent2 = shifted(sent0, "batch", 2)
-    (
-        passage_unit, passage_inverse, embed, turned, powers0, totals0, scores0, log0
-    ) = call(
-        functools.partial(own_score_body, queries, passages),
-        (
-            of((slots, dim), f32), of((slots, dim), f32), of((slots, dim), bf16),
-            of((dim, slots), bf16), of((slots, rows), f32), pair, pair, of((8, rows), f32),
-        ),
-        (vmem,) * 4,
-        (valid, passage_rows, weight, sent0),
-        scratch=(pairs,),
-        flops=2 * slots * dim * (width + rows),
-        trans=slots * rows,
-    )
-    far0 = shifted(log0, "batch", 2)
     block_outs = (
         of((slots, rows), f32), pair, pair, of((8, rows), f32), of((dim + ROWS, rows), bf16)
     )
@@ -373,8 +375,8 @@
     powers1, totals1, scores1, logs, back1 = call(
         functools.partial(near_score_body, queries, passages),
         block_outs,
-        (vmem,) * 7,
-        (valid, embed, turned, sent1, log0, log2, far0),
+        (vmem,) * 6,
+        (valid, embed, turned, sent1, log0, log2),
         scratch=(pairs, pltpu.VMEM((slots, rows), bf16)),
         flops=4 * slots * dim * rows,
         trans=slots * rows,

time: 49.1 us -> 50.3 us (1.024)
  waiting for transfers between devices: 11.2 us -> 13.6 us
  starting transfers between devices: 10.7 us -> 8.79 us
    ppermute x6 -> x5, waiting for transfers between devices: 4.91 us -> 7.35 us  [shifted(): return lax.ppermute(block, axis, route)]
    ppermute x6 -> x5, starting transfers between devices: 8.28 us -> 6.42 us  [shifted(): return lax.ppermute(block, axis, route)]
    pallas_call x6 -> x5, Pallas kernels: 8.19 us -> 8.28 us  [call(): pl.pallas_call(body, out_shape=tuple(outs), in_specs=list(in_specs), out_...]
  transfers between devices with their start and end apart: 7 -> 6, of which waited for: 3 -> 4; matrix products, arithmetic and copies ran while one was open for 6% -> 6% of each run, Pallas kernels for 8% -> 4%
where the time goes in v8:
time: 50.3 us; the launch traced here: 50 us
  blocking collectives  14.9 us (30%)
  waiting for transfers between devices  13.6 us (27%)
  starting transfers between devices  8.79 us (17%)
  Pallas kernels  8.28 us (16%)
  matrix products  2.96 us (6%)
  other arithmetic  0.78 us (2%)
  between operations  0.68 us (1%)
    all_to_all x1, blocking collectives, mean_over_devices(): pieces = lax.all_to_all(padded.reshape(devices, share, columns), axes, 0, 0)  14.9 us
    pallas_call x5, Pallas kernels, call(): pl.pallas_call(body, out_shape=tuple(outs), in_specs=list(in_specs), out_...  8.28 us
    ppermute x5, waiting for transfers between devices, shifted(): return lax.ppermute(block, axis, route)  7.35 us
    ppermute x5, starting transfers between devices, shifted(): return lax.ppermute(block, axis, route)  6.42 us
    all_to_all x1, waiting for transfers between devices, mean_over_devices(): whole = lax.all_to_all(means, axes, 0, 0)  6.27 us
    dot_general x2, matrix products, dot32(): lax.dot_general(left, right, dims, preferred_element_type=jnp.float32)  2.96 us
    all_to_all x1, starting transfers between devices, mean_over_devices(): whole = lax.all_to_all(means, axes, 0, 0)  2.37 us
  transfers between devices with their start and end apart: 6, of which 4 were waited for; matrix products, arithmetic and copies ran while one was open for 6% of the time, Pallas kernels for 4%

profile of v8, /device:TPU:1, one launch (start us, length us, event | category | flops | bytes accessed | tf_op | source)
XLA Modules:
  0.0 50.0 jit_solution(16462645974943803221)
XLA Ops:
  0.6 3.4 %shard_map.93 = (f32[256,128]{1,0:T(8,128)S(1)}, f32[256,128]{1,0:T(8,128)S(1)}, f32[1280,128]{1,0:T(8,128)S(1)}, f32[1280,128]{1,0:T(8,128)S(1)}, bf16[272,128]...) custom-call(s32[8]{0:T(128)} %query_lengths_in.1, ...), custom_call_target="tpu_custom_call" | custom-call | flops 385875968 | bytes 8778856 | tf_op jit(solution)/shard_map/pallas_call | solution.py:38
  4.1 2.2 %collective-permute-start.1 = (bf16[272,128]{1,0:T(8,128)(2,1)S(1)}, bf16[272,128]{1,0:T(8,128)(2,1)S(1)}, u32[]{:S(2)}, u32[]{:S(2)}) collective-permute-start(bf16[272,128]{1,0:T(8,128)(2,1)S(1)} %get-tuple-element.45.sent0), channel_id=1, source_target_pairs={{24,0},{28,4},{0,8},{4,12},{8,16},{12,20},{16,24},{20,28},{25,1},{... | collective-permute-start | bytes 208904 | tf_op jit(solution)/shard_map/ppermute | solution.py:28
  6.2 1.2 %collective-permute-start = (bf16[272,128]{1,0:T(8,128)(2,1)S(1)}, bf16[272,128]{1,0:T(8,128)(2,1)S(1)}, u32[]{:S(2)}, u32[]{:S(2)}) collective-permute-start(bf16[272,128]{1,0:T(8,128)(2,1)S(1)} %get-tuple-element.45.sent0), channel_id=1, source_target_pairs={{28,0},{0,4},{4,8},{8,12},{12,16},{16,20},{20,24},{24,28},{29,1},{... | collective-permute-start | bytes 208904 | tf_op jit(solution)/shard_map/ppermute | solution.py:28
  7.4 2.5 %collective-permute-done.1.sent.sent2 = bf16[272,128]{1,0:T(8,128)(2,1)S(1)} collective-permute-done((bf16[272,128]{1,0:T(8,128)(2,1)S(1)}, bf16[272,128]{1,0:T(8,128)(2,1)S(1)}, u32[]{:S(2)}, u32[]{:S(2)}) %collective-permute-start.1) | collective-permute-done | bytes 69664 | tf_op jit(solution)/shard_map/ppermute | solution.py:28
  10.0 1.1 %shard_map.94 = (f32[1280,256]{1,0:T(8,128)S(1)}, f32[16,256]{1,0:T(8,128)S(1)}, f32[16,256]{1,0:T(8,128)S(1)}, f32[8,256]{1,0:T(8,128)S(1)}, bf16[144,256]{1,0:T(8,128)(2,1)S(1)}) custom-call(s32[16,256]{1,0:T(8,128)S(1)} %get-tuple-element.43.valid, bf16[1280,128]{1,0:T(8,128)(2,1)S(1)} %get-tuple-element.44.embed, ...), custom_call_target="tpu_custom_call" | custom-call | flops 167772160 | bytes 2166784 | tf_op jit(solution)/shard_map/pallas_call | solution.py:38
  11.1 1.5 %collective-permute-start.4 = (bf16[144,256]{1,0:T(8,128)(2,1)S(1)}, bf16[144,256]{1,0:T(8,128)(2,1)S(1)}, u32[]{:S(2)}, u32[]{:S(2)}) collective-permute-start(bf16[144,256]{1,0:T(8,128)(2,1)S(1)} %get-tuple-element.58), channel_id=1, source_target_pairs={{8,0},{12,4},{16,8},{20,12},{24,16},{28,20},{0,24},{4,28},{9,1},{1... | collective-permute-start | bytes 221192 | tf_op jit(solution)/shard_map/ppermute | solution.py:28
  12.6 0.1 collective-permute-done.sent.sent1
  12.7 1.1 %shard_map.95 = (f32[1280,256]{1,0:T(8,128)S(1)}, f32[16,256]{1,0:T(8,128)S(1)}, f32[16,256]{1,0:T(8,128)S(1)}, f32[8,256]{1,0:T(8,128)S(1)}, bf16[144,256]{1,0:T(8,128)(2,1)S(1)}) custom-call(s32[16,256]{1,0:T(8,128)S(1)} %get-tuple-element.43.valid, bf16[1280,128]{1,0:T(8,128)(2,1)S(1)} %get-tuple-element.44.embed, ...), custom_call_target="tpu_custom_call" | custom-call | flops 167772160 | bytes 2183168 | tf_op jit(solution)/shard_map/pallas_call | solution.py:38
  13.8 1.0 %collective-permute-start.3 = (bf16[144,256]{1,0:T(8,128)(2,1)S(1)}, bf16[144,256]{1,0:T(8,128)(2,1)S(1)}, u32[]{:S(2)}, u32[]{:S(2)}) collective-permute-start(bf16[144,256]{1,0:T(8,128)(2,1)S(1)} %get-tuple-element.57), channel_id=1, source_target_pairs={{4,0},{8,4},{12,8},{16,12},{20,16},{24,20},{28,24},{0,28},{5,1},{9... | collective-permute-start | bytes 221192 | tf_op jit(solution)/shard_map/ppermute | solution.py:28
  14.9 0.5 collective-permute-start.2
  15.3 4.7 %collective-permute-done.2.logs1 = f32[8,256]{1,0:T(8,128)S(1)} collective-permute-done((f32[8,256]{1,0:T(8,128)S(1)}, f32[8,256]{1,0:T(8,128)S(1)}, u32[]{:S(2)}, u32[]{:S(2)}) %collective-permute-start.2) | collective-permute-done | bytes 8224 | tf_op jit(solution)/shard_map/ppermute | solution.py:28
  20.1 0.0 collective-permute-done.4.back2
  20.1 0.0 collective-permute-done.3.back1
  20.1 1.9 %shard_map.96 = (f32[1,8]{1,0:T(1,128)}, bf16[256,128]{1,0:T(8,128)(2,1)S(1)}, bf16[1280,128]{1,0:T(8,128)(2,1)S(1)}, bf16[768,128]{1,0:T(8,128)(2,1)S(1)}) custom-call(s32[1,256]{1,0:T(1,128)S(1)} %get-tuple-element.34.wanted, bf16[256,768]{1,0:T(8,128)(2,1)S(1)} %get-tuple-element.35.query_hidden, bf16[1280,768]{1,0:T(8,128)(2,1)S(1)} %get-tuple-element.36.passage_hidden, ...), custom_call_target="tpu_custom_call" | custom-call | flops 637534208 | bytes 9253920 | tf_op jit(solution)/shard_map/pallas_call | solution.py:38
  22.0 14.9 %all_to_all.10.pieces = bf16[32,24,128]{2,1,0:T(8,128)(2,1)S(1)} all-to-all(bf16[32,24,128]{2,1,0:T(8,128)(2,1)S(1)} %bitcast.9), channel_id=1, replica_groups=mesh['batch'=8,'mp'=4] {'batch','mp'}, dimensions={0} | all-to-all | bytes 393216 | tf_op jit(solution)/shard_map/all_to_all | solution.py:310
  36.9 0.7 %shard_map.97 = bf16[32,24,128]{2,1,0:T(8,128)(2,1)} custom-call(bf16[32,24,128]{2,1,0:T(8,128)(2,1)S(1)} %all_to_all.10.pieces), custom_call_target="tpu_custom_call" | custom-call | bytes 393216 | tf_op jit(solution)/shard_map/pallas_call | solution.py:38
  37.7 2.4 %all-to-all-start.1 = ((bf16[32,24,128]{2,1,0:T(8,128)(2,1)}), bf16[32,24,128]{2,1,0:T(8,128)(2,1)S(1)}, u32[]{:S(2)}, u32[]{:S(2)}) async-start(bf16[32,24,128]{2,1,0:T(8,128)(2,1)} %shard_map.97), calls=%async_computation.1 | async-start | bytes 393216 | tf_op jit(solution)/shard_map/all_to_all | solution.py:317
  40.0 1.0 %convolution_convert_fusion.1 = bf16[256,768]{1,0:T(8,128)(2,1)} fusion(bf16[256,128]{1,0:T(8,128)(2,1)S(1)} %get-tuple-element.60, bf16[768,128]{1,0:T(8,128)(2,1)S(1)} %get-tuple-element.61), kind=kOutput, calls=%fused_computation.1 | convolution fusion | flops 50528256 | bytes 655360 | tf_op jit(solution)/shard_map/dot_general | solution.py:32
  41.0 1.9 %convolution_convert_fusion = bf16[1280,768]{1,0:T(8,128)(2,1)} fusion(bf16[1280,128]{1,0:T(8,128)(2,1)S(1)} %get-tuple-element.62, bf16[768,128]{1,0:T(8,128)(2,1)S(1)} %get-tuple-element.61), kind=kOutput, calls=%fused_computation | convolution fusion | flops 252641280 | bytes 2490368 | tf_op jit(solution)/shard_map/dot_general | solution.py:32
  43.0 6.3 %all-to-all-done.1 = bf16[32,24,128]{2,1,0:T(8,128)(2,1)S(1)} async-done(((bf16[32,24,128]{2,1,0:T(8,128)(2,1)}), bf16[32,24,128]{2,1,0:T(8,128)(2,1)S(1)}, u32[]{:S(2)}, u32[]{:S(2)}) %all-to-all-start.1) | async-done | bytes 196640 | tf_op jit(solution)/shard_map/all_to_all | solution.py:317
  49.3 0.8 %bitcast_convert_fusion = f32[768,128]{1,0:T(8,128)} fusion(bf16[32,24,128]{2,1,0:T(8,128)(2,1)S(1)} %all-to-all-done.1), kind=kLoop, calls=%fused_computation.2 | loop fusion | flops 98304 | bytes 589824 | tf_op jit(solution)/shard_map/convert_element_type | solution.py:318
Async XLA Ops:
  4.1 5.9 %collective-permute-start.1 = (bf16[272,128]{1,0:T(8,128)(2,1)S(1)}, bf16[272,128]{1,0:T(8,128)(2,1)S(1)}, u32[]{:S(2)}, u32[]{:S(2)}) collective-permute-start(bf16[272,128]{1,0:T(8,128)(2,1)S(1)} %get-tuple-element.45.sent0), channel_id=1, source_target_pairs={{24,0},{28,4},{0,8},{4,12},{8,16},{12,20},{16,24},{20,28},{25,1},{... | collective-permute-start | bytes 208904 | tf_op jit(solution)/shard_map/ppermute | solution.py:28
  6.2 6.5 %collective-permute-start = (bf16[272,128]{1,0:T(8,128)(2,1)S(1)}, bf16[272,128]{1,0:T(8,128)(2,1)S(1)}, u32[]{:S(2)}, u32[]{:S(2)}) collective-permute-start(bf16[272,128]{1,0:T(8,128)(2,1)S(1)} %get-tuple-element.45.sent0), channel_id=1, source_target_pairs={{28,0},{0,4},{4,8},{8,12},{12,16},{16,20},{20,24},{24,28},{29,1},{... | collective-permute-start | bytes 208904 | tf_op jit(solution)/shard_map/ppermute | solution.py:28
  11.1 9.0 %collective-permute-start.4 = (bf16[144,256]{1,0:T(8,128)(2,1)S(1)}, bf16[144,256]{1,0:T(8,128)(2,1)S(1)}, u32[]{:S(2)}, u32[]{:S(2)}) collective-permute-start(bf16[144,256]{1,0:T(8,128)(2,1)S(1)} %get-tuple-element.58), channel_id=1, source_target_pairs={{8,0},{12,4},{16,8},{20,12},{24,16},{28,20},{0,24},{4,28},{9,1},{1... | collective-permute-start | bytes 221192 | tf_op jit(solution)/shard_map/ppermute | solution.py:28
  13.8 6.2 %collective-permute-start.3 = (bf16[144,256]{1,0:T(8,128)(2,1)S(1)}, bf16[144,256]{1,0:T(8,128)(2,1)S(1)}, u32[]{:S(2)}, u32[]{:S(2)}) collective-permute-start(bf16[144,256]{1,0:T(8,128)(2,1)S(1)} %get-tuple-element.57), channel_id=1, source_target_pairs={{4,0},{8,4},{12,8},{16,12},{20,16},{24,20},{28,24},{0,28},{5,1},{9... | collective-permute-start | bytes 221192 | tf_op jit(solution)/shard_map/ppermute | solution.py:28
  14.9 5.2 %collective-permute-start.2 = (f32[8,256]{1,0:T(8,128)S(1)}, f32[8,256]{1,0:T(8,128)S(1)}, u32[]{:S(2)}, u32[]{:S(2)}) collective-permute-start(f32[8,256]{1,0:T(8,128)S(1)} %get-tuple-element.56.logs), channel_id=1, source_target_pairs={{28,0},{0,4},{4,8},{8,12},{12,16},{16,20},{20,24},{24,28},{29,1},{... | collective-permute-start | bytes 24584 | tf_op jit(solution)/shard_map/ppermute | solution.py:28
  37.7 11.6 %all-to-all-start.1 = ((bf16[32,24,128]{2,1,0:T(8,128)(2,1)}), bf16[32,24,128]{2,1,0:T(8,128)(2,1)S(1)}, u32[]{:S(2)}, u32[]{:S(2)}) async-start(bf16[32,24,128]{2,1,0:T(8,128)(2,1)} %shard_map.97), calls=%async_computation.1 | async-start | bytes 393216 | tf_op jit(solution)/shard_map/all_to_all | solution.py:317

commit v9 on v5

--- a/solution.py
+++ b/solution.py
@@ -221,14 +221,16 @@
 
 
 def near_score_body(
-    queries, passages, valid, embed, turned, sent, log0, log2, far0,
-    powers, totals, scores, logs, back, tops, grad_sim,
+    queries, passages, valid, embed, sent, log0, log2, powers, totals, scores, logs, tops
 ):
     score_block(queries, passages, valid, embed, sent, powers, totals, scores, tops)
     log = log_sum(scores[...])
-    other = log2[0:1, :]
-    logs[...] = stack_rows(logs.shape, (log0[0:1, :], log, other, far0[0:1, :]))
-    tail = split(log) + split(other)
+    logs[...] = stack_rows(logs.shape, (log0[0:1, :], log, log2[0:1, :]))
+
+
+def near_grad_body(passages, turned, sent, powers, totals, scores, logs, back, grad_sim):
+    log = logs[1:2, :]
+    tail = split(log) + split(logs[2:3, :])
     send_back(passages, turned, sent, powers, totals, scores, log, tail, back, grad_sim)
 
 
@@ -238,19 +240,31 @@
     return high + (middle + low)
 
 
+def far_passage_body(
+    passages, powers, totals, scores, sent, logs, logs1, far0, back2, grad, partial, grad_sim
+):
+    rows = powers.shape[1]
+    third = joined(back2, grad.shape[1], 0)
+    partial[...] = stack_rows(partial.shape, (log_add((logs[0:1, :], third)), third))
+    total = log_add((far0[0:1, :], logs1[1:2, :], logs[2:3, :]))
+    dscore = loss_scale * jnp.exp(scores[...] - total)
+    coefficient = outer_scale * dscore * sent_keep(sent, rows) / totals[...]
+    fill_grad_sim(passages, coefficient, powers, grad_sim, 0)
+    grad[...] = dot32(grad_sim[...], sent[:rows, :])
+
+
 def grad_body(
     queries, passages, wanted, query_hidden, passage_hidden, turned,
     query_unit, query_inverse, passage_unit, passage_inverse,
-    powers0, powers1, powers2, totals0, totals1, totals2, scores0, scores1, scores2,
-    sent0, sent1, sent2, logs, logs1, back1, back2,
+    powers0, powers1, totals0, totals1, scores0, scores1, sent0, sent1, far_grad,
+    two_logs, logs, logs1, back1, back2,
     losses, query_pre_grad, passage_pre_grad, partial, grad_sim, query_rows,
 ):
     rows = powers0.shape[1]
     dim = turned.shape[0]
-    second, third = joined(back1, dim, 0), joined(back2, dim, 0)
-    total0 = log_add((logs[0:1, :], second, third))
+    second, third = joined(back1, dim, 0), two_logs[1:2, :]
+    total0 = log_add((two_logs[0:1, :], second))
     total1 = log_add((logs1[0:1, :], logs[1:2, :], joined(back1, dim, 3)))
-    total2 = log_add((logs[3:4, :], logs1[1:2, :], logs[2:3, :]))
     scores = scores0[...]
     onehot = lax.broadcasted_iota(jnp.int32, scores.shape, 0) == wanted[...]
     loss = total0 - jnp.sum(jnp.where(onehot, scores, 0.0), axis=0, keepdims=True)
@@ -261,7 +275,6 @@
     for block, (total, query, powers, totals, scores) in enumerate((
         (total0, sent0, powers0, totals0, scores0),
         (total1, sent1, powers1, totals1, scores1),
-        (total2, sent2, powers2, totals2, scores2),
     )):
         dscore = jnp.exp(scores[...] - total)
         if block == 0:
@@ -270,7 +283,7 @@
         fill_grad_sim(passages, coefficient, powers, grad_sim, block * rows)
         query_rows[block * rows : (block + 1) * rows, :] = query[:rows, :]
 
-    grad = dot32(grad_sim[...], query_rows[...])
+    grad = far_grad[...] + dot32(grad_sim[...], query_rows[...])
     pre = back_rows(grad, passage_unit[...], passage_inverse[...])
     passage_pre_grad[...] = pre
     both = dot32(pre.T, passage_hidden[...])
@@ -370,30 +383,46 @@
         trans=slots * rows,
     )
     back2 = shifted(back2, "batch", -2)
-    powers1, totals1, scores1, logs, back1 = call(
+    powers1, totals1, scores1, logs = call(
         functools.partial(near_score_body, queries, passages),
-        block_outs,
-        (vmem,) * 7,
-        (valid, embed, turned, sent1, log0, log2, far0),
-        scratch=(pairs, pltpu.VMEM((slots, rows), bf16)),
-        flops=4 * slots * dim * rows,
+        block_outs[:4],
+        (vmem,) * 5,
+        (valid, embed, sent1, log0, log2),
+        scratch=(pairs,),
+        flops=2 * slots * dim * rows,
         trans=slots * rows,
     )
+    logs1 = shifted(logs, "batch", 1)
+    back1 = call(
+        functools.partial(near_grad_body, passages),
+        block_outs[4:],
+        (vmem,) * 6,
+        (turned, sent1, powers1, totals1, scores1, logs),
+        scratch=(pltpu.VMEM((slots, rows), bf16),),
+        flops=2 * slots * dim * rows,
+    )[0]
     back1 = shifted(back1, "batch", -1)
-    logs1 = shifted(logs, "batch", 1)
+    far_grad, two_logs = call(
+        functools.partial(far_passage_body, passages),
+        (of((slots, dim), f32), of((8, rows), f32)),
+        (vmem,) * 8,
+        (powers2, totals2, scores2, sent2, logs, logs1, far0, back2),
+        scratch=(pltpu.VMEM((slots, rows), bf16),),
+        flops=20 * slots * dim * rows,
+    )
     losses, query_pre_grad, passage_pre_grad, partial = call(
         functools.partial(grad_body, queries, passages),
         (
             of((1, queries), f32), of((rows, dim), bf16), of((slots, dim), bf16),
             of((width, dim), bf16),
         ),
-        (vmem,) * 24,
+        (vmem,) * 22,
         (wanted, query_rows, passage_rows, turned,
          query_unit, query_inverse, passage_unit, passage_inverse,
-         powers0, powers1, powers2, totals0, totals1, totals2, scores0, scores1, scores2,
-         sent0, sent1, sent2, logs, logs1, back1, back2),
-        scratch=(pltpu.VMEM((slots, 3 * rows), bf16), pltpu.VMEM((3 * rows, dim), bf16)),
-        flops=8 * slots * dim * rows + 2 * (slots + rows) * width * dim,
+         powers0, powers1, totals0, totals1, scores0, scores1, sent0, sent1, far_grad,
+         two_logs, logs, logs1, back1, back2),
+        scratch=(pltpu.VMEM((slots, 2 * rows), bf16), pltpu.VMEM((2 * rows, dim), bf16)),
+        flops=6 * slots * dim * rows + 2 * (slots + rows) * width * dim,
     )
     grad_projection = mean_over_devices(partial)
     grad_query_hidden = dot32(query_pre_grad, weight, NT).astype(bf16)

time: 49.1 us -> 52 us (1.059)
  blocking collectives: 14.5 us -> 18.7 us
  waiting for transfers between devices: 11.2 us -> 8.41 us
  starting transfers between devices: 10.7 us -> 11.5 us
    all_to_all x1, blocking collectives: 14.5 us -> 18.7 us  [mean_over_devices(): pieces = lax.all_to_all(padded.reshape(devices, share, columns), axes, 0, 0)]
    ppermute x6, waiting for transfers between devices: 4.91 us -> 2.13 us  [shifted(): return lax.ppermute(block, axis, route)]
    ppermute x6, starting transfers between devices: 8.28 us -> 9.18 us  [shifted(): return lax.ppermute(block, axis, route)]
    pallas_call x6 -> x8, Pallas kernels: 8.19 us -> 8.66 us  [call(): pl.pallas_call(body, out_shape=tuple(outs), in_specs=list(in_specs), out_...]
  transfers between devices with their start and end apart: 7 -> 7, of which waited for: 3 -> 5; matrix products, arithmetic and copies ran while one was open for 6% -> 6% of each run, Pallas kernels for 8% -> 8%
where the time goes in v9:
time: 52 us; the launch traced here: 51.8 us
  blocking collectives  18.7 us (36%)
  starting transfers between devices  11.5 us (22%)
  Pallas kernels  8.66 us (17%)
  waiting for transfers between devices  8.41 us (16%)
  matrix products  2.95 us (6%)
  other arithmetic  0.78 us (2%)
  between operations  0.7 us (1%)
    all_to_all x1, blocking collectives, mean_over_devices(): pieces = lax.all_to_all(padded.reshape(devices, share, columns), axes, 0, 0)  18.7 us
    ppermute x6, starting transfers between devices, shifted(): return lax.ppermute(block, axis, route)  9.18 us
    pallas_call x8, Pallas kernels, call(): pl.pallas_call(body, out_shape=tuple(outs), in_specs=list(in_specs), out_...  8.66 us
    all_to_all x1, waiting for transfers between devices, mean_over_devices(): whole = lax.all_to_all(means, axes, 0, 0)  6.27 us
    dot_general x2, matrix products, dot32(): lax.dot_general(left, right, dims, preferred_element_type=jnp.float32)  2.95 us
    all_to_all x1, starting transfers between devices, mean_over_devices(): whole = lax.all_to_all(means, axes, 0, 0)  2.37 us
    ppermute x6, waiting for transfers between devices, shifted(): return lax.ppermute(block, axis, route)  2.13 us
  transfers between devices with their start and end apart: 7, of which 5 were waited for; matrix products, arithmetic and copies ran while one was open for 6% of the time, Pallas kernels for 8%

profile of v9, /device:TPU:1, one launch (start us, length us, event | category | flops | bytes accessed | tf_op | source)
XLA Modules:
  0.0 51.8 jit_solution(5620965139707567788)
XLA Ops:
  0.6 1.8 %shard_map.93 = (f32[256,128]{1,0:T(8,128)S(1)}, f32[256,128]{1,0:T(8,128)S(1)}, bf16[272,128]{1,0:T(8,128)(2,1)S(1)}, s32[16,256]{1,0:T(8,128)S(1)}, s32[1,256]...) custom-call(s32[8]{0:T(128)} %query_lengths_in.1, ...), custom_call_target="tpu_custom_call" | custom-call | flops 50331648 | bytes 5461096 | tf_op jit(solution)/shard_map/pallas_call | solution.py:38
  2.5 2.2 %collective-permute-start.1 = (bf16[272,128]{1,0:T(8,128)(2,1)S(1)}, bf16[272,128]{1,0:T(8,128)(2,1)S(1)}, u32[]{:S(2)}, u32[]{:S(2)}) collective-permute-start(bf16[272,128]{1,0:T(8,128)(2,1)S(1)} %get-tuple-element.40.sent.sent0), channel_id=1, source_target_pairs={{24,0},{28,4},{0,8},{4,12},{8,16},{12,20},{16,24},{20,28},{25,1},{... | collective-permute-start | bytes 208904 | tf_op jit(solution)/shard_map/ppermute | solution.py:28
  4.7 1.2 %collective-permute-start = (bf16[272,128]{1,0:T(8,128)(2,1)S(1)}, bf16[272,128]{1,0:T(8,128)(2,1)S(1)}, u32[]{:S(2)}, u32[]{:S(2)}) collective-permute-start(bf16[272,128]{1,0:T(8,128)(2,1)S(1)} %get-tuple-element.40.sent.sent0), channel_id=1, source_target_pairs={{28,0},{0,4},{4,8},{8,12},{12,16},{16,20},{20,24},{24,28},{29,1},{... | collective-permute-start | bytes 208904 | tf_op jit(solution)/shard_map/ppermute | solution.py:28
  5.9 1.5 %shard_map.94 = (f32[1280,128]{1,0:T(8,128)S(1)}, f32[1280,128]{1,0:T(8,128)S(1)}, bf16[1280,128]{1,0:T(8,128)(2,1)S(1)}, bf16[128,1280]{1,0:T(8,128)(2,1)S(1)},...) custom-call(s32[16,256]{1,0:T(8,128)S(1)} %get-tuple-element.38.valid, ...), custom_call_target="tpu_custom_call" | custom-call | flops 335544320 | bytes 5566464 | tf_op jit(solution)/shard_map/pallas_call | solution.py:38
  7.4 1.0 %collective-permute-done.1.sent = bf16[272,128]{1,0:T(8,128)(2,1)S(1)} collective-permute-done((bf16[272,128]{1,0:T(8,128)(2,1)S(1)}, bf16[272,128]{1,0:T(8,128)(2,1)S(1)}, u32[]{:S(2)}, u32[]{:S(2)}) %collective-permute-start.1) | collective-permute-done | bytes 69664 | tf_op jit(solution)/shard_map/ppermute | solution.py:28
  8.4 1.1 %shard_map.95 = (f32[1280,256]{1,0:T(8,128)S(1)}, f32[16,256]{1,0:T(8,128)S(1)}, f32[16,256]{1,0:T(8,128)S(1)}, f32[8,256]{1,0:T(8,128)S(1)}, bf16[144,256]{1,0:T(8,128)(2,1)S(1)}) custom-call(s32[16,256]{1,0:T(8,128)S(1)} %get-tuple-element.38.valid, bf16[1280,128]{1,0:T(8,128)(2,1)S(1)} %get-tuple-element.47.embed, ...), custom_call_target="tpu_custom_call" | custom-call | flops 167772160 | bytes 2166784 | tf_op jit(solution)/shard_map/pallas_call | solution.py:38
  9.5 1.5 %collective-permute-start.4 = (bf16[144,256]{1,0:T(8,128)(2,1)S(1)}, bf16[144,256]{1,0:T(8,128)(2,1)S(1)}, u32[]{:S(2)}, u32[]{:S(2)}) collective-permute-start(bf16[144,256]{1,0:T(8,128)(2,1)S(1)} %get-tuple-element.59), channel_id=1, source_target_pairs={{8,0},{12,4},{16,8},{20,12},{24,16},{28,20},{0,24},{4,28},{9,1},{1... | collective-permute-start | bytes 221192 | tf_op jit(solution)/shard_map/ppermute | solution.py:28
  11.0 0.0 collective-permute-start.3
  11.0 0.1 collective-permute-done.sent.sent1
  11.1 0.8 %shard_map.96 = (f32[1280,256]{1,0:T(8,128)S(1)}, f32[16,256]{1,0:T(8,128)S(1)}, f32[16,256]{1,0:T(8,128)S(1)}, f32[8,256]{1,0:T(8,128)S(1)}) custom-call(s32[16,256]{1,0:T(8,128)S(1)} %get-tuple-element.38.valid, bf16[1280,128]{1,0:T(8,128)(2,1)S(1)} %get-tuple-element.47.embed, bf16[272,128]{1,0:T(8,128)(2,1)S(1)} %collective-permute-done.sent.sent1, ...), custom_call_target="tpu_custom_call" | custom-call | flops 83886080 | bytes 1781760 | tf_op jit(solution)/shard_map/pallas_call | solution.py:38
  11.9 1.2 %collective-permute-start.2 = (f32[8,256]{1,0:T(8,128)S(1)}, f32[8,256]{1,0:T(8,128)S(1)}, u32[]{:S(2)}, u32[]{:S(2)}) collective-permute-start(f32[8,256]{1,0:T(8,128)S(1)} %get-tuple-element.58.logs), channel_id=1, source_target_pairs={{28,0},{0,4},{4,8},{8,12},{12,16},{16,20},{20,24},{24,28},{29,1},{... | collective-permute-start | bytes 24584 | tf_op jit(solution)/shard_map/ppermute | solution.py:28
  13.1 0.3 shard_map.98
  13.4 3.1 %collective-permute-start.5 = (bf16[144,256]{1,0:T(8,128)(2,1)S(1)}, bf16[144,256]{1,0:T(8,128)(2,1)S(1)}, u32[]{:S(2)}, u32[]{:S(2)}) collective-permute-start(bf16[144,256]{1,0:T(8,128)(2,1)S(1)} %shard_map.98), channel_id=1, source_target_pairs={{4,0},{8,4},{12,8},{16,12},{20,16},{24,20},{28,24},{0,28},{5,1},{9... | collective-permute-start | bytes 221192 | tf_op jit(solution)/shard_map/ppermute | solution.py:28
  16.5 0.0 collective-permute-done.3.far0
  16.5 0.7 %collective-permute-done.2.logs1 = f32[8,256]{1,0:T(8,128)S(1)} collective-permute-done((f32[8,256]{1,0:T(8,128)S(1)}, f32[8,256]{1,0:T(8,128)S(1)}, u32[]{:S(2)}, u32[]{:S(2)}) %collective-permute-start.2) | collective-permute-done | bytes 8224 | tf_op jit(solution)/shard_map/ppermute | solution.py:28
  17.1 0.0 collective-permute-done.4.back2
  17.1 0.3 shard_map.97
  17.5 0.4 collective-permute-done.5.back1
  17.9 2.1 %shard_map.99 = (f32[1,8]{1,0:T(1,128)}, bf16[256,128]{1,0:T(8,128)(2,1)S(1)}, bf16[1280,128]{1,0:T(8,128)(2,1)S(1)}, bf16[768,128]{1,0:T(8,128)(2,1)S(1)}) custom-call(s32[1,256]{1,0:T(1,128)S(1)} %get-tuple-element.35.wanted, bf16[256,768]{1,0:T(8,128)(2,1)S(1)} %get-tuple-element.36.query_hidden, ...), custom_call_target="tpu_custom_call" | custom-call | flops 553648128 | bytes 8504352 | tf_op jit(solution)/shard_map/pallas_call | solution.py:38
  19.9 18.7 %all_to_all.10.pieces = bf16[32,24,128]{2,1,0:T(8,128)(2,1)S(1)} all-to-all(bf16[32,24,128]{2,1,0:T(8,128)(2,1)S(1)} %bitcast.9), channel_id=1, replica_groups=mesh['batch'=8,'mp'=4] {'batch','mp'}, dimensions={0} | all-to-all | bytes 393216 | tf_op jit(solution)/shard_map/all_to_all | solution.py:312
  38.6 0.7 %shard_map.100 = bf16[32,24,128]{2,1,0:T(8,128)(2,1)} custom-call(bf16[32,24,128]{2,1,0:T(8,128)(2,1)S(1)} %all_to_all.10.pieces), custom_call_target="tpu_custom_call" | custom-call | bytes 393216 | tf_op jit(solution)/shard_map/pallas_call | solution.py:38
  39.4 2.4 %all-to-all-start.1 = ((bf16[32,24,128]{2,1,0:T(8,128)(2,1)}), bf16[32,24,128]{2,1,0:T(8,128)(2,1)S(1)}, u32[]{:S(2)}, u32[]{:S(2)}) async-start(bf16[32,24,128]{2,1,0:T(8,128)(2,1)} %shard_map.100), calls=%async_computation.1 | async-start | bytes 393216 | tf_op jit(solution)/shard_map/all_to_all | solution.py:319
  41.7 1.0 %convolution_convert_fusion.1 = bf16[256,768]{1,0:T(8,128)(2,1)} fusion(bf16[256,128]{1,0:T(8,128)(2,1)S(1)} %get-tuple-element.63, bf16[768,128]{1,0:T(8,128)(2,1)S(1)} %get-tuple-element.39.projection), kind=kOutput, calls=%fused_computation.1 | convolution fusion | flops 50528256 | bytes 655360 | tf_op jit(solution)/shard_map/dot_general | solution.py:32
  42.8 1.9 %convolution_convert_fusion = bf16[1280,768]{1,0:T(8,128)(2,1)} fusion(bf16[1280,128]{1,0:T(8,128)(2,1)S(1)} %get-tuple-element.64, bf16[768,128]{1,0:T(8,128)(2,1)S(1)} %get-tuple-element.39.projection), kind=kOutput, calls=%fused_computation | convolution fusion | flops 252641280 | bytes 2490368 | tf_op jit(solution)/shard_map/dot_general | solution.py:32
  44.7 6.3 %all-to-all-done.1 = bf16[32,24,128]{2,1,0:T(8,128)(2,1)S(1)} async-done(((bf16[32,24,128]{2,1,0:T(8,128)(2,1)}), bf16[32,24,128]{2,1,0:T(8,128)(2,1)S(1)}, u32[]{:S(2)}, u32[]{:S(2)}) %all-to-all-start.1) | async-done | bytes 196640 | tf_op jit(solution)/shard_map/all_to_all | solution.py:319
  51.0 0.8 %bitcast_convert_fusion = f32[768,128]{1,0:T(8,128)} fusion(bf16[32,24,128]{2,1,0:T(8,128)(2,1)S(1)} %all-to-all-done.1), kind=kLoop, calls=%fused_computation.2 | loop fusion | flops 98304 | bytes 589824 | tf_op jit(solution)/shard_map/convert_element_type | solution.py:320
Async XLA Ops:
  2.5 5.9 %collective-permute-start.1 = (bf16[272,128]{1,0:T(8,128)(2,1)S(1)}, bf16[272,128]{1,0:T(8,128)(2,1)S(1)}, u32[]{:S(2)}, u32[]{:S(2)}) collective-permute-start(bf16[272,128]{1,0:T(8,128)(2,1)S(1)} %get-tuple-element.40.sent.sent0), channel_id=1, source_target_pairs={{24,0},{28,4},{0,8},{4,12},{8,16},{12,20},{16,24},{20,28},{25,1},{... | collective-permute-start | bytes 208904 | tf_op jit(solution)/shard_map/ppermute | solution.py:28
  4.7 6.5 %collective-permute-start = (bf16[272,128]{1,0:T(8,128)(2,1)S(1)}, bf16[272,128]{1,0:T(8,128)(2,1)S(1)}, u32[]{:S(2)}, u32[]{:S(2)}) collective-permute-start(bf16[272,128]{1,0:T(8,128)(2,1)S(1)} %get-tuple-element.40.sent.sent0), channel_id=1, source_target_pairs={{28,0},{0,4},{4,8},{8,12},{12,16},{16,20},{20,24},{24,28},{29,1},{... | collective-permute-start | bytes 208904 | tf_op jit(solution)/shard_map/ppermute | solution.py:28
  9.5 7.6 %collective-permute-start.4 = (bf16[144,256]{1,0:T(8,128)(2,1)S(1)}, bf16[144,256]{1,0:T(8,128)(2,1)S(1)}, u32[]{:S(2)}, u32[]{:S(2)}) collective-permute-start(bf16[144,256]{1,0:T(8,128)(2,1)S(1)} %get-tuple-element.59), channel_id=1, source_target_pairs={{8,0},{12,4},{16,8},{20,12},{24,16},{28,20},{0,24},{4,28},{9,1},{1... | collective-permute-start | bytes 221192 | tf_op jit(solution)/shard_map/ppermute | solution.py:28
  11.0 5.4 %collective-permute-start.3 = (f32[8,256]{1,0:T(8,128)S(1)}, f32[8,256]{1,0:T(8,128)S(1)}, u32[]{:S(2)}, u32[]{:S(2)}) collective-permute-start(f32[8,256]{1,0:T(8,128)S(1)} %get-tuple-element.48.log0), channel_id=1, source_target_pairs={{24,0},{28,4},{0,8},{4,12},{8,16},{12,20},{16,24},{20,28},{25,1},{... | collective-permute-start | bytes 24584 | tf_op jit(solution)/shard_map/ppermute | solution.py:28
  11.9 5.3 %collective-permute-start.2 = (f32[8,256]{1,0:T(8,128)S(1)}, f32[8,256]{1,0:T(8,128)S(1)}, u32[]{:S(2)}, u32[]{:S(2)}) collective-permute-start(f32[8,256]{1,0:T(8,128)S(1)} %get-tuple-element.58.logs), channel_id=1, source_target_pairs={{28,0},{0,4},{4,8},{8,12},{12,16},{16,20},{20,24},{24,28},{29,1},{... | collective-permute-start | bytes 24584 | tf_op jit(solution)/shard_map/ppermute | solution.py:28
  13.4 4.5 %collective-permute-start.5 = (bf16[144,256]{1,0:T(8,128)(2,1)S(1)}, bf16[144,256]{1,0:T(8,128)(2,1)S(1)}, u32[]{:S(2)}, u32[]{:S(2)}) collective-permute-start(bf16[144,256]{1,0:T(8,128)(2,1)S(1)} %shard_map.98), channel_id=1, source_target_pairs={{4,0},{8,4},{12,8},{16,12},{20,16},{24,20},{28,24},{0,28},{5,1},{9... | collective-permute-start | bytes 221192 | tf_op jit(solution)/shard_map/ppermute | solution.py:28
  39.4 11.6 %all-to-all-start.1 = ((bf16[32,24,128]{2,1,0:T(8,128)(2,1)}), bf16[32,24,128]{2,1,0:T(8,128)(2,1)S(1)}, u32[]{:S(2)}, u32[]{:S(2)}) async-start(bf16[32,24,128]{2,1,0:T(8,128)(2,1)} %shard_map.100), calls=%async_computation.1 | async-start | bytes 393216 | tf_op jit(solution)/shard_map/all_to_all | solution.py:319

commit v10 on v5

--- a/solution.py
+++ b/solution.py
@@ -238,12 +238,19 @@
     return high + (middle + low)
 
 
+def turn_body(query_hidden, passage_hidden, out):
+    rows = query_hidden.shape[0]
+    out[:, :rows] = query_hidden[...].T
+    out[:, rows:] = passage_hidden[...].T
+
+
 def grad_body(
-    queries, passages, wanted, query_hidden, passage_hidden, turned,
+    queries, passages, wanted, hidden_turned, turned,
     query_unit, query_inverse, passage_unit, passage_inverse,
     powers0, powers1, powers2, totals0, totals1, totals2, scores0, scores1, scores2,
     sent0, sent1, sent2, logs, logs1, back1, back2,
-    losses, query_pre_grad, passage_pre_grad, partial, grad_sim, query_rows,
+    all_logs, wanted_logs, query_pre_grad, passage_pre_grad, partial,
+    grad_sim, query_rows, pre_rows,
 ):
     rows = powers0.shape[1]
     dim = turned.shape[0]
@@ -253,10 +260,13 @@
     total2 = log_add((logs[3:4, :], logs1[1:2, :], logs[2:3, :]))
     scores = scores0[...]
     onehot = lax.broadcasted_iota(jnp.int32, scores.shape, 0) == wanted[...]
-    loss = total0 - jnp.sum(jnp.where(onehot, scores, 0.0), axis=0, keepdims=True)
+    wanted_score = jnp.sum(jnp.where(onehot, scores, 0.0), axis=0, keepdims=True)
     pick = lax.broadcasted_iota(jnp.int32, (rows, LANES), 1) * (rows // queries)
     pick = (pick == lax.broadcasted_iota(jnp.int32, (rows, LANES), 0)).astype(jnp.bfloat16)
-    losses[...] = sum(dot32(part, pick) for part in split(loss))[:, :queries]
+    lines = [part.astype(jnp.float32) for part in split(total0) + split(wanted_score)]
+    lines = dot32(stack_rows((ROWS, rows), lines).astype(jnp.bfloat16), pick)[:, :queries]
+    all_logs[...] = lines[0:1] + (lines[1:2] + lines[2:3])
+    wanted_logs[...] = lines[3:4] + (lines[4:5] + lines[5:6])
 
     for block, (total, query, powers, totals, scores) in enumerate((
         (total0, sent0, powers0, totals0, scores0),
@@ -273,14 +283,14 @@
     grad = dot32(grad_sim[...], query_rows[...])
     pre = back_rows(grad, passage_unit[...], passage_inverse[...])
     passage_pre_grad[...] = pre
-    both = dot32(pre.T, passage_hidden[...])
+    pre_rows[rows:, :] = pre
     to_query = dot32(turned[...], grad_sim[:, :rows])
     to_query += back1[:dim, :].astype(jnp.float32) * jnp.exp(second - total0)
     to_query += back2[:dim, :].astype(jnp.float32) * jnp.exp(third - total0)
     pre = back_rows(to_query.T, query_unit[...], query_inverse[...])
     query_pre_grad[...] = pre
-    both += dot32(pre.T, query_hidden[...])
-    partial[...] = both.T.astype(jnp.bfloat16)
+    pre_rows[:rows, :] = pre
+    partial[...] = dot32(hidden_turned[...], pre_rows[...]).astype(jnp.bfloat16)
 
 
 def sum_body(scale, copies, pieces, out):
@@ -381,24 +391,36 @@
     )
     back1 = shifted(back1, "batch", -1)
     logs1 = shifted(logs, "batch", 1)
-    losses, query_pre_grad, passage_pre_grad, partial = call(
+    hidden_turned = call(
+        turn_body,
+        (of((width, rows + slots), bf16),),
+        (vmem,) * 2,
+        (query_rows, passage_rows),
+        flops=500 * slots * width,
+    )[0]
+    all_logs, wanted_logs, query_pre_grad, passage_pre_grad, partial = call(
         functools.partial(grad_body, queries, passages),
         (
-            of((1, queries), f32), of((rows, dim), bf16), of((slots, dim), bf16),
+            of((1, queries), f32), of((1, queries), f32), of((rows, dim), bf16),
+            of((slots, dim), bf16),
             of((width, dim), bf16),
         ),
-        (vmem,) * 24,
-        (wanted, query_rows, passage_rows, turned,
+        (vmem,) * 23,
+        (wanted, hidden_turned, turned,
          query_unit, query_inverse, passage_unit, passage_inverse,
          powers0, powers1, powers2, totals0, totals1, totals2, scores0, scores1, scores2,
          sent0, sent1, sent2, logs, logs1, back1, back2),
-        scratch=(pltpu.VMEM((slots, 3 * rows), bf16), pltpu.VMEM((3 * rows, dim), bf16)),
+        scratch=(
+            pltpu.VMEM((slots, 3 * rows), bf16),
+            pltpu.VMEM((3 * rows, dim), bf16),
+            pltpu.VMEM((rows + slots, dim), bf16),
+        ),
         flops=8 * slots * dim * rows + 2 * (slots + rows) * width * dim,
     )
     grad_projection = mean_over_devices(partial)
     grad_query_hidden = dot32(query_pre_grad, weight, NT).astype(bf16)
     grad_passage_hidden = dot32(passage_pre_grad, weight, NT).astype(bf16)
-    losses = losses.reshape(queries)
+    losses = (all_logs - wanted_logs).reshape(queries)
     return (losses, grad_query_hidden, grad_passage_hidden, grad_projection)
 
 

time: 49.1 us -> 50.7 us (1.033)
  blocking collectives: 14.5 us -> 0 us
  waiting for transfers between devices: 11.2 us -> 19.3 us
  starting transfers between devices: 10.7 us -> 16.4 us
  Pallas kernels: 8.19 us -> 9.74 us
  other arithmetic: 0.78 us -> 1.3 us
    all_to_all x1 -> x0, blocking collectives: 14.5 us -> none  [mean_over_devices(): pieces = lax.all_to_all(padded.reshape(devices, share, columns), axes, 0, 0)]
    all_to_all x0 -> x1, waiting for transfers between devices: none -> 8.36 us  [mean_over_devices(): pieces = lax.all_to_all(padded.reshape(devices, share, columns), axes, 0, 0)]
    all_to_all x0 -> x1, starting transfers between devices: none -> 5.85 us  [mean_over_devices(): pieces = lax.all_to_all(padded.reshape(devices, share, columns), axes, 0, 0)]
    pallas_call x6 -> x7, Pallas kernels: 8.19 us -> 9.74 us  [call(): pl.pallas_call(body, out_shape=tuple(outs), in_specs=list(in_specs), out_...]
    ppermute x6, waiting for transfers between devices: 4.91 us -> 4.26 us  [shifted(): return lax.ppermute(block, axis, route)]
    reshape x0 -> x1, other arithmetic: none -> 0.51 us  [per_device(): losses = (all_logs - wanted_logs).reshape(queries)]
  transfers between devices with their start and end apart: 7 -> 8, of which waited for: 3 -> 4; matrix products, arithmetic and copies ran while one was open for 6% -> 7% of each run, Pallas kernels for 8% -> 9%
where the time goes in v10:
time: 50.7 us; the launch traced here: 50.5 us
  waiting for transfers between devices  19.3 us (38%)
  starting transfers between devices  16.4 us (32%)
  Pallas kernels  9.74 us (19%)
  matrix products  2.96 us (6%)
  other arithmetic  1.3 us (3%)
  between operations  0.7 us (1%)
    pallas_call x7, Pallas kernels, call(): pl.pallas_call(body, out_shape=tuple(outs), in_specs=list(in_specs), out_...  9.74 us
    all_to_all x1, waiting for transfers between devices, mean_over_devices(): pieces = lax.all_to_all(padded.reshape(devices, share, columns), axes, 0, 0)  8.36 us
    ppermute x6, starting transfers between devices, shifted(): return lax.ppermute(block, axis, route)  8.28 us
    all_to_all x1, waiting for transfers between devices, mean_over_devices(): whole = lax.all_to_all(means, axes, 0, 0)  6.71 us
    all_to_all x1, starting transfers between devices, mean_over_devices(): pieces = lax.all_to_all(padded.reshape(devices, share, columns), axes, 0, 0)  5.85 us
    ppermute x6, waiting for transfers between devices, shifted(): return lax.ppermute(block, axis, route)  4.26 us
    dot_general x2, matrix products, dot32(): lax.dot_general(left, right, dims, preferred_element_type=jnp.float32)  2.96 us
    all_to_all x1, starting transfers between devices, mean_over_devices(): whole = lax.all_to_all(means, axes, 0, 0)  2.32 us
  transfers between devices with their start and end apart: 8, of which 4 were waited for; matrix products, arithmetic and copies ran while one was open for 7% of the time, Pallas kernels for 9%

profile of v10, /device:TPU:1, one launch (start us, length us, event | category | flops | bytes accessed | tf_op | source)
XLA Modules:
  0.0 50.5 jit_solution(4930803496682789017)
XLA Ops:
  0.6 1.8 %shard_map.93 = (f32[256,128]{1,0:T(8,128)S(1)}, f32[256,128]{1,0:T(8,128)S(1)}, bf16[272,128]{1,0:T(8,128)(2,1)S(1)}, s32[16,256]{1,0:T(8,128)S(1)}, s32[1,256]...) custom-call(s32[8]{0:T(128)} %query_lengths_in.1, ...), custom_call_target="tpu_custom_call" | custom-call | flops 50331648 | bytes 5461096 | tf_op jit(solution)/shard_map/pallas_call | solution.py:38
  2.5 2.2 %collective-permute-start.1 = (bf16[272,128]{1,0:T(8,128)(2,1)S(1)}, bf16[272,128]{1,0:T(8,128)(2,1)S(1)}, u32[]{:S(2)}, u32[]{:S(2)}) collective-permute-start(bf16[272,128]{1,0:T(8,128)(2,1)S(1)} %get-tuple-element.40.sent.sent0), channel_id=1, source_target_pairs={{24,0},{28,4},{0,8},{4,12},{8,16},{12,20},{16,24},{20,28},{25,1},{... | collective-permute-start | bytes 208904 | tf_op jit(solution)/shard_map/ppermute | solution.py:28
  4.7 1.2 %collective-permute-start = (bf16[272,128]{1,0:T(8,128)(2,1)S(1)}, bf16[272,128]{1,0:T(8,128)(2,1)S(1)}, u32[]{:S(2)}, u32[]{:S(2)}) collective-permute-start(bf16[272,128]{1,0:T(8,128)(2,1)S(1)} %get-tuple-element.40.sent.sent0), channel_id=1, source_target_pairs={{28,0},{0,4},{4,8},{8,12},{12,16},{16,20},{20,24},{24,28},{29,1},{... | collective-permute-start | bytes 208904 | tf_op jit(solution)/shard_map/ppermute | solution.py:28
  5.9 1.5 %shard_map.95 = (f32[1280,128]{1,0:T(8,128)S(1)}, f32[1280,128]{1,0:T(8,128)S(1)}, bf16[1280,128]{1,0:T(8,128)(2,1)S(1)}, bf16[128,1280]{1,0:T(8,128)(2,1)S(1)},...) custom-call(s32[16,256]{1,0:T(8,128)S(1)} %get-tuple-element.38.valid, ...), custom_call_target="tpu_custom_call" | custom-call | flops 335544320 | bytes 5566464 | tf_op jit(solution)/shard_map/pallas_call | solution.py:38
  7.4 1.3 %collective-permute-start.2 = (f32[8,256]{1,0:T(8,128)S(1)}, f32[8,256]{1,0:T(8,128)S(1)}, u32[]{:S(2)}, u32[]{:S(2)}) collective-permute-start(f32[8,256]{1,0:T(8,128)S(1)} %get-tuple-element.48.log0), channel_id=1, source_target_pairs={{24,0},{28,4},{0,8},{4,12},{8,16},{12,20},{16,24},{20,28},{25,1},{... | collective-permute-start | bytes 24584 | tf_op jit(solution)/shard_map/ppermute | solution.py:28
  8.8 0.0 collective-permute-done.1.sent.sent2
  8.8 1.1 %shard_map.96 = (f32[1280,256]{1,0:T(8,128)S(1)}, f32[16,256]{1,0:T(8,128)S(1)}, f32[16,256]{1,0:T(8,128)S(1)}, f32[8,256]{1,0:T(8,128)S(1)}, bf16[144,256]{1,0:T(8,128)(2,1)S(1)}) custom-call(s32[16,256]{1,0:T(8,128)S(1)} %get-tuple-element.38.valid, bf16[1280,128]{1,0:T(8,128)(2,1)S(1)} %get-tuple-element.47.embed, ...), custom_call_target="tpu_custom_call" | custom-call | flops 167772160 | bytes 2166784 | tf_op jit(solution)/shard_map/pallas_call | solution.py:38
  9.9 2.0 %collective-permute-start.5 = (bf16[144,256]{1,0:T(8,128)(2,1)S(1)}, bf16[144,256]{1,0:T(8,128)(2,1)S(1)}, u32[]{:S(2)}, u32[]{:S(2)}) collective-permute-start(bf16[144,256]{1,0:T(8,128)(2,1)S(1)} %get-tuple-element.60), channel_id=1, source_target_pairs={{8,0},{12,4},{16,8},{20,12},{24,16},{28,20},{0,24},{4,28},{9,1},{1... | collective-permute-start | bytes 221192 | tf_op jit(solution)/shard_map/ppermute | solution.py:28
  11.9 0.2 collective-permute-done.2.far0
  12.1 0.0 collective-permute-done.sent.sent1
  12.1 1.1 %shard_map.97 = (f32[1280,256]{1,0:T(8,128)S(1)}, f32[16,256]{1,0:T(8,128)S(1)}, f32[16,256]{1,0:T(8,128)S(1)}, f32[8,256]{1,0:T(8,128)S(1)}, bf16[144,256]{1,0:T(8,128)(2,1)S(1)}) custom-call(s32[16,256]{1,0:T(8,128)S(1)} %get-tuple-element.38.valid, bf16[1280,128]{1,0:T(8,128)(2,1)S(1)} %get-tuple-element.47.embed, ...), custom_call_target="tpu_custom_call" | custom-call | flops 167772160 | bytes 2191360 | tf_op jit(solution)/shard_map/pallas_call | solution.py:38
  13.2 1.1 %collective-permute-start.4 = (bf16[144,256]{1,0:T(8,128)(2,1)S(1)}, bf16[144,256]{1,0:T(8,128)(2,1)S(1)}, u32[]{:S(2)}, u32[]{:S(2)}) collective-permute-start(bf16[144,256]{1,0:T(8,128)(2,1)S(1)} %get-tuple-element.59), channel_id=1, source_target_pairs={{4,0},{8,4},{12,8},{16,12},{20,16},{24,20},{28,24},{0,28},{5,1},{9... | collective-permute-start | bytes 221192 | tf_op jit(solution)/shard_map/ppermute | solution.py:28
  14.2 0.5 collective-permute-start.3
  14.7 0.7 %shard_map.94.hidden_turned = bf16[768,1536]{1,0:T(8,128)(2,1)S(1)} custom-call(bf16[256,768]{1,0:T(8,128)(2,1)S(1)} %get-tuple-element.36.query_hidden, bf16[1280,768]{1,0:T(8,128)(2,1)S(1)} %get-tuple-element.37.passage_hidden.hidden), custom_call_target="tpu_custom_call" | custom-call | flops 491520000 | bytes 4718592 | tf_op jit(solution)/shard_map/pallas_call | solution.py:38
  15.3 4.1 %collective-permute-done.3.logs1 = f32[8,256]{1,0:T(8,128)S(1)} collective-permute-done((f32[8,256]{1,0:T(8,128)S(1)}, f32[8,256]{1,0:T(8,128)S(1)}, u32[]{:S(2)}, u32[]{:S(2)}) %collective-permute-start.3) | collective-permute-done | bytes 8224 | tf_op jit(solution)/shard_map/ppermute | solution.py:28
  19.4 0.0 collective-permute-done.5.back2
  19.4 0.0 collective-permute-done.4.back1
  19.4 2.8 %shard_map.98 = (f32[1,8]{1,0:T(1,128)S(1)}, f32[1,8]{1,0:T(1,128)S(1)}, bf16[256,128]{1,0:T(8,128)(2,1)S(1)}, bf16[1280,128]{1,0:T(8,128)(2,1)S(1)}, bf16[768,128]{1,0:T(8,128)(2,1)}) custom-call(s32[1,256]{1,0:T(1,128)S(1)} %get-tuple-element.35.wanted, bf16[768,1536]{1,0:T(8,128)(2,1)S(1)} %shard_map.94.hidden_turned, ...), custom_call_target="tpu_custom_call" | custom-call | flops 637534208 | bytes 9253952 | tf_op jit(solution)/shard_map/pallas_call | solution.py:38
  22.2 5.8 %all-to-all-start = ((bf16[32,24,128]{2,1,0:T(8,128)(2,1)}), bf16[32,24,128]{2,1,0:T(8,128)(2,1)S(1)}, u32[]{:S(2)}, u32[]{:S(2)}) async-start(bf16[32,24,128]{2,1,0:T(8,128)(2,1)} %bitcast.1), calls=%async_computation | async-start | bytes 393216 | tf_op jit(solution)/shard_map/all_to_all | solution.py:309
  28.1 1.0 %convolution_convert_fusion.1 = bf16[256,768]{1,0:T(8,128)(2,1)} fusion(bf16[256,128]{1,0:T(8,128)(2,1)S(1)} %get-tuple-element.63, bf16[768,128]{1,0:T(8,128)(2,1)S(1)} %get-tuple-element.39.projection), kind=kOutput, calls=%fused_computation.1 | convolution fusion | flops 50528256 | bytes 655360 | tf_op jit(solution)/shard_map/dot_general | solution.py:32
  29.1 8.4 %all-to-all-done.pieces = bf16[32,24,128]{2,1,0:T(8,128)(2,1)S(1)} async-done(((bf16[32,24,128]{2,1,0:T(8,128)(2,1)}), bf16[32,24,128]{2,1,0:T(8,128)(2,1)S(1)}, u32[]{:S(2)}, u32[]{:S(2)}) %all-to-all-start) | async-done | bytes 196640 | tf_op jit(solution)/shard_map/all_to_all | solution.py:309
  37.5 0.7 %shard_map.99 = bf16[32,24,128]{2,1,0:T(8,128)(2,1)} custom-call(bf16[32,24,128]{2,1,0:T(8,128)(2,1)S(1)} %all-to-all-done.pieces), custom_call_target="tpu_custom_call" | custom-call | bytes 393216 | tf_op jit(solution)/shard_map/pallas_call | solution.py:38
  38.2 2.3 %all-to-all-start.1 = ((bf16[32,24,128]{2,1,0:T(8,128)(2,1)}), bf16[32,24,128]{2,1,0:T(8,128)(2,1)S(1)}, u32[]{:S(2)}, u32[]{:S(2)}) async-start(bf16[32,24,128]{2,1,0:T(8,128)(2,1)} %shard_map.99), calls=%async_computation.1 | async-start | bytes 393216 | tf_op jit(solution)/shard_map/all_to_all | solution.py:316
  40.5 0.5 %subtract_bitcast_fusion = f32[8]{0:T(128)} fusion(f32[1,8]{1,0:T(1,128)S(1)} %get-tuple-element.61, f32[1,8]{1,0:T(1,128)S(1)} %get-tuple-element.62), kind=kLoop, calls=%fused_computation.3 | loop fusion | flops 8 | bytes 96 | tf_op jit(solution)/shard_map/reshape | solution.py:423
  41.0 1.9 %convolution_convert_fusion = bf16[1280,768]{1,0:T(8,128)(2,1)} fusion(bf16[1280,128]{1,0:T(8,128)(2,1)S(1)} %get-tuple-element.64, bf16[768,128]{1,0:T(8,128)(2,1)S(1)} %get-tuple-element.39.projection), kind=kOutput, calls=%fused_computation | convolution fusion | flops 252641280 | bytes 2490368 | tf_op jit(solution)/shard_map/dot_general | solution.py:32
  43.0 6.7 %all-to-all-done.1 = bf16[32,24,128]{2,1,0:T(8,128)(2,1)S(1)} async-done(((bf16[32,24,128]{2,1,0:T(8,128)(2,1)}), bf16[32,24,128]{2,1,0:T(8,128)(2,1)S(1)}, u32[]{:S(2)}, u32[]{:S(2)}) %all-to-all-start.1) | async-done | bytes 196640 | tf_op jit(solution)/shard_map/all_to_all | solution.py:316
  49.7 0.8 %bitcast_convert_fusion = f32[768,128]{1,0:T(8,128)} fusion(bf16[32,24,128]{2,1,0:T(8,128)(2,1)S(1)} %all-to-all-done.1), kind=kLoop, calls=%fused_computation.2 | loop fusion | flops 98304 | bytes 589824 | tf_op jit(solution)/shard_map/convert_element_type | solution.py:317
Async XLA Ops:
  2.5 6.3 %collective-permute-start.1 = (bf16[272,128]{1,0:T(8,128)(2,1)S(1)}, bf16[272,128]{1,0:T(8,128)(2,1)S(1)}, u32[]{:S(2)}, u32[]{:S(2)}) collective-permute-start(bf16[272,128]{1,0:T(8,128)(2,1)S(1)} %get-tuple-element.40.sent.sent0), channel_id=1, source_target_pairs={{24,0},{28,4},{0,8},{4,12},{8,16},{12,20},{16,24},{20,28},{25,1},{... | collective-permute-start | bytes 208904 | tf_op jit(solution)/shard_map/ppermute | solution.py:28
  4.7 7.4 %collective-permute-start = (bf16[272,128]{1,0:T(8,128)(2,1)S(1)}, bf16[272,128]{1,0:T(8,128)(2,1)S(1)}, u32[]{:S(2)}, u32[]{:S(2)}) collective-permute-start(bf16[272,128]{1,0:T(8,128)(2,1)S(1)} %get-tuple-element.40.sent.sent0), channel_id=1, source_target_pairs={{28,0},{0,4},{4,8},{8,12},{12,16},{16,20},{20,24},{24,28},{29,1},{... | collective-permute-start | bytes 208904 | tf_op jit(solution)/shard_map/ppermute | solution.py:28
  7.4 4.6 %collective-permute-start.2 = (f32[8,256]{1,0:T(8,128)S(1)}, f32[8,256]{1,0:T(8,128)S(1)}, u32[]{:S(2)}, u32[]{:S(2)}) collective-permute-start(f32[8,256]{1,0:T(8,128)S(1)} %get-tuple-element.48.log0), channel_id=1, source_target_pairs={{24,0},{28,4},{0,8},{4,12},{8,16},{12,20},{16,24},{20,28},{25,1},{... | collective-permute-start | bytes 24584 | tf_op jit(solution)/shard_map/ppermute | solution.py:28
  9.9 9.6 %collective-permute-start.5 = (bf16[144,256]{1,0:T(8,128)(2,1)S(1)}, bf16[144,256]{1,0:T(8,128)(2,1)S(1)}, u32[]{:S(2)}, u32[]{:S(2)}) collective-permute-start(bf16[144,256]{1,0:T(8,128)(2,1)S(1)} %get-tuple-element.60), channel_id=1, source_target_pairs={{8,0},{12,4},{16,8},{20,12},{24,16},{28,20},{0,24},{4,28},{9,1},{1... | collective-permute-start | bytes 221192 | tf_op jit(solution)/shard_map/ppermute | solution.py:28
  13.2 6.3 %collective-permute-start.4 = (bf16[144,256]{1,0:T(8,128)(2,1)S(1)}, bf16[144,256]{1,0:T(8,128)(2,1)S(1)}, u32[]{:S(2)}, u32[]{:S(2)}) collective-permute-start(bf16[144,256]{1,0:T(8,128)(2,1)S(1)} %get-tuple-element.59), channel_id=1, source_target_pairs={{4,0},{8,4},{12,8},{16,12},{20,16},{24,20},{28,24},{0,28},{5,1},{9... | collective-permute-start | bytes 221192 | tf_op jit(solution)/shard_map/ppermute | solution.py:28
  14.2 5.2 %collective-permute-start.3 = (f32[8,256]{1,0:T(8,128)S(1)}, f32[8,256]{1,0:T(8,128)S(1)}, u32[]{:S(2)}, u32[]{:S(2)}) collective-permute-start(f32[8,256]{1,0:T(8,128)S(1)} %get-tuple-element.58.logs), channel_id=1, source_target_pairs={{28,0},{0,4},{4,8},{8,12},{12,16},{16,20},{20,24},{24,28},{29,1},{... | collective-permute-start | bytes 24584 | tf_op jit(solution)/shard_map/ppermute | solution.py:28
  22.2 15.2 %all-to-all-start = ((bf16[32,24,128]{2,1,0:T(8,128)(2,1)}), bf16[32,24,128]{2,1,0:T(8,128)(2,1)S(1)}, u32[]{:S(2)}, u32[]{:S(2)}) async-start(bf16[32,24,128]{2,1,0:T(8,128)(2,1)} %bitcast.1), calls=%async_computation | async-start | bytes 393216 | tf_op jit(solution)/shard_map/all_to_all | solution.py:309
  38.2 11.5 %all-to-all-start.1 = ((bf16[32,24,128]{2,1,0:T(8,128)(2,1)}), bf16[32,24,128]{2,1,0:T(8,128)(2,1)S(1)}, u32[]{:S(2)}, u32[]{:S(2)}) async-start(bf16[32,24,128]{2,1,0:T(8,128)(2,1)} %shard_map.99), calls=%async_computation.1 | async-start | bytes 393216 | tf_op jit(solution)/shard_map/all_to_all | solution.py:316

commit v11 on v5

--- a/solution.py
+++ b/solution.py
@@ -32,14 +32,14 @@
     return lax.dot_general(left, right, dims, preferred_element_type=jnp.float32)
 
 
-def call(body, outs, in_specs, args, scratch=(), flops=0, trans=0):
+def call(body, outs, in_specs, args, scratch=(), flops=0, trans=0, out_specs=None):
     moved = sum(a.size * a.dtype.itemsize for a in args)
     moved += sum(math.prod(o.shape) * jnp.dtype(o.dtype).itemsize for o in outs)
     return pl.pallas_call(
         body,
         out_shape=tuple(outs),
         in_specs=list(in_specs),
-        out_specs=tuple(vmem for _ in outs),
+        out_specs=out_specs or tuple(vmem for _ in outs),
         scratch_shapes=list(scratch),
         compiler_params=pltpu.CompilerParams(vmem_limit_bytes=24 * 2**20),
         cost_estimate=pl.CostEstimate(flops=flops, bytes_accessed=moved, transcendentals=trans),
@@ -243,7 +243,7 @@
     query_unit, query_inverse, passage_unit, passage_inverse,
     powers0, powers1, powers2, totals0, totals1, totals2, scores0, scores1, scores2,
     sent0, sent1, sent2, logs, logs1, back1, back2,
-    losses, query_pre_grad, passage_pre_grad, partial, grad_sim, query_rows,
+    all_logs, wanted_logs, query_pre_grad, passage_pre_grad, partial, grad_sim, query_rows,
 ):
     rows = powers0.shape[1]
     dim = turned.shape[0]
@@ -253,10 +253,13 @@
     total2 = log_add((logs[3:4, :], logs1[1:2, :], logs[2:3, :]))
     scores = scores0[...]
     onehot = lax.broadcasted_iota(jnp.int32, scores.shape, 0) == wanted[...]
-    loss = total0 - jnp.sum(jnp.where(onehot, scores, 0.0), axis=0, keepdims=True)
+    wanted_score = jnp.sum(jnp.where(onehot, scores, 0.0), axis=0, keepdims=True)
     pick = lax.broadcasted_iota(jnp.int32, (rows, LANES), 1) * (rows // queries)
     pick = (pick == lax.broadcasted_iota(jnp.int32, (rows, LANES), 0)).astype(jnp.bfloat16)
-    losses[...] = sum(dot32(part, pick) for part in split(loss))[:, :queries]
+    lines = [part.astype(jnp.float32) for part in split(total0) + split(wanted_score)]
+    lines = dot32(stack_rows((ROWS, rows), lines).astype(jnp.bfloat16), pick)[:, :queries]
+    all_logs[...] = lines[0:1] + (lines[1:2] + lines[2:3])
+    wanted_logs[...] = lines[3:4] + (lines[4:5] + lines[5:6])
 
     for block, (total, query, powers, totals, scores) in enumerate((
         (total0, sent0, powers0, totals0, scores0),
@@ -290,13 +293,26 @@
         out[copy] = total
 
 
-def mean_over_devices(partial):
+def cast_body(count, source, out, wide, sems):
+    size = source.shape[0] // count
+    copies = []
+    for piece in range(count):
+        part = pl.ds(piece * size, size)
+        wide[part, :] = source[part, :].astype(jnp.float32)
+        copies.append(pltpu.make_async_copy(wide.at[part], out.at[part], sems.at[piece]))
+        copies[-1].start()
+    for copy in copies:
+        copy.wait()
+
+
+def mean_over_devices(partial, later):
     axes = ("batch", "mp")
     devices = lax.axis_size("batch") * lax.axis_size("mp")
     rows, columns = partial.shape
     share = -(-rows // (devices * 8)) * 8
     padded = jnp.pad(partial, ((0, share * devices - rows), (0, 0)))
     pieces = lax.all_to_all(padded.reshape(devices, share, columns), axes, 0, 0)
+    pieces, later = lax.optimization_barrier((pieces, later))
     means = call(
         functools.partial(sum_body, 1.0 / devices, devices),
         (jax.ShapeDtypeStruct(pieces.shape, jnp.bfloat16),),
@@ -304,7 +320,17 @@
         (pieces,),
     )[0]
     whole = lax.all_to_all(means, axes, 0, 0)
-    return whole.reshape(devices * share, columns)[:rows].astype(jnp.float32)
+    whole = whole.reshape(devices * share, columns)[:rows]
+    count = 4 if rows % 64 == 0 else 1
+    whole = call(
+        functools.partial(cast_body, count),
+        (jax.ShapeDtypeStruct((rows, columns), jnp.float32),),
+        (vmem,),
+        (whole,),
+        scratch=(pltpu.VMEM((rows, columns), jnp.float32), pltpu.SemaphoreType.DMA((count,))),
+        out_specs=(hbm,),
+    )[0]
+    return whole, later
 
 
 def per_device(query_hidden, passage_hidden, projection, query_lengths, passage_lengths, positives):
@@ -381,10 +407,11 @@
     )
     back1 = shifted(back1, "batch", -1)
     logs1 = shifted(logs, "batch", 1)
-    losses, query_pre_grad, passage_pre_grad, partial = call(
+    all_logs, wanted_logs, query_pre_grad, passage_pre_grad, partial = call(
         functools.partial(grad_body, queries, passages),
         (
-            of((1, queries), f32), of((rows, dim), bf16), of((slots, dim), bf16),
+            of((1, queries), f32), of((1, queries), f32), of((rows, dim), bf16),
+            of((slots, dim), bf16),
             of((width, dim), bf16),
         ),
         (vmem,) * 24,
@@ -395,10 +422,12 @@
         scratch=(pltpu.VMEM((slots, 3 * rows), bf16), pltpu.VMEM((3 * rows, dim), bf16)),
         flops=8 * slots * dim * rows + 2 * (slots + rows) * width * dim,
     )
-    grad_projection = mean_over_devices(partial)
+    later = (query_pre_grad, passage_pre_grad, all_logs, wanted_logs)
+    grad_projection, later = mean_over_devices(partial, later)
+    query_pre_grad, passage_pre_grad, all_logs, wanted_logs = later
     grad_query_hidden = dot32(query_pre_grad, weight, NT).astype(bf16)
     grad_passage_hidden = dot32(passage_pre_grad, weight, NT).astype(bf16)
-    losses = losses.reshape(queries)
+    losses = (all_logs - wanted_logs).reshape(queries)
     return (losses, grad_query_hidden, grad_passage_hidden, grad_projection)
 
 

time: 49.1 us -> 49.1 us (level)
  Pallas kernels: 8.19 us -> 8.97 us
  waiting for transfers between devices: 11.2 us -> 10.7 us
    convert_element_type x1 -> x0, other arithmetic: 0.78 us -> none  [mean_over_devices(): return whole.reshape(devices * share, columns)[:rows].astype(jnp.float32)]
    pallas_call x6 -> x7, Pallas kernels: 8.19 us -> 8.97 us  [call(): pl.pallas_call(body, out_shape=tuple(outs), in_specs=list(in_specs), out_...]
    all_to_all x1, waiting for transfers between devices: 6.28 us -> 5.76 us  [mean_over_devices(): whole = lax.all_to_all(means, axes, 0, 0)]
    reshape x0 -> x1, other arithmetic: none -> 0.51 us  [per_device(): losses = (all_logs - wanted_logs).reshape(queries)]
  transfers between devices with their start and end apart: 7 -> 7, of which waited for: 3 -> 3; matrix products, arithmetic and copies ran while one was open for 6% -> 7% of each run, Pallas kernels for 8% -> 8%
where the time goes in v11:
time: 49.1 us; the launch traced here: 48.9 us
  blocking collectives  14.5 us (30%)
  starting transfers between devices  10.7 us (22%)
  waiting for transfers between devices  10.7 us (22%)
  Pallas kernels  8.97 us (18%)
  matrix products  2.95 us (6%)
  between operations  0.69 us (1%)
  other arithmetic  0.51 us (1%)
    all_to_all x1, blocking collectives, mean_over_devices(): pieces = lax.all_to_all(padded.reshape(devices, share, columns), axes, 0, 0)  14.5 us
    pallas_call x7, Pallas kernels, call(): pl.pallas_call(body, out_shape=tuple(outs), in_specs=list(in_specs), out_...  8.97 us
    ppermute x6, starting transfers between devices, shifted(): return lax.ppermute(block, axis, route)  8.28 us
    all_to_all x1, waiting for transfers between devices, mean_over_devices(): whole = lax.all_to_all(means, axes, 0, 0)  5.76 us
    ppermute x6, waiting for transfers between devices, shifted(): return lax.ppermute(block, axis, route)  4.91 us
    dot_general x2, matrix products, dot32(): lax.dot_general(left, right, dims, preferred_element_type=jnp.float32)  2.95 us
    all_to_all x1, starting transfers between devices, mean_over_devices(): whole = lax.all_to_all(means, axes, 0, 0)  2.37 us
  transfers between devices with their start and end apart: 7, of which 3 were waited for; matrix products, arithmetic and copies ran while one was open for 7% of the time, Pallas kernels for 8%

profile of v11, /device:TPU:1, one launch (start us, length us, event | category | flops | bytes accessed | tf_op | source)
XLA Modules:
  0.0 48.9 jit_solution(7884237409608636164)
XLA Ops:
  0.6 1.8 %shard_map.93 = (f32[256,128]{1,0:T(8,128)S(1)}, f32[256,128]{1,0:T(8,128)S(1)}, bf16[272,128]{1,0:T(8,128)(2,1)S(1)}, s32[16,256]{1,0:T(8,128)S(1)}, s32[1,256]...) custom-call(s32[8]{0:T(128)} %query_lengths_in.1, ...), custom_call_target="tpu_custom_call" | custom-call | flops 50331648 | bytes 5461096 | tf_op jit(solution)/shard_map/pallas_call | solution.py:38
  2.5 2.2 %collective-permute-start.1 = (bf16[272,128]{1,0:T(8,128)(2,1)S(1)}, bf16[272,128]{1,0:T(8,128)(2,1)S(1)}, u32[]{:S(2)}, u32[]{:S(2)}) collective-permute-start(bf16[272,128]{1,0:T(8,128)(2,1)S(1)} %get-tuple-element.45.sent.sent0), channel_id=1, source_target_pairs={{24,0},{28,4},{0,8},{4,12},{8,16},{12,20},{16,24},{20,28},{25,1},{... | collective-permute-start | bytes 208904 | tf_op jit(solution)/shard_map/ppermute | solution.py:28
  4.7 1.2 %collective-permute-start = (bf16[272,128]{1,0:T(8,128)(2,1)S(1)}, bf16[272,128]{1,0:T(8,128)(2,1)S(1)}, u32[]{:S(2)}, u32[]{:S(2)}) collective-permute-start(bf16[272,128]{1,0:T(8,128)(2,1)S(1)} %get-tuple-element.45.sent.sent0), channel_id=1, source_target_pairs={{28,0},{0,4},{4,8},{8,12},{12,16},{16,20},{20,24},{24,28},{29,1},{... | collective-permute-start | bytes 208904 | tf_op jit(solution)/shard_map/ppermute | solution.py:28
  5.9 1.5 %shard_map.94 = (f32[1280,128]{1,0:T(8,128)S(1)}, f32[1280,128]{1,0:T(8,128)S(1)}, bf16[1280,128]{1,0:T(8,128)(2,1)S(1)}, bf16[128,1280]{1,0:T(8,128)(2,1)S(1)},...) custom-call(s32[16,256]{1,0:T(8,128)S(1)} %get-tuple-element.43.valid, ...), custom_call_target="tpu_custom_call" | custom-call | flops 335544320 | bytes 5566464 | tf_op jit(solution)/shard_map/pallas_call | solution.py:38
  7.4 1.3 %collective-permute-start.2 = (f32[8,256]{1,0:T(8,128)S(1)}, f32[8,256]{1,0:T(8,128)S(1)}, u32[]{:S(2)}, u32[]{:S(2)}) collective-permute-start(f32[8,256]{1,0:T(8,128)S(1)} %get-tuple-element.53.log0), channel_id=1, source_target_pairs={{24,0},{28,4},{0,8},{4,12},{8,16},{12,20},{16,24},{20,28},{25,1},{... | collective-permute-start | bytes 24584 | tf_op jit(solution)/shard_map/ppermute | solution.py:28
  8.8 0.0 collective-permute-done.1.sent.sent2
  8.8 1.1 %shard_map.95 = (f32[1280,256]{1,0:T(8,128)S(1)}, f32[16,256]{1,0:T(8,128)S(1)}, f32[16,256]{1,0:T(8,128)S(1)}, f32[8,256]{1,0:T(8,128)S(1)}, bf16[144,256]{1,0:T(8,128)(2,1)S(1)}) custom-call(s32[16,256]{1,0:T(8,128)S(1)} %get-tuple-element.43.valid, bf16[1280,128]{1,0:T(8,128)(2,1)S(1)} %get-tuple-element.52.embed, ...), custom_call_target="tpu_custom_call" | custom-call | flops 167772160 | bytes 2166784 | tf_op jit(solution)/shard_map/pallas_call | solution.py:38
  9.9 2.0 %collective-permute-start.5 = (bf16[144,256]{1,0:T(8,128)(2,1)S(1)}, bf16[144,256]{1,0:T(8,128)(2,1)S(1)}, u32[]{:S(2)}, u32[]{:S(2)}) collective-permute-start(bf16[144,256]{1,0:T(8,128)(2,1)S(1)} %get-tuple-element.65), channel_id=1, source_target_pairs={{8,0},{12,4},{16,8},{20,12},{24,16},{28,20},{0,24},{4,28},{9,1},{1... | collective-permute-start | bytes 221192 | tf_op jit(solution)/shard_map/ppermute | solution.py:28
  11.9 0.2 collective-permute-done.2.far0
  12.1 0.0 collective-permute-done.sent.sent1
  12.1 1.1 %shard_map.96 = (f32[1280,256]{1,0:T(8,128)S(1)}, f32[16,256]{1,0:T(8,128)S(1)}, f32[16,256]{1,0:T(8,128)S(1)}, f32[8,256]{1,0:T(8,128)S(1)}, bf16[144,256]{1,0:T(8,128)(2,1)S(1)}) custom-call(s32[16,256]{1,0:T(8,128)S(1)} %get-tuple-element.43.valid, bf16[1280,128]{1,0:T(8,128)(2,1)S(1)} %get-tuple-element.52.embed, ...), custom_call_target="tpu_custom_call" | custom-call | flops 167772160 | bytes 2191360 | tf_op jit(solution)/shard_map/pallas_call | solution.py:38
  13.2 1.1 %collective-permute-start.4 = (bf16[144,256]{1,0:T(8,128)(2,1)S(1)}, bf16[144,256]{1,0:T(8,128)(2,1)S(1)}, u32[]{:S(2)}, u32[]{:S(2)}) collective-permute-start(bf16[144,256]{1,0:T(8,128)(2,1)S(1)} %get-tuple-element.64), channel_id=1, source_target_pairs={{4,0},{8,4},{12,8},{16,12},{20,16},{24,20},{28,24},{0,28},{5,1},{9... | collective-permute-start | bytes 221192 | tf_op jit(solution)/shard_map/ppermute | solution.py:28
  14.2 0.5 collective-permute-start.3
  14.7 4.7 %collective-permute-done.3.logs1 = f32[8,256]{1,0:T(8,128)S(1)} collective-permute-done((f32[8,256]{1,0:T(8,128)S(1)}, f32[8,256]{1,0:T(8,128)S(1)}, u32[]{:S(2)}, u32[]{:S(2)}) %collective-permute-start.3) | collective-permute-done | bytes 8224 | tf_op jit(solution)/shard_map/ppermute | solution.py:28
  19.4 0.0 collective-permute-done.5.back2
  19.4 0.0 collective-permute-done.4.back1
  19.4 1.9 %shard_map.97 = (f32[1,8]{1,0:T(1,128)S(1)}, f32[1,8]{1,0:T(1,128)S(1)}, bf16[256,128]{1,0:T(8,128)(2,1)S(1)}, bf16[1280,128]{1,0:T(8,128)(2,1)S(1)}, bf16[768,128]{1,0:T(8,128)(2,1)S(1)}) custom-call(s32[1,256]{1,0:T(1,128)S(1)} %get-tuple-element.40.wanted, bf16[256,768]{1,0:T(8,128)(2,1)S(1)} %get-tuple-element.41.query_hidden, ...), custom_call_target="tpu_custom_call" | custom-call | flops 637534208 | bytes 9253952 | tf_op jit(solution)/shard_map/pallas_call | solution.py:38
  21.3 14.5 %all_to_all.10.pieces = bf16[32,24,128]{2,1,0:T(8,128)(2,1)S(1)} all-to-all(bf16[32,24,128]{2,1,0:T(8,128)(2,1)S(1)} %bitcast.9), channel_id=1, replica_groups=mesh['batch'=8,'mp'=4] {'batch','mp'}, dimensions={0} | all-to-all | bytes 393216 | tf_op jit(solution)/shard_map/all_to_all | solution.py:314
  35.8 0.7 %shard_map.98 = bf16[32,24,128]{2,1,0:T(8,128)(2,1)} custom-call(bf16[32,24,128]{2,1,0:T(8,128)(2,1)S(1)} %all_to_all.10.pieces), custom_call_target="tpu_custom_call" | custom-call | bytes 393216 | tf_op jit(solution)/shard_map/pallas_call | solution.py:38
  36.5 2.4 %all-to-all-start.1 = ((bf16[32,24,128]{2,1,0:T(8,128)(2,1)}), bf16[32,24,128]{2,1,0:T(8,128)(2,1)S(1)}, u32[]{:S(2)}, u32[]{:S(2)}) async-start(bf16[32,24,128]{2,1,0:T(8,128)(2,1)} %shard_map.98), calls=%async_computation.1 | async-start | bytes 393216 | tf_op jit(solution)/shard_map/all_to_all | solution.py:322
  38.9 1.0 %convolution_convert_fusion.1 = bf16[256,768]{1,0:T(8,128)(2,1)} fusion(bf16[256,128]{1,0:T(8,128)(2,1)S(1)} %get-tuple-element.73, bf16[768,128]{1,0:T(8,128)(2,1)S(1)} %get-tuple-element.44.projection), kind=kOutput, calls=%fused_computation.1 | convolution fusion | flops 50528256 | bytes 655360 | tf_op jit(solution)/shard_map/dot_general | solution.py:32
  39.9 0.5 %subtract_bitcast_fusion = f32[8]{0:T(128)} fusion(f32[1,8]{1,0:T(1,128)S(1)} %get-tuple-element.71, f32[1,8]{1,0:T(1,128)S(1)} %get-tuple-element.72), kind=kLoop, calls=%fused_computation.2 | loop fusion | flops 8 | bytes 96 | tf_op jit(solution)/shard_map/reshape | solution.py:430
  40.4 1.9 %convolution_convert_fusion = bf16[1280,768]{1,0:T(8,128)(2,1)} fusion(bf16[1280,128]{1,0:T(8,128)(2,1)S(1)} %get-tuple-element.74, bf16[768,128]{1,0:T(8,128)(2,1)S(1)} %get-tuple-element.44.projection), kind=kOutput, calls=%fused_computation | convolution fusion | flops 252641280 | bytes 2490368 | tf_op jit(solution)/shard_map/dot_general | solution.py:32
  42.4 5.8 %all-to-all-done.1 = bf16[32,24,128]{2,1,0:T(8,128)(2,1)S(1)} async-done(((bf16[32,24,128]{2,1,0:T(8,128)(2,1)}), bf16[32,24,128]{2,1,0:T(8,128)(2,1)S(1)}, u32[]{:S(2)}, u32[]{:S(2)}) %all-to-all-start.1) | async-done | bytes 196640 | tf_op jit(solution)/shard_map/all_to_all | solution.py:322
  48.1 0.8 %shard_map.99 = f32[768,128]{1,0:T(8,128)} custom-call(bf16[768,128]{1,0:T(8,128)(2,1)S(1)} %bitcast.8), custom_call_target="tpu_custom_call" | custom-call | bytes 589824 | tf_op jit(solution)/shard_map/pallas_call | solution.py:38
Async XLA Ops:
  2.5 6.3 %collective-permute-start.1 = (bf16[272,128]{1,0:T(8,128)(2,1)S(1)}, bf16[272,128]{1,0:T(8,128)(2,1)S(1)}, u32[]{:S(2)}, u32[]{:S(2)}) collective-permute-start(bf16[272,128]{1,0:T(8,128)(2,1)S(1)} %get-tuple-element.45.sent.sent0), channel_id=1, source_target_pairs={{24,0},{28,4},{0,8},{4,12},{8,16},{12,20},{16,24},{20,28},{25,1},{... | collective-permute-start | bytes 208904 | tf_op jit(solution)/shard_map/ppermute | solution.py:28
  4.7 7.4 %collective-permute-start = (bf16[272,128]{1,0:T(8,128)(2,1)S(1)}, bf16[272,128]{1,0:T(8,128)(2,1)S(1)}, u32[]{:S(2)}, u32[]{:S(2)}) collective-permute-start(bf16[272,128]{1,0:T(8,128)(2,1)S(1)} %get-tuple-element.45.sent.sent0), channel_id=1, source_target_pairs={{28,0},{0,4},{4,8},{8,12},{12,16},{16,20},{20,24},{24,28},{29,1},{... | collective-permute-start | bytes 208904 | tf_op jit(solution)/shard_map/ppermute | solution.py:28
  7.4 4.6 %collective-permute-start.2 = (f32[8,256]{1,0:T(8,128)S(1)}, f32[8,256]{1,0:T(8,128)S(1)}, u32[]{:S(2)}, u32[]{:S(2)}) collective-permute-start(f32[8,256]{1,0:T(8,128)S(1)} %get-tuple-element.53.log0), channel_id=1, source_target_pairs={{24,0},{28,4},{0,8},{4,12},{8,16},{12,20},{16,24},{20,28},{25,1},{... | collective-permute-start | bytes 24584 | tf_op jit(solution)/shard_map/ppermute | solution.py:28
  9.9 9.6 %collective-permute-start.5 = (bf16[144,256]{1,0:T(8,128)(2,1)S(1)}, bf16[144,256]{1,0:T(8,128)(2,1)S(1)}, u32[]{:S(2)}, u32[]{:S(2)}) collective-permute-start(bf16[144,256]{1,0:T(8,128)(2,1)S(1)} %get-tuple-element.65), channel_id=1, source_target_pairs={{8,0},{12,4},{16,8},{20,12},{24,16},{28,20},{0,24},{4,28},{9,1},{1... | collective-permute-start | bytes 221192 | tf_op jit(solution)/shard_map/ppermute | solution.py:28
  13.2 6.3 %collective-permute-start.4 = (bf16[144,256]{1,0:T(8,128)(2,1)S(1)}, bf16[144,256]{1,0:T(8,128)(2,1)S(1)}, u32[]{:S(2)}, u32[]{:S(2)}) collective-permute-start(bf16[144,256]{1,0:T(8,128)(2,1)S(1)} %get-tuple-element.64), channel_id=1, source_target_pairs={{4,0},{8,4},{12,8},{16,12},{20,16},{24,20},{28,24},{0,28},{5,1},{9... | collective-permute-start | bytes 221192 | tf_op jit(solution)/shard_map/ppermute | solution.py:28
  14.2 5.2 %collective-permute-start.3 = (f32[8,256]{1,0:T(8,128)S(1)}, f32[8,256]{1,0:T(8,128)S(1)}, u32[]{:S(2)}, u32[]{:S(2)}) collective-permute-start(f32[8,256]{1,0:T(8,128)S(1)} %get-tuple-element.63.logs), channel_id=1, source_target_pairs={{28,0},{0,4},{4,8},{8,12},{12,16},{16,20},{20,24},{24,28},{29,1},{... | collective-permute-start | bytes 24584 | tf_op jit(solution)/shard_map/ppermute | solution.py:28
  36.5 11.6 %all-to-all-start.1 = ((bf16[32,24,128]{2,1,0:T(8,128)(2,1)}), bf16[32,24,128]{2,1,0:T(8,128)(2,1)S(1)}, u32[]{:S(2)}, u32[]{:S(2)}) async-start(bf16[32,24,128]{2,1,0:T(8,128)(2,1)} %shard_map.98), calls=%async_computation.1 | async-start | bytes 393216 | tf_op jit(solution)/shard_map/all_to_all | solution.py:322

commit v12 on v5

--- a/solution.py
+++ b/solution.py
@@ -114,9 +114,20 @@
     copies[5].wait()
 
 
+def sent_row(sent, rows, place):
+    tail = sent[rows:, :].astype(jnp.float32)
+    count = rows // LANES
+    return jnp.concatenate(
+        [tail[i : i + 1, :] for i in range(place * count, (place + 1) * count)], axis=1
+    )
+
+
 def sent_keep(sent, rows):
-    tail = sent[rows:, :].astype(jnp.float32)
-    return jnp.concatenate([tail[i : i + 1, :] for i in range(rows // LANES)], axis=1)
+    return sent_row(sent, rows, 0)
+
+
+def sent_log(sent, rows):
+    return sent_row(sent, rows, 1) + (sent_row(sent, rows, 2) + sent_row(sent, rows, 3))
 
 
 def split(values):
@@ -160,7 +171,7 @@
 
 def own_score_body(
     queries, passages, valid, hidden, projection, sent,
-    unit_out, inverse_out, embed_out, turned_out, powers, totals, scores, log_out, tops,
+    unit_out, inverse_out, embed_out, turned_out, powers, totals, scores, log_out, far_out, tops,
 ):
     unit, inverse = unit_rows(dot32(hidden[...], projection[...]))
     unit_out[...] = unit
@@ -168,7 +179,15 @@
     embed = unit.astype(jnp.bfloat16)
     embed_out[...] = embed
     score_block(queries, passages, valid, embed_out, sent, powers, totals, scores, tops)
-    log_out[...] = stack_rows(log_out.shape, (log_sum(scores[...]),))
+    log = log_sum(scores[...])
+    log_out[...] = stack_rows(log_out.shape, (log,))
+    rows = powers.shape[1]
+    far_out[:rows, :] = sent[:rows, :]
+    lines = [sent_keep(sent, rows)] + [part.astype(jnp.float32) for part in split(log)]
+    lines = [
+        line[:, i * LANES : (i + 1) * LANES] for line in lines for i in range(rows // LANES)
+    ]
+    far_out[rows:, :] = stack_rows((ROWS, LANES), lines).astype(jnp.bfloat16)
     turned_out[...] = embed.T
 
 
@@ -200,36 +219,38 @@
         )
 
 
-def send_back(passages, turned, sent, powers, totals, scores, log, tail, back, grad_sim):
-    dim, rows = turned.shape[0], powers.shape[1]
+def query_gradient(passages, turned, sent, powers, totals, scores, log, grad_sim):
+    rows = powers.shape[1]
     dscore = loss_scale * jnp.exp(scores[...] - log)
     coefficient = outer_scale * dscore * sent_keep(sent, rows) / totals[...]
     fill_grad_sim(passages, coefficient, powers, grad_sim, 0)
-    back[:dim, :] = dot32(turned[...], grad_sim[...]).astype(jnp.bfloat16)
-    tail = stack_rows((ROWS, rows), [part.astype(jnp.float32) for part in tail])
-    back[dim:, :] = tail.astype(jnp.bfloat16)
-
-
-def far_score_body(
-    queries, passages, valid, embed, turned, sent,
-    powers, totals, scores, log_out, back, tops, grad_sim,
+    return dot32(turned[...], grad_sim[...]).astype(jnp.bfloat16)
+
+
+def near_score_body(
+    queries, passages, valid, embed, turned, sent, log0,
+    powers, totals, scores, logs, near, tops, grad_sim,
 ):
     score_block(queries, passages, valid, embed, sent, powers, totals, scores, tops)
     log = log_sum(scores[...])
-    log_out[...] = stack_rows(log_out.shape, (log,))
-    send_back(passages, turned, sent, powers, totals, scores, log, split(log), back, grad_sim)
-
-
-def near_score_body(
-    queries, passages, valid, embed, turned, sent, log0, log2, far0,
-    powers, totals, scores, logs, back, tops, grad_sim,
+    logs[...] = stack_rows(logs.shape, (log0[0:1, :], log))
+    near[...] = query_gradient(passages, turned, sent, powers, totals, scores, log, grad_sim)
+
+
+def far_score_body(
+    queries, passages, valid, embed, turned, sent, near, logs,
+    powers, totals, scores, log_out, back2, back1, tops, grad_sim,
 ):
+    dim, rows = turned.shape[0], powers.shape[1]
     score_block(queries, passages, valid, embed, sent, powers, totals, scores, tops)
     log = log_sum(scores[...])
-    other = log2[0:1, :]
-    logs[...] = stack_rows(logs.shape, (log0[0:1, :], log, other, far0[0:1, :]))
-    tail = split(log) + split(other)
-    send_back(passages, turned, sent, powers, totals, scores, log, tail, back, grad_sim)
+    log_out[...] = stack_rows(log_out.shape, (log,))
+    back2[:dim, :] = query_gradient(passages, turned, sent, powers, totals, scores, log, grad_sim)
+    back1[:dim, :] = near[...]
+    tail = split(log)
+    for back, lines in ((back2, tail), (back1, split(logs[1:2, :]) + tail)):
+        lines = stack_rows((ROWS, rows), [line.astype(jnp.float32) for line in lines])
+        back[dim:, :] = lines.astype(jnp.bfloat16)
 
 
 def joined(back, dim, place):
@@ -238,19 +259,26 @@
     return high + (middle + low)
 
 
+def pair_logs_body(logs, logs1, sent2, out):
+    far = sent_log(sent2, out.shape[1])
+    out[...] = stack_rows(
+        out.shape, (log_add((logs1[0:1, :], logs[1:2, :])), log_add((far, logs1[1:2, :])))
+    )
+
+
 def grad_body(
     queries, passages, wanted, query_hidden, passage_hidden, turned,
     query_unit, query_inverse, passage_unit, passage_inverse,
     powers0, powers1, powers2, totals0, totals1, totals2, scores0, scores1, scores2,
-    sent0, sent1, sent2, logs, logs1, back1, back2,
+    sent0, sent1, sent2, logs, log2, pair_logs, back1, back2,
     losses, query_pre_grad, passage_pre_grad, partial, grad_sim, query_rows,
 ):
     rows = powers0.shape[1]
     dim = turned.shape[0]
     second, third = joined(back1, dim, 0), joined(back2, dim, 0)
     total0 = log_add((logs[0:1, :], second, third))
-    total1 = log_add((logs1[0:1, :], logs[1:2, :], joined(back1, dim, 3)))
-    total2 = log_add((logs[3:4, :], logs1[1:2, :], logs[2:3, :]))
+    total1 = log_add((pair_logs[0:1, :], joined(back1, dim, 3)))
+    total2 = log_add((pair_logs[1:2, :], log2[0:1, :]))
     scores = scores0[...]
     onehot = lax.broadcasted_iota(jnp.int32, scores.shape, 0) == wanted[...]
     loss = total0 - jnp.sum(jnp.where(onehot, scores, 0.0), axis=0, keepdims=True)
@@ -341,14 +369,14 @@
         flops=2 * rows * width * dim,
     )
     sent1 = shifted(sent0, "batch", 1)
-    sent2 = shifted(sent0, "batch", 2)
     (
-        passage_unit, passage_inverse, embed, turned, powers0, totals0, scores0, log0
+        passage_unit, passage_inverse, embed, turned, powers0, totals0, scores0, log0, far_sent
     ) = call(
         functools.partial(own_score_body, queries, passages),
         (
             of((slots, dim), f32), of((slots, dim), f32), of((slots, dim), bf16),
             of((dim, slots), bf16), of((slots, rows), f32), pair, pair, of((8, rows), f32),
+            of((rows + ROWS, dim), bf16),
         ),
         (vmem,) * 4,
         (valid, passage_rows, weight, sent0),
@@ -356,42 +384,48 @@
         flops=2 * slots * dim * (width + rows),
         trans=slots * rows,
     )
-    far0 = shifted(log0, "batch", 2)
-    block_outs = (
-        of((slots, rows), f32), pair, pair, of((8, rows), f32), of((dim + ROWS, rows), bf16)
-    )
-    powers2, totals2, scores2, log2, back2 = call(
-        functools.partial(far_score_body, queries, passages),
-        block_outs,
-        (vmem,) * 4,
-        (valid, embed, turned, sent2),
+    sent2 = shifted(far_sent, "batch", 2)
+    block_outs = (of((slots, rows), f32), pair, pair, of((8, rows), f32))
+    message = of((dim + ROWS, rows), bf16)
+    powers1, totals1, scores1, logs, near = call(
+        functools.partial(near_score_body, queries, passages),
+        block_outs + (of((dim, rows), bf16),),
+        (vmem,) * 5,
+        (valid, embed, turned, sent1, log0),
         scratch=(pairs, pltpu.VMEM((slots, rows), bf16)),
         flops=4 * slots * dim * rows,
         trans=slots * rows,
     )
-    back2 = shifted(back2, "batch", -2)
-    powers1, totals1, scores1, logs, back1 = call(
-        functools.partial(near_score_body, queries, passages),
-        block_outs,
-        (vmem,) * 7,
-        (valid, embed, turned, sent1, log0, log2, far0),
+    logs1 = shifted(logs, "batch", 1)
+    powers2, totals2, scores2, log2, back2, back1 = call(
+        functools.partial(far_score_body, queries, passages),
+        block_outs + (message, message),
+        (vmem,) * 6,
+        (valid, embed, turned, sent2, near, logs),
         scratch=(pairs, pltpu.VMEM((slots, rows), bf16)),
         flops=4 * slots * dim * rows,
         trans=slots * rows,
     )
+    back2 = shifted(back2, "batch", -2)
     back1 = shifted(back1, "batch", -1)
-    logs1 = shifted(logs, "batch", 1)
+    pair_logs = call(
+        pair_logs_body,
+        (of((8, rows), f32),),
+        (vmem,) * 3,
+        (logs, logs1, sent2),
+        flops=20 * slots * dim * rows,
+    )[0]
     losses, query_pre_grad, passage_pre_grad, partial = call(
         functools.partial(grad_body, queries, passages),
         (
             of((1, queries), f32), of((rows, dim), bf16), of((slots, dim), bf16),
             of((width, dim), bf16),
         ),
-        (vmem,) * 24,
+        (vmem,) * 25,
         (wanted, query_rows, passage_rows, turned,
          query_unit, query_inverse, passage_unit, passage_inverse,
          powers0, powers1, powers2, totals0, totals1, totals2, scores0, scores1, scores2,
-         sent0, sent1, sent2, logs, logs1, back1, back2),
+         sent0, sent1, sent2, logs, log2, pair_logs, back1, back2),
         scratch=(pltpu.VMEM((slots, 3 * rows), bf16), pltpu.VMEM((3 * rows, dim), bf16)),
         flops=8 * slots * dim * rows + 2 * (slots + rows) * width * dim,
     )

time: 49.1 us -> 50.5 us (1.029)
  waiting for transfers between devices: 11.2 us -> 12.7 us
  starting transfers between devices: 10.7 us -> 9.37 us
  blocking collectives: 14.5 us -> 15.5 us
    ppermute x6 -> x5, waiting for transfers between devices: 4.91 us -> 6.47 us  [shifted(): return lax.ppermute(block, axis, route)]
    ppermute x6 -> x5, starting transfers between devices: 8.28 us -> 7 us  [shifted(): return lax.ppermute(block, axis, route)]
    all_to_all x1, blocking collectives: 14.5 us -> 15.5 us  [mean_over_devices(): pieces = lax.all_to_all(padded.reshape(devices, share, columns), axes, 0, 0)]
    pallas_call x6 -> x7, Pallas kernels: 8.19 us -> 8.24 us  [call(): pl.pallas_call(body, out_shape=tuple(outs), in_specs=list(in_specs), out_...]
  transfers between devices with their start and end apart: 7 -> 6, of which waited for: 3 -> 5; matrix products, arithmetic and copies ran while one was open for 6% -> 6% of each run, Pallas kernels for 8% -> 8%
where the time goes in v12:
time: 50.5 us; the launch traced here: 50.3 us
  blocking collectives  15.5 us (31%)
  waiting for transfers between devices  12.7 us (25%)
  starting transfers between devices  9.37 us (19%)
  Pallas kernels  8.24 us (16%)
  matrix products  2.96 us (6%)
  other arithmetic  0.78 us (2%)
  between operations  0.7 us (1%)
    all_to_all x1, blocking collectives, mean_over_devices(): pieces = lax.all_to_all(padded.reshape(devices, share, columns), axes, 0, 0)  15.5 us
    pallas_call x7, Pallas kernels, call(): pl.pallas_call(body, out_shape=tuple(outs), in_specs=list(in_specs), out_...  8.24 us
    ppermute x5, starting transfers between devices, shifted(): return lax.ppermute(block, axis, route)  7 us
    ppermute x5, waiting for transfers between devices, shifted(): return lax.ppermute(block, axis, route)  6.47 us
    all_to_all x1, waiting for transfers between devices, mean_over_devices(): whole = lax.all_to_all(means, axes, 0, 0)  6.27 us
    dot_general x2, matrix products, dot32(): lax.dot_general(left, right, dims, preferred_element_type=jnp.float32)  2.96 us
    all_to_all x1, starting transfers between devices, mean_over_devices(): whole = lax.all_to_all(means, axes, 0, 0)  2.37 us
  transfers between devices with their start and end apart: 6, of which 5 were waited for; matrix products, arithmetic and copies ran while one was open for 6% of the time, Pallas kernels for 8%

profile of v12, /device:TPU:1, one launch (start us, length us, event | category | flops | bytes accessed | tf_op | source)
XLA Modules:
  0.0 50.3 jit_solution(3883474427603966066)
XLA Ops:
  0.6 1.8 %shard_map.93 = (f32[256,128]{1,0:T(8,128)S(1)}, f32[256,128]{1,0:T(8,128)S(1)}, bf16[272,128]{1,0:T(8,128)(2,1)S(1)}, s32[16,256]{1,0:T(8,128)S(1)}, s32[1,256]...) custom-call(s32[8]{0:T(128)} %query_lengths_in.1, ...), custom_call_target="tpu_custom_call" | custom-call | flops 50331648 | bytes 5461096 | tf_op jit(solution)/shard_map/pallas_call | solution.py:38
  2.5 2.1 %collective-permute-start = (bf16[272,128]{1,0:T(8,128)(2,1)S(1)}, bf16[272,128]{1,0:T(8,128)(2,1)S(1)}, u32[]{:S(2)}, u32[]{:S(2)}) collective-permute-start(bf16[272,128]{1,0:T(8,128)(2,1)S(1)} %get-tuple-element.41.sent.sent0), channel_id=1, source_target_pairs={{28,0},{0,4},{4,8},{8,12},{12,16},{16,20},{20,24},{24,28},{29,1},{... | collective-permute-start | bytes 208904 | tf_op jit(solution)/shard_map/ppermute | solution.py:28
  4.6 1.5 %shard_map.94 = (f32[1280,128]{1,0:T(8,128)S(1)}, f32[1280,128]{1,0:T(8,128)S(1)}, bf16[1280,128]{1,0:T(8,128)(2,1)S(1)}, bf16[128,1280]{1,0:T(8,128)(2,1)S(1)},...) custom-call(s32[16,256]{1,0:T(8,128)S(1)} %get-tuple-element.39.vali, ...), custom_call_target="tpu_custom_call" | custom-call | flops 335544320 | bytes 5636096 | tf_op jit(solution)/shard_map/pallas_call | solution.py:38
  6.1 1.3 %collective-permute-start.1 = (bf16[272,128]{1,0:T(8,128)(2,1)S(1)}, bf16[272,128]{1,0:T(8,128)(2,1)S(1)}, u32[]{:S(2)}, u32[]{:S(2)}) collective-permute-start(bf16[272,128]{1,0:T(8,128)(2,1)S(1)} %get-tuple-element.51), channel_id=1, source_target_pairs={{24,0},{28,4},{0,8},{4,12},{8,16},{12,20},{16,24},{20,28},{25,1},{... | collective-permute-start | bytes 208904 | tf_op jit(solution)/shard_map/ppermute | solution.py:28
  7.5 1.8 %collective-permute-done.sent.sent1 = bf16[272,128]{1,0:T(8,128)(2,1)S(1)} collective-permute-done((bf16[272,128]{1,0:T(8,128)(2,1)S(1)}, bf16[272,128]{1,0:T(8,128)(2,1)S(1)}, u32[]{:S(2)}, u32[]{:S(2)}) %collective-permute-start) | collective-permute-done | bytes 69664 | tf_op jit(solution)/shard_map/ppermute | solution.py:28
  9.3 1.1 %shard_map.95 = (f32[1280,256]{1,0:T(8,128)S(1)}, f32[16,256]{1,0:T(8,128)S(1)}, f32[16,256]{1,0:T(8,128)S(1)}, f32[8,256]{1,0:T(8,128)S(1)}, bf16[128,256]{1,0:T(8,128)(2,1)S(1)}) custom-call(s32[16,256]{1,0:T(8,128)S(1)} %get-tuple-element.39.valid, bf16[1280,128]{1,0:T(8,128)(2,1)S(1)} %get-tuple-element.48.embed, ...), custom_call_target="tpu_custom_call" | custom-call | flops 167772160 | bytes 2166784 | tf_op jit(solution)/shard_map/pallas_call | solution.py:38
  10.4 0.1 collective-permute-start.2
  10.5 0.7 %collective-permute-done.1.sent.sent2 = bf16[272,128]{1,0:T(8,128)(2,1)S(1)} collective-permute-done((bf16[272,128]{1,0:T(8,128)(2,1)S(1)}, bf16[272,128]{1,0:T(8,128)(2,1)S(1)}, u32[]{:S(2)}, u32[]{:S(2)}) %collective-permute-start.1) | collective-permute-done | bytes 69664 | tf_op jit(solution)/shard_map/ppermute | solution.py:28
  11.2 1.1 %shard_map.96 = (f32[1280,256]{1,0:T(8,128)S(1)}, f32[16,256]{1,0:T(8,128)S(1)}, f32[16,256]{1,0:T(8,128)S(1)}, f32[8,256]{1,0:T(8,128)S(1)}, bf16[144,256]{1,0:...) custom-call(s32[16,256]{1,0:T(8,128)S(1)} %get-tuple-element.39.valid, bf16[1280,128]{1,0:T(8,128)(2,1)S(1)} %get-tuple-element.48.embed, ...), custom_call_target="tpu_custom_call" | custom-call | flops 167772160 | bytes 2314240 | tf_op jit(solution)/shard_map/pallas_call | solution.py:38
  12.3 3.5 %collective-permute-start.3 = (bf16[144,256]{1,0:T(8,128)(2,1)S(1)}, bf16[144,256]{1,0:T(8,128)(2,1)S(1)}, u32[]{:S(2)}, u32[]{:S(2)}) collective-permute-start(bf16[144,256]{1,0:T(8,128)(2,1)S(1)} %get-tuple-element.62), channel_id=1, source_target_pairs={{4,0},{8,4},{12,8},{16,12},{20,16},{24,20},{28,24},{0,28},{5,1},{9... | collective-permute-start | bytes 221192 | tf_op jit(solution)/shard_map/ppermute | solution.py:28
  15.8 0.0 collective-permute-start.4
  15.8 0.0 collective-permute-done.2.logs1
  15.8 1.4 %collective-permute-done.3.back1 = bf16[144,256]{1,0:T(8,128)(2,1)S(1)} collective-permute-done((bf16[144,256]{1,0:T(8,128)(2,1)S(1)}, bf16[144,256]{1,0:T(8,128)(2,1)S(1)}, u32[]{:S(2)}, u32[]{:S(2)}) %collective-permute-start.3) | collective-permute-done | bytes 73760 | tf_op jit(solution)/shard_map/ppermute | solution.py:28
  17.2 2.5 %collective-permute-done.4.back2 = bf16[144,256]{1,0:T(8,128)(2,1)S(1)} collective-permute-done((bf16[144,256]{1,0:T(8,128)(2,1)S(1)}, bf16[144,256]{1,0:T(8,128)(2,1)S(1)}, u32[]{:S(2)}, u32[]{:S(2)}) %collective-permute-start.4) | collective-permute-done | bytes 73760 | tf_op jit(solution)/shard_map/ppermute | solution.py:28
  19.8 1.9 %shard_map.98 = (f32[1,8]{1,0:T(1,128)}, bf16[256,128]{1,0:T(8,128)(2,1)S(1)}, bf16[1280,128]{1,0:T(8,128)(2,1)S(1)}, bf16[768,128]{1,0:T(8,128)(2,1)S(1)}) custom-call(s32[1,256]{1,0:T(1,128)S(1)} %get-tuple-element.36.wanted, bf16[256,768]{1,0:T(8,128)(2,1)S(1)} %get-tuple-element.37.query_hidden, ...), custom_call_target="tpu_custom_call" | custom-call | flops 637534208 | bytes 9262112 | tf_op jit(solution)/shard_map/pallas_call | solution.py:38
  21.7 15.5 %all_to_all.10.pieces = bf16[32,24,128]{2,1,0:T(8,128)(2,1)S(1)} all-to-all(bf16[32,24,128]{2,1,0:T(8,128)(2,1)S(1)} %bitcast.9), channel_id=1, replica_groups=mesh['batch'=8,'mp'=4] {'batch','mp'}, dimensions={0} | all-to-all | bytes 393216 | tf_op jit(solution)/shard_map/all_to_all | solution.py:327
  37.2 0.7 %shard_map.99 = bf16[32,24,128]{2,1,0:T(8,128)(2,1)} custom-call(bf16[32,24,128]{2,1,0:T(8,128)(2,1)S(1)} %all_to_all.10.pieces), custom_call_target="tpu_custom_call" | custom-call | bytes 393216 | tf_op jit(solution)/shard_map/pallas_call | solution.py:38
  37.9 2.4 %all-to-all-start.1 = ((bf16[32,24,128]{2,1,0:T(8,128)(2,1)}), bf16[32,24,128]{2,1,0:T(8,128)(2,1)S(1)}, u32[]{:S(2)}, u32[]{:S(2)}) async-start(bf16[32,24,128]{2,1,0:T(8,128)(2,1)} %shard_map.99), calls=%async_computation.1 | async-start | bytes 393216 | tf_op jit(solution)/shard_map/all_to_all | solution.py:334
  40.3 1.0 %convolution_convert_fusion.1 = bf16[256,768]{1,0:T(8,128)(2,1)} fusion(bf16[256,128]{1,0:T(8,128)(2,1)S(1)} %get-tuple-element.65, bf16[768,128]{1,0:T(8,128)(2,1)S(1)} %get-tuple-element.40.projection), kind=kOutput, calls=%fused_computation.1 | convolution fusion | flops 50528256 | bytes 655360 | tf_op jit(solution)/shard_map/dot_general | solution.py:32
  41.3 1.9 %convolution_convert_fusion = bf16[1280,768]{1,0:T(8,128)(2,1)} fusion(bf16[1280,128]{1,0:T(8,128)(2,1)S(1)} %get-tuple-element.66, bf16[768,128]{1,0:T(8,128)(2,1)S(1)} %get-tuple-element.40.projection), kind=kOutput, calls=%fused_computation | convolution fusion | flops 252641280 | bytes 2490368 | tf_op jit(solution)/shard_map/dot_general | solution.py:32
  43.2 6.3 %all-to-all-done.1 = bf16[32,24,128]{2,1,0:T(8,128)(2,1)S(1)} async-done(((bf16[32,24,128]{2,1,0:T(8,128)(2,1)}), bf16[32,24,128]{2,1,0:T(8,128)(2,1)S(1)}, u32[]{:S(2)}, u32[]{:S(2)}) %all-to-all-start.1) | async-done | bytes 196640 | tf_op jit(solution)/shard_map/all_to_all | solution.py:334
  49.5 0.8 %bitcast_convert_fusion = f32[768,128]{1,0:T(8,128)} fusion(bf16[32,24,128]{2,1,0:T(8,128)(2,1)S(1)} %all-to-all-done.1), kind=kLoop, calls=%fused_computation.2 | loop fusion | flops 98304 | bytes 589824 | tf_op jit(solution)/shard_map/convert_element_type | solution.py:335
  (1 shorter events, 0.0 us)
Async XLA Ops:
  2.5 6.8 %collective-permute-start = (bf16[272,128]{1,0:T(8,128)(2,1)S(1)}, bf16[272,128]{1,0:T(8,128)(2,1)S(1)}, u32[]{:S(2)}, u32[]{:S(2)}) collective-permute-start(bf16[272,128]{1,0:T(8,128)(2,1)S(1)} %get-tuple-element.41.sent.sent0), channel_id=1, source_target_pairs={{28,0},{0,4},{4,8},{8,12},{12,16},{16,20},{20,24},{24,28},{29,1},{... | collective-permute-start | bytes 208904 | tf_op jit(solution)/shard_map/ppermute | solution.py:28
  6.1 5.1 %collective-permute-start.1 = (bf16[272,128]{1,0:T(8,128)(2,1)S(1)}, bf16[272,128]{1,0:T(8,128)(2,1)S(1)}, u32[]{:S(2)}, u32[]{:S(2)}) collective-permute-start(bf16[272,128]{1,0:T(8,128)(2,1)S(1)} %get-tuple-element.51), channel_id=1, source_target_pairs={{24,0},{28,4},{0,8},{4,12},{8,16},{12,20},{16,24},{20,28},{25,1},{... | collective-permute-start | bytes 208904 | tf_op jit(solution)/shard_map/ppermute | solution.py:28
  10.4 5.4 %collective-permute-start.2 = (f32[8,256]{1,0:T(8,128)S(1)}, f32[8,256]{1,0:T(8,128)S(1)}, u32[]{:S(2)}, u32[]{:S(2)}) collective-permute-start(f32[8,256]{1,0:T(8,128)S(1)} %get-tuple-element.53.logs), channel_id=1, source_target_pairs={{28,0},{0,4},{4,8},{8,12},{12,16},{16,20},{20,24},{24,28},{29,1},{... | collective-permute-start | bytes 24584 | tf_op jit(solution)/shard_map/ppermute | solution.py:28
  12.3 4.9 %collective-permute-start.3 = (bf16[144,256]{1,0:T(8,128)(2,1)S(1)}, bf16[144,256]{1,0:T(8,128)(2,1)S(1)}, u32[]{:S(2)}, u32[]{:S(2)}) collective-permute-start(bf16[144,256]{1,0:T(8,128)(2,1)S(1)} %get-tuple-element.62), channel_id=1, source_target_pairs={{4,0},{8,4},{12,8},{16,12},{20,16},{24,20},{28,24},{0,28},{5,1},{9... | collective-permute-start | bytes 221192 | tf_op jit(solution)/shard_map/ppermute | solution.py:28
  15.8 4.0 %collective-permute-start.4 = (bf16[144,256]{1,0:T(8,128)(2,1)S(1)}, bf16[144,256]{1,0:T(8,128)(2,1)S(1)}, u32[]{:S(2)}, u32[]{:S(2)}) collective-permute-start(bf16[144,256]{1,0:T(8,128)(2,1)S(1)} %get-tuple-element.63), channel_id=1, source_target_pairs={{8,0},{12,4},{16,8},{20,12},{24,16},{28,20},{0,24},{4,28},{9,1},{1... | collective-permute-start | bytes 221192 | tf_op jit(solution)/shard_map/ppermute | solution.py:28
  37.9 11.6 %all-to-all-start.1 = ((bf16[32,24,128]{2,1,0:T(8,128)(2,1)}), bf16[32,24,128]{2,1,0:T(8,128)(2,1)S(1)}, u32[]{:S(2)}, u32[]{:S(2)}) async-start(bf16[32,24,128]{2,1,0:T(8,128)(2,1)} %shard_map.99), calls=%async_computation.1 | async-start | bytes 393216 | tf_op jit(solution)/shard_map/all_to_all | solution.py:334

commit v13 on v11

--- a/solution.py
+++ b/solution.py
@@ -82,11 +82,15 @@
     unit_out, inverse_out, sent_out, slots_out, wanted_out, query_hidden, passage_hidden, projection,
     query_lengths, passage_lengths, positives, sems,
 ):
-    pairs = (
+    pairs = [
         (projection_in, projection), (query_hidden_in, query_hidden),
         (query_lengths_in, query_lengths), (positives_in, positives),
-        (passage_lengths_in, passage_lengths), (passage_hidden_in, passage_hidden),
-    )
+        (passage_lengths_in, passage_lengths),
+    ]
+    pieces = sems.shape[0] - len(pairs)
+    size = passage_hidden.shape[0] // pieces
+    parts = [pl.ds(piece * size, size) for piece in range(pieces)]
+    pairs += [(passage_hidden_in.at[part], passage_hidden.at[part]) for part in parts]
     copies = load_all(pairs, sems)
     copies[0].wait()
     copies[1].wait()
@@ -111,7 +115,8 @@
     for item in range(passage_lengths.shape[0]):
         valid = jnp.where(c == item, passage_lengths[item], valid)
     slots_out[...] = valid
-    copies[5].wait()
+    for copy in copies[5:]:
+        copy.wait()
 
 
 def sent_keep(sent, rows):
@@ -343,6 +348,7 @@
     of = jax.ShapeDtypeStruct
     pair = of((ROWS, rows), f32)
     pairs = pltpu.VMEM((ROWS, rows), f32)
+    pieces = passages // 2 if passages % 2 == 0 else passages
 
     taken = (
         query_lengths, passage_lengths, positives, query_hidden, passage_hidden, projection
@@ -362,7 +368,7 @@
             pltpu.SMEM((queries,), jnp.int32),
             pltpu.SMEM((passages,), jnp.int32),
             pltpu.SMEM((queries,), jnp.int32),
-            pltpu.SemaphoreType.DMA((6,)),
+            pltpu.SemaphoreType.DMA((5 + pieces,)),
         ),
         flops=2 * rows * width * dim,
     )

time: 49.1 us -> 49.1 us (level)
  no operation moved by 1% of the time
where the time goes in v13:
time: 49.1 us; the launch traced here: 48.8 us
  blocking collectives  14.5 us (30%)
  starting transfers between devices  10.7 us (22%)
  waiting for transfers between devices  10.7 us (22%)
  Pallas kernels  8.91 us (18%)
  matrix products  2.95 us (6%)
  between operations  0.69 us (1%)
  other arithmetic  0.51 us (1%)
    all_to_all x1, blocking collectives, mean_over_devices(): pieces = lax.all_to_all(padded.reshape(devices, share, columns), axes, 0, 0)  14.5 us
    pallas_call x7, Pallas kernels, call(): pl.pallas_call(body, out_shape=tuple(outs), in_specs=list(in_specs), out_...  8.91 us
    ppermute x6, starting transfers between devices, shifted(): return lax.ppermute(block, axis, route)  8.28 us
    all_to_all x1, waiting for transfers between devices, mean_over_devices(): whole = lax.all_to_all(means, axes, 0, 0)  5.76 us
    ppermute x6, waiting for transfers between devices, shifted(): return lax.ppermute(block, axis, route)  4.91 us
    dot_general x2, matrix products, dot32(): lax.dot_general(left, right, dims, preferred_element_type=jnp.float32)  2.95 us
    all_to_all x1, starting transfers between devices, mean_over_devices(): whole = lax.all_to_all(means, axes, 0, 0)  2.37 us
  transfers between devices with their start and end apart: 7, of which 3 were waited for; matrix products, arithmetic and copies ran while one was open for 7% of the time, Pallas kernels for 8%

profile of v13, /device:TPU:1, one launch (start us, length us, event | category | flops | bytes accessed | tf_op | source)
XLA Modules:
  0.0 48.8 jit_solution(4374988152670203473)
XLA Ops:
  0.6 1.8 %shard_map.93 = (f32[256,128]{1,0:T(8,128)S(1)}, f32[256,128]{1,0:T(8,128)S(1)}, bf16[272,128]{1,0:T(8,128)(2,1)S(1)}, s32[16,256]{1,0:T(8,128)S(1)}, s32[1,256]...) custom-call(s32[8]{0:T(128)} %query_lengths_in.1, ...), custom_call_target="tpu_custom_call" | custom-call | flops 50331648 | bytes 5461096 | tf_op jit(solution)/shard_map/pallas_call | solution.py:38
  2.4 2.2 %collective-permute-start.1 = (bf16[272,128]{1,0:T(8,128)(2,1)S(1)}, bf16[272,128]{1,0:T(8,128)(2,1)S(1)}, u32[]{:S(2)}, u32[]{:S(2)}) collective-permute-start(bf16[272,128]{1,0:T(8,128)(2,1)S(1)} %get-tuple-element.45.sent.sent0), channel_id=1, source_target_pairs={{24,0},{28,4},{0,8},{4,12},{8,16},{12,20},{16,24},{20,28},{25,1},{... | collective-permute-start | bytes 208904 | tf_op jit(solution)/shard_map/ppermute | solution.py:28
  4.6 1.2 %collective-permute-start = (bf16[272,128]{1,0:T(8,128)(2,1)S(1)}, bf16[272,128]{1,0:T(8,128)(2,1)S(1)}, u32[]{:S(2)}, u32[]{:S(2)}) collective-permute-start(bf16[272,128]{1,0:T(8,128)(2,1)S(1)} %get-tuple-element.45.sent.sent0), channel_id=1, source_target_pairs={{28,0},{0,4},{4,8},{8,12},{12,16},{16,20},{20,24},{24,28},{29,1},{... | collective-permute-start | bytes 208904 | tf_op jit(solution)/shard_map/ppermute | solution.py:28
  5.8 1.5 %shard_map.94 = (f32[1280,128]{1,0:T(8,128)S(1)}, f32[1280,128]{1,0:T(8,128)S(1)}, bf16[1280,128]{1,0:T(8,128)(2,1)S(1)}, bf16[128,1280]{1,0:T(8,128)(2,1)S(1)},...) custom-call(s32[16,256]{1,0:T(8,128)S(1)} %get-tuple-element.43.valid, ...), custom_call_target="tpu_custom_call" | custom-call | flops 335544320 | bytes 5566464 | tf_op jit(solution)/shard_map/pallas_call | solution.py:38
  7.4 1.3 %collective-permute-start.2 = (f32[8,256]{1,0:T(8,128)S(1)}, f32[8,256]{1,0:T(8,128)S(1)}, u32[]{:S(2)}, u32[]{:S(2)}) collective-permute-start(f32[8,256]{1,0:T(8,128)S(1)} %get-tuple-element.53.log0), channel_id=1, source_target_pairs={{24,0},{28,4},{0,8},{4,12},{8,16},{12,20},{16,24},{20,28},{25,1},{... | collective-permute-start | bytes 24584 | tf_op jit(solution)/shard_map/ppermute | solution.py:28
  8.7 0.0 collective-permute-done.1.sent.sent2
  8.7 1.1 %shard_map.95 = (f32[1280,256]{1,0:T(8,128)S(1)}, f32[16,256]{1,0:T(8,128)S(1)}, f32[16,256]{1,0:T(8,128)S(1)}, f32[8,256]{1,0:T(8,128)S(1)}, bf16[144,256]{1,0:T(8,128)(2,1)S(1)}) custom-call(s32[16,256]{1,0:T(8,128)S(1)} %get-tuple-element.43.valid, bf16[1280,128]{1,0:T(8,128)(2,1)S(1)} %get-tuple-element.52.embed, ...), custom_call_target="tpu_custom_call" | custom-call | flops 167772160 | bytes 2166784 | tf_op jit(solution)/shard_map/pallas_call | solution.py:38
  9.8 2.0 %collective-permute-start.5 = (bf16[144,256]{1,0:T(8,128)(2,1)S(1)}, bf16[144,256]{1,0:T(8,128)(2,1)S(1)}, u32[]{:S(2)}, u32[]{:S(2)}) collective-permute-start(bf16[144,256]{1,0:T(8,128)(2,1)S(1)} %get-tuple-element.65), channel_id=1, source_target_pairs={{8,0},{12,4},{16,8},{20,12},{24,16},{28,20},{0,24},{4,28},{9,1},{1... | collective-permute-start | bytes 221192 | tf_op jit(solution)/shard_map/ppermute | solution.py:28
  11.8 0.2 collective-permute-done.2.far0
  12.0 0.0 collective-permute-done.sent.sent1
  12.0 1.1 %shard_map.96 = (f32[1280,256]{1,0:T(8,128)S(1)}, f32[16,256]{1,0:T(8,128)S(1)}, f32[16,256]{1,0:T(8,128)S(1)}, f32[8,256]{1,0:T(8,128)S(1)}, bf16[144,256]{1,0:T(8,128)(2,1)S(1)}) custom-call(s32[16,256]{1,0:T(8,128)S(1)} %get-tuple-element.43.valid, bf16[1280,128]{1,0:T(8,128)(2,1)S(1)} %get-tuple-element.52.embed, ...), custom_call_target="tpu_custom_call" | custom-call | flops 167772160 | bytes 2191360 | tf_op jit(solution)/shard_map/pallas_call | solution.py:38
  13.1 1.1 %collective-permute-start.4 = (bf16[144,256]{1,0:T(8,128)(2,1)S(1)}, bf16[144,256]{1,0:T(8,128)(2,1)S(1)}, u32[]{:S(2)}, u32[]{:S(2)}) collective-permute-start(bf16[144,256]{1,0:T(8,128)(2,1)S(1)} %get-tuple-element.64), channel_id=1, source_target_pairs={{4,0},{8,4},{12,8},{16,12},{20,16},{24,20},{28,24},{0,28},{5,1},{9... | collective-permute-start | bytes 221192 | tf_op jit(solution)/shard_map/ppermute | solution.py:28
  14.2 0.5 collective-permute-start.3
  14.6 4.7 %collective-permute-done.3.logs1 = f32[8,256]{1,0:T(8,128)S(1)} collective-permute-done((f32[8,256]{1,0:T(8,128)S(1)}, f32[8,256]{1,0:T(8,128)S(1)}, u32[]{:S(2)}, u32[]{:S(2)}) %collective-permute-start.3) | collective-permute-done | bytes 8224 | tf_op jit(solution)/shard_map/ppermute | solution.py:28
  19.4 0.0 collective-permute-done.5.back2
  19.4 0.0 collective-permute-done.4.back1
  19.4 1.9 %shard_map.97 = (f32[1,8]{1,0:T(1,128)S(1)}, f32[1,8]{1,0:T(1,128)S(1)}, bf16[256,128]{1,0:T(8,128)(2,1)S(1)}, bf16[1280,128]{1,0:T(8,128)(2,1)S(1)}, bf16[768,128]{1,0:T(8,128)(2,1)S(1)}) custom-call(s32[1,256]{1,0:T(1,128)S(1)} %get-tuple-element.40.wanted, bf16[256,768]{1,0:T(8,128)(2,1)S(1)} %get-tuple-element.41.query_hidden, ...), custom_call_target="tpu_custom_call" | custom-call | flops 637534208 | bytes 9253952 | tf_op jit(solution)/shard_map/pallas_call | solution.py:38
  21.3 14.5 %all_to_all.10.pieces = bf16[32,24,128]{2,1,0:T(8,128)(2,1)S(1)} all-to-all(bf16[32,24,128]{2,1,0:T(8,128)(2,1)S(1)} %bitcast.9), channel_id=1, replica_groups=mesh['batch'=8,'mp'=4] {'batch','mp'}, dimensions={0} | all-to-all | bytes 393216 | tf_op jit(solution)/shard_map/all_to_all | solution.py:319
  35.7 0.7 %shard_map.98 = bf16[32,24,128]{2,1,0:T(8,128)(2,1)} custom-call(bf16[32,24,128]{2,1,0:T(8,128)(2,1)S(1)} %all_to_all.10.pieces), custom_call_target="tpu_custom_call" | custom-call | bytes 393216 | tf_op jit(solution)/shard_map/pallas_call | solution.py:38
  36.5 2.4 %all-to-all-start.1 = ((bf16[32,24,128]{2,1,0:T(8,128)(2,1)}), bf16[32,24,128]{2,1,0:T(8,128)(2,1)S(1)}, u32[]{:S(2)}, u32[]{:S(2)}) async-start(bf16[32,24,128]{2,1,0:T(8,128)(2,1)} %shard_map.98), calls=%async_computation.1 | async-start | bytes 393216 | tf_op jit(solution)/shard_map/all_to_all | solution.py:327
  38.8 1.0 %convolution_convert_fusion.1 = bf16[256,768]{1,0:T(8,128)(2,1)} fusion(bf16[256,128]{1,0:T(8,128)(2,1)S(1)} %get-tuple-element.73, bf16[768,128]{1,0:T(8,128)(2,1)S(1)} %get-tuple-element.44.projection), kind=kOutput, calls=%fused_computation.1 | convolution fusion | flops 50528256 | bytes 655360 | tf_op jit(solution)/shard_map/dot_general | solution.py:32
  39.8 0.5 %subtract_bitcast_fusion = f32[8]{0:T(128)} fusion(f32[1,8]{1,0:T(1,128)S(1)} %get-tuple-element.71, f32[1,8]{1,0:T(1,128)S(1)} %get-tuple-element.72), kind=kLoop, calls=%fused_computation.2 | loop fusion | flops 8 | bytes 96 | tf_op jit(solution)/shard_map/reshape | solution.py:436
  40.4 1.9 %convolution_convert_fusion = bf16[1280,768]{1,0:T(8,128)(2,1)} fusion(bf16[1280,128]{1,0:T(8,128)(2,1)S(1)} %get-tuple-element.74, bf16[768,128]{1,0:T(8,128)(2,1)S(1)} %get-tuple-element.44.projection), kind=kOutput, calls=%fused_computation | convolution fusion | flops 252641280 | bytes 2490368 | tf_op jit(solution)/shard_map/dot_general | solution.py:32
  42.3 5.8 %all-to-all-done.1 = bf16[32,24,128]{2,1,0:T(8,128)(2,1)S(1)} async-done(((bf16[32,24,128]{2,1,0:T(8,128)(2,1)}), bf16[32,24,128]{2,1,0:T(8,128)(2,1)S(1)}, u32[]{:S(2)}, u32[]{:S(2)}) %all-to-all-start.1) | async-done | bytes 196640 | tf_op jit(solution)/shard_map/all_to_all | solution.py:327
  48.1 0.8 %shard_map.99 = f32[768,128]{1,0:T(8,128)} custom-call(bf16[768,128]{1,0:T(8,128)(2,1)S(1)} %bitcast.8), custom_call_target="tpu_custom_call" | custom-call | bytes 589824 | tf_op jit(solution)/shard_map/pallas_call | solution.py:38
Async XLA Ops:
  2.4 6.3 %collective-permute-start.1 = (bf16[272,128]{1,0:T(8,128)(2,1)S(1)}, bf16[272,128]{1,0:T(8,128)(2,1)S(1)}, u32[]{:S(2)}, u32[]{:S(2)}) collective-permute-start(bf16[272,128]{1,0:T(8,128)(2,1)S(1)} %get-tuple-element.45.sent.sent0), channel_id=1, source_target_pairs={{24,0},{28,4},{0,8},{4,12},{8,16},{12,20},{16,24},{20,28},{25,1},{... | collective-permute-start | bytes 208904 | tf_op jit(solution)/shard_map/ppermute | solution.py:28
  4.6 7.4 %collective-permute-start = (bf16[272,128]{1,0:T(8,128)(2,1)S(1)}, bf16[272,128]{1,0:T(8,128)(2,1)S(1)}, u32[]{:S(2)}, u32[]{:S(2)}) collective-permute-start(bf16[272,128]{1,0:T(8,128)(2,1)S(1)} %get-tuple-element.45.sent.sent0), channel_id=1, source_target_pairs={{28,0},{0,4},{4,8},{8,12},{12,16},{16,20},{20,24},{24,28},{29,1},{... | collective-permute-start | bytes 208904 | tf_op jit(solution)/shard_map/ppermute | solution.py:28
  7.4 4.6 %collective-permute-start.2 = (f32[8,256]{1,0:T(8,128)S(1)}, f32[8,256]{1,0:T(8,128)S(1)}, u32[]{:S(2)}, u32[]{:S(2)}) collective-permute-start(f32[8,256]{1,0:T(8,128)S(1)} %get-tuple-element.53.log0), channel_id=1, source_target_pairs={{24,0},{28,4},{0,8},{4,12},{8,16},{12,20},{16,24},{20,28},{25,1},{... | collective-permute-start | bytes 24584 | tf_op jit(solution)/shard_map/ppermute | solution.py:28
  9.8 9.6 %collective-permute-start.5 = (bf16[144,256]{1,0:T(8,128)(2,1)S(1)}, bf16[144,256]{1,0:T(8,128)(2,1)S(1)}, u32[]{:S(2)}, u32[]{:S(2)}) collective-permute-start(bf16[144,256]{1,0:T(8,128)(2,1)S(1)} %get-tuple-element.65), channel_id=1, source_target_pairs={{8,0},{12,4},{16,8},{20,12},{24,16},{28,20},{0,24},{4,28},{9,1},{1... | collective-permute-start | bytes 221192 | tf_op jit(solution)/shard_map/ppermute | solution.py:28
  13.1 6.3 %collective-permute-start.4 = (bf16[144,256]{1,0:T(8,128)(2,1)S(1)}, bf16[144,256]{1,0:T(8,128)(2,1)S(1)}, u32[]{:S(2)}, u32[]{:S(2)}) collective-permute-start(bf16[144,256]{1,0:T(8,128)(2,1)S(1)} %get-tuple-element.64), channel_id=1, source_target_pairs={{4,0},{8,4},{12,8},{16,12},{20,16},{24,20},{28,24},{0,28},{5,1},{9... | collective-permute-start | bytes 221192 | tf_op jit(solution)/shard_map/ppermute | solution.py:28
  14.2 5.2 %collective-permute-start.3 = (f32[8,256]{1,0:T(8,128)S(1)}, f32[8,256]{1,0:T(8,128)S(1)}, u32[]{:S(2)}, u32[]{:S(2)}) collective-permute-start(f32[8,256]{1,0:T(8,128)S(1)} %get-tuple-element.63.logs), channel_id=1, source_target_pairs={{28,0},{0,4},{4,8},{8,12},{12,16},{16,20},{20,24},{24,28},{29,1},{... | collective-permute-start | bytes 24584 | tf_op jit(solution)/shard_map/ppermute | solution.py:28
  36.5 11.6 %all-to-all-start.1 = ((bf16[32,24,128]{2,1,0:T(8,128)(2,1)}), bf16[32,24,128]{2,1,0:T(8,128)(2,1)S(1)}, u32[]{:S(2)}, u32[]{:S(2)}) async-start(bf16[32,24,128]{2,1,0:T(8,128)(2,1)} %shard_map.98), calls=%async_computation.1 | async-start | bytes 393216 | tf_op jit(solution)/shard_map/all_to_all | solution.py:327
